TPU v7x, 128 devices: a whole 4x4x4 slice. The times are simulated.
128 devices in a mesh: seq: 16 (over y_hi, x, core), ch: 8 (over z, y_lo).
Axes of the slice: x: 4, y: 4 (y_hi: 2, y_lo: 2; y = y_hi * 2 + y_lo), z: 4, core: 2. Of those that a mesh axis runs over, the one named last changes fastest.
Arguments:
- keys: bfloat16 [4096, 8192], P('seq', 'ch'), may hold values from -6 to 6
- values: bfloat16 [4096, 8192], P('seq', 'ch'), may hold values from -6 to 6
- queries: bfloat16 [4096, 8192], P('seq', 'ch'), may hold values from -6 to 6
- decay: float32 [8192, 16], P('ch'), may hold values from 1 to 600
- residue: float32 [8192, 16], P('ch'), may hold values from -2 to 2
- skip: float32 [8192], P('ch'), may hold values from -4 to 4
- out_weight: bfloat16 [8192, 4096], P('ch', 'seq'), may hold values from -0.0625 to 0.0625
Outputs:
- projected: bfloat16 [4096, 4096], P('seq', 'ch')
All inputs are finite; a program needn't handle non-finite values.
Results may differ from a plain program's by a relative error of at most 0.023.
Values may be sent and summed in bfloat16 or wider, within the bound.
No kernel may reach another device: no remote copies, remote signals or barrier semaphores. Data moves between devices by JAX's collectives and lax.ppermute only.
A program may use at most 64 MiB of HBM per device.

v0:
```python
import jax
import jax.numpy as jnp
from jax import lax
from jax.experimental import pallas as pl
from jax.experimental.pallas import tpu as pltpu
from jax.sharding import Mesh, PartitionSpec as P

SEQ = ("yh", "x", "core")
CH = ("z", "yl")
ALL = SEQ + CH
SIZES = {"yh": 2, "x": 4, "core": 2, "z": 4, "yl": 2}
LANES = 128
ROWS = 8


def shift(value, axis, step):
    size = SIZES[axis]
    return lax.ppermute(value, axis, [(i, (i + step) % size) for i in range(size)])


def spread_rows(keys_ref, values_ref, z_ref):
    steps = keys_ref.shape[0]
    for block in range(ROWS):
        lanes = pl.ds(block * LANES, LANES)
        product = keys_ref[:, lanes].astype(jnp.float32) * values_ref[:, lanes].astype(jnp.float32)
        z_ref[pl.ds(block * steps, steps), :] = product.astype(jnp.bfloat16).astype(jnp.float32)


def end_state_kernel(keys_ref, values_ref, rate_ref, state_ref, z_ref):
    steps = keys_ref.shape[0]
    modes = rate_ref.shape[0]
    spread_rows(keys_ref, values_ref, z_ref)
    keep = [jnp.exp(-rate_ref[n]) for n in range(modes)]

    def step(t, states):
        z = z_ref[pl.ds(t, ROWS, stride=steps), :]
        return tuple(keep[n] * states[n] + z for n in range(modes))

    start = tuple(jnp.zeros((ROWS, LANES), jnp.float32) for _ in range(modes))
    states = lax.fori_loop(0, steps, step, start, unroll=8)
    for n in range(modes):
        state_ref[n] = states[n]


def gated_kernel(
    keys_ref, values_ref, queries_ref, rate_ref, gain_ref, skip_ref, state_ref, out_ref, z_ref, y_ref
):
    steps = keys_ref.shape[0]
    modes = rate_ref.shape[0]
    spread_rows(keys_ref, values_ref, z_ref)
    keep = [jnp.exp(-rate_ref[n]) for n in range(modes)]
    gain = [gain_ref[n] for n in range(modes)]
    skip = skip_ref[...]

    def step(t, states):
        at = pl.ds(t, ROWS, stride=steps)
        z = z_ref[at, :]
        states = tuple(keep[n] * states[n] + z for n in range(modes))
        terms = [gain[n] * states[n] for n in range(modes)] + [skip * z]
        while len(terms) > 1:
            terms = [sum(terms[i : i + 2]) for i in range(0, len(terms), 2)]
        y_ref[at, :] = terms[0]
        return states

    lax.fori_loop(0, steps, step, tuple(state_ref[n] for n in range(modes)), unroll=4)
    for block in range(ROWS):
        lanes = pl.ds(block * LANES, LANES)
        y = y_ref[pl.ds(block * steps, steps), :]
        out_ref[:, lanes] = (queries_ref[:, lanes].astype(jnp.float32) * y).astype(jnp.bfloat16)


def end_state(keys, values, rate):
    steps = keys.shape[0]
    return pl.pallas_call(
        end_state_kernel,
        out_shape=jax.ShapeDtypeStruct(rate.shape, jnp.float32),
        scratch_shapes=[pltpu.VMEM((ROWS * steps, LANES), jnp.float32)],
        compiler_params=pltpu.CompilerParams(vmem_limit_bytes=32 * 1024 * 1024),
        cost_estimate=pl.CostEstimate(flops=9000000, bytes_accessed=1200000, transcendentals=0),
        name="end_state",
    )(keys, values, rate)


def gate(keys, values, queries, rate, gain, skip, state):
    steps = keys.shape[0]
    return pl.pallas_call(
        gated_kernel,
        out_shape=jax.ShapeDtypeStruct(keys.shape, jnp.bfloat16),
        scratch_shapes=[pltpu.VMEM((ROWS * steps, LANES), jnp.float32) for _ in range(2)],
        compiler_params=pltpu.CompilerParams(vmem_limit_bytes=32 * 1024 * 1024),
        cost_estimate=pl.CostEstimate(flops=18000000, bytes_accessed=2500000, transcendentals=0),
        name="gated",
    )(keys, values, queries, rate, gain, skip, state)


def incoming_state(own, rate, steps):
    core, x, yh = (lax.axis_index(name) for name in ("core", "x", "yh"))
    other = shift(own, "core", 1)
    first = jnp.where(core == 0, own, other)
    second = jnp.where(core == 0, other, own)
    hop = rate * jnp.float32(steps)
    pair = jnp.exp(-hop) * first + second
    ring = [pair] + [shift(pair, "x", j) for j in (1, 2, 3)]
    before = jnp.zeros_like(own)
    total = jnp.zeros_like(own)
    for j in range(4):
        source = (x - j) % 4
        total = total + jnp.exp(-hop * (2 * (3 - source)).astype(jnp.float32)) * ring[j]
        if j:
            before = before + jnp.where(x >= j, jnp.exp(-hop * (2.0 * (j - 1))), 0.0) * ring[j]
    earlier = lax.ppermute(total, "yh", [(0, 1)])
    before = before + jnp.where(yh == 1, jnp.exp(-hop * (2 * x).astype(jnp.float32)), 0.0) * earlier
    return jnp.where(core == 0, before, jnp.exp(-hop) * before + first)


def by_mode(array):
    return array.T.reshape(array.shape[1], ROWS, LANES)


def body(keys, values, queries, decay, residue, skip, out_weight):
    steps = keys.shape[0]
    seq_len = steps * 16
    weight = lax.all_gather(out_weight, SEQ, axis=1, tiled=True)
    rate = by_mode(decay) / jnp.float32(seq_len)
    gain = by_mode(residue) * jnp.sqrt(rate)
    own = end_state(keys, values, rate)
    state = incoming_state(own, rate, steps)
    gated = gate(keys, values, queries, rate, gain, skip.reshape(ROWS, LANES), state)
    partial = jnp.dot(gated, weight, preferred_element_type=jnp.float32).astype(jnp.bfloat16)
    blocks = partial.reshape(steps, 8, partial.shape[1] // 8).transpose(1, 0, 2)
    blocks = lax.all_to_all(blocks, CH, 0, 0)
    return blocks.astype(jnp.float32).sum(0).astype(jnp.bfloat16)


def solution(mesh):
    fine = Mesh(
        mesh.devices.reshape(tuple(SIZES[name] for name in ALL)),
        ALL,
    )
    return jax.shard_map(
        body,
        mesh=fine,
        in_specs=(
            P(SEQ, CH),
            P(SEQ, CH),
            P(SEQ, CH),
            P(CH, None),
            P(CH, None),
            P(CH),
            P(CH, SEQ),
        ),
        out_specs=P(SEQ, CH),
        check_vma=False,
    )
```

profile of v0, /device:TPU:1, one launch (start us, length us, event | category | flops | bytes accessed | tf_op | source)
XLA Modules:
  0.0 137.4 jit_solution(1399784053069034646)
XLA Ops:
  6.5 0.0 copy-start.3
  6.5 0.0 copy-start.1
  6.5 0.0 copy-start.5
  6.5 0.0 all-gather.2.cloned.1.call-start
  6.5 0.7 all-gather.2.cloned.1.call-update
  7.3 0.9 select_bitcast_fusion.3
  8.3 0.0 copy-start
  8.3 1.0 copy-done
  9.3 0.0 copy-start.2
  9.3 1.0 copy-done.2
  10.4 0.0 copy-start.4
  10.4 1.7 %end_state.1 = f32[16,8,128]{2,1,0:T(8,128)S(1)} custom-call(bf16[256,1024]{1,0:T(8,128)(2,1)S(1)} %copy-done, bf16[256,1024]{1,0:T(8,128)(2,1)S(1)} %copy-done.2, f32[16,8,128]{2,1,0:T(8,128)S(1)} %bitcast.101), custom_call_target="tpu_custom_call" | custom-call | flops 9000000 | bytes 1200000 | tf_op jit(solution)/shard_map/end_state/pallas_call | solution.py:74
  12.1 1.5 %collective-permute-start = (f32[16,8,128]{2,1,0:T(8,128)S(1)}, f32[16,8,128]{2,1,0:T(8,128)S(1)}, u32[]{:S(2)}, u32[]{:S(2)}) collective-permute-start(f32[16,8,128]{2,1,0:T(8,128)S(1)} %end_state.1), channel_id=1, source_target_pairs={{0,8},{8,0},{1,9},{9,1},{2,10},{10,2},{3,11},{11,3},{4,12},{12,4},... | collective-permute-start | bytes 196616 | tf_op jit(solution)/shard_map/ppermute | solution.py:18
  13.6 0.9 collective-permute-done
  14.5 2.6 %collective-permute-start.3 = (f32[16,8,128]{2,1,0:T(8,128)S(1)}, f32[16,8,128]{2,1,0:T(8,128)S(1)}, u32[]{:S(2)}, u32[]{:S(2)}) collective-permute-start(f32[16,8,128]{2,1,0:T(8,128)S(1)} %fusion.6), channel_id=1, source_target_pairs={{0,48},{16,0},{32,16},{48,32},{1,49},{17,1},{33,17},{49,33},{2,50}... | collective-permute-start | bytes 196616 | tf_op jit(solution)/shard_map/ppermute | solution.py:18
  17.2 0.5 collective-permute-start.2
  17.7 0.6 collective-permute-start.1
  18.3 0.9 copy.11
  19.2 0.0 collective-permute-done.3
  19.2 2.6 %collective-permute-done.2 = f32[16,8,128]{2,1,0:T(8,128)S(1)} collective-permute-done((f32[16,8,128]{2,1,0:T(8,128)S(1)}, f32[16,8,128]{2,1,0:T(8,128)S(1)}, u32[]{:S(2)}, u32[]{:S(2)}) %collective-permute-start.2) | collective-permute-done | bytes 65568 | tf_op jit(solution)/shard_map/ppermute | solution.py:18
  21.8 1.2 collective-permute-done.1
  23.1 4.8 %collective-permute-start.4 = (f32[16,8,128]{2,1,0:T(8,128)S(1)}, f32[16,8,128]{2,1,0:T(8,128)S(1)}, u32[]{:S(2)}, u32[]{:S(2)}) collective-permute-start(f32[16,8,128]{2,1,0:T(8,128)S(1)} %fusion), channel_id=1, source_target_pairs={{0,64},{1,65},{2,66},{3,67},{4,68},{5,69},{6,70},{7,71},{8,72},{9,... | collective-permute-start | bytes 196616 | tf_op jit(solution)/shard_map/ppermute | solution.py:111
  28.1 2.1 %collective-permute-done.4 = f32[16,8,128]{2,1,0:T(8,128)S(1)} collective-permute-done((f32[16,8,128]{2,1,0:T(8,128)S(1)}, f32[16,8,128]{2,1,0:T(8,128)S(1)}, u32[]{:S(2)}, u32[]{:S(2)}) %collective-permute-start.4) | collective-permute-done | bytes 65568 | tf_op jit(solution)/shard_map/ppermute | solution.py:111
  30.2 0.1 fusion.8.state_ref
  30.3 0.0 copy-done.3
  30.3 0.0 copy-done.1
  30.3 0.0 copy-done.5
  30.3 0.0 copy-done.4
  30.3 3.8 %gated.1 = bf16[256,1024]{1,0:T(8,128)(2,1)S(1)} custom-call(bf16[256,1024]{1,0:T(8,128)(2,1)S(1)} %copy-done.1, bf16[256,1024]{1,0:T(8,128)(2,1)S(1)} %copy-done.3, bf16[256,1024]{1,0:T(8,128)(2,1)S(1)} %copy-done.4, f32[16,8,128]{2,1,0:T(8,128)S(1)} %bitcast.102, f32[16,8,128]{2,1,0:T(8,128)S(1)} %bitcast_multiply_fusion.10.gain_ref, ...), custom_call_target="tpu_custom_call" | custom-call | flops 18000000 | bytes 2500000 | tf_op jit(solution)/shard_map/gated/pallas_call | solution.py:86
  34.1 59.3 %all-gather.2.cloned.1.call-done = bf16[1024,4096]{1,0:T(8,128)(2,1)} async-done(((bf16[1024,256]{1,0:T(8,128)(2,1)}), bf16[1024,4096]{1,0:T(8,128)(2,1)}) %all-gather.2.cloned.1.call-update) | async-done | bytes 8388624 | tf_op jit(solution)/shard_map/all_gather | solution.py:123
  93.4 5.7 %convolution_convert_fusion = bf16[256,4096]{1,0:T(8,128)(2,1)S(1)} fusion(bf16[256,1024]{1,0:T(8,128)(2,1)S(1)} %gated.1, bf16[1024,4096]{1,0:T(8,128)(2,1)} %all-gather.2.cloned.1.call-done), kind=kOutput, calls=%fused_computation | convolution fusion | flops 2148532224 | bytes 11010048 | tf_op jit(solution)/shard_map/dot_general | solution.py:129
  99.1 0.2 copy.22
  99.3 30.2 %all_to_all.5 = bf16[8,256,512]{2,1,0:T(8,128)(2,1)S(1)} all-to-all(bf16[8,256,512]{2,1,0:T(8,128)(2,1)S(1)} %bitcast.104), channel_id=1, replica_groups=mesh['yh'=2,'x'=4,'core'=2,'z'=4,'yl'=2] {'z','yl'}, dimensions={0} | all-to-all | bytes 4194304 | tf_op jit(solution)/shard_map/all_to_all | solution.py:131
  129.5 1.1 reduce_sum.12
  (13 shorter events, 0.2 us)
Async XLA Ops:
  6.5 23.7 %copy-start.3 = (bf16[256,1024]{1,0:T(8,128)(2,1)S(1)}, bf16[256,1024]{1,0:T(8,128)(2,1)}, u32[]{:S(2)}) copy-start(bf16[256,1024]{1,0:T(8,128)(2,1)} %values_ref.3) | copy-start | bytes 1572868
  6.5 23.7 %copy-start.1 = (bf16[256,1024]{1,0:T(8,128)(2,1)S(1)}, bf16[256,1024]{1,0:T(8,128)(2,1)}, u32[]{:S(2)}) copy-start(bf16[256,1024]{1,0:T(8,128)(2,1)} %keys_ref.3) | copy-start | bytes 1572868
  6.5 23.7 %copy-start.5 = (f32[1024]{0:T(1024)S(1)}, f32[1024]{0:T(1024)}, u32[]{:S(2)}) copy-start(f32[1024]{0:T(1024)} %param.12) | copy-start | bytes 12292
  6.5 86.8 %all-gather.2.cloned.1.call-start = ((), (), s32[]{:S(2)}) async-start(), calls=%async_computation.1 | async-start | bytes 8912896 | tf_op jit(solution)/shard_map/all_gather | solution.py:123
  8.3 1.0 copy-start
  9.3 1.0 copy-start.2
  10.4 19.9 %copy-start.4 = (bf16[256,1024]{1,0:T(8,128)(2,1)S(1)}, bf16[256,1024]{1,0:T(8,128)(2,1)}, u32[]{:S(2)}) copy-start(bf16[256,1024]{1,0:T(8,128)(2,1)} %queries_ref.1) | copy-start | bytes 1572868
  12.1 2.4 %collective-permute-start = (f32[16,8,128]{2,1,0:T(8,128)S(1)}, f32[16,8,128]{2,1,0:T(8,128)S(1)}, u32[]{:S(2)}, u32[]{:S(2)}) collective-permute-start(f32[16,8,128]{2,1,0:T(8,128)S(1)} %end_state.1), channel_id=1, source_target_pairs={{0,8},{8,0},{1,9},{9,1},{2,10},{10,2},{3,11},{11,3},{4,12},{12,4},... | collective-permute-start | bytes 196616 | tf_op jit(solution)/shard_map/ppermute | solution.py:18
  14.5 4.7 %collective-permute-start.3 = (f32[16,8,128]{2,1,0:T(8,128)S(1)}, f32[16,8,128]{2,1,0:T(8,128)S(1)}, u32[]{:S(2)}, u32[]{:S(2)}) collective-permute-start(f32[16,8,128]{2,1,0:T(8,128)S(1)} %fusion.6), channel_id=1, source_target_pairs={{0,48},{16,0},{32,16},{48,32},{1,49},{17,1},{33,17},{49,33},{2,50}... | collective-permute-start | bytes 196616 | tf_op jit(solution)/shard_map/ppermute | solution.py:18
  17.2 4.7 %collective-permute-start.2 = (f32[16,8,128]{2,1,0:T(8,128)S(1)}, f32[16,8,128]{2,1,0:T(8,128)S(1)}, u32[]{:S(2)}, u32[]{:S(2)}) collective-permute-start(f32[16,8,128]{2,1,0:T(8,128)S(1)} %fusion.6), channel_id=1, source_target_pairs={{0,32},{16,48},{32,0},{48,16},{1,33},{17,49},{33,1},{49,17},{2,34}... | collective-permute-start | bytes 196616 | tf_op jit(solution)/shard_map/ppermute | solution.py:18
  17.7 5.4 %collective-permute-start.1 = (f32[16,8,128]{2,1,0:T(8,128)S(1)}, f32[16,8,128]{2,1,0:T(8,128)S(1)}, u32[]{:S(2)}, u32[]{:S(2)}) collective-permute-start(f32[16,8,128]{2,1,0:T(8,128)S(1)} %fusion.6), channel_id=1, source_target_pairs={{0,16},{16,32},{32,48},{48,0},{1,17},{17,33},{33,49},{49,1},{2,18}... | collective-permute-start | bytes 196616 | tf_op jit(solution)/shard_map/ppermute | solution.py:18
  23.1 7.1 %collective-permute-start.4 = (f32[16,8,128]{2,1,0:T(8,128)S(1)}, f32[16,8,128]{2,1,0:T(8,128)S(1)}, u32[]{:S(2)}, u32[]{:S(2)}) collective-permute-start(f32[16,8,128]{2,1,0:T(8,128)S(1)} %fusion), channel_id=1, source_target_pairs={{0,64},{1,65},{2,66},{3,67},{4,68},{5,69},{6,70},{7,71},{8,72},{9,... | collective-permute-start | bytes 196616 | tf_op jit(solution)/shard_map/ppermute | solution.py:111
Sparse Core Ops, SparseCore 0:
  9.6 83.6 all-gather.1
where the time goes:
time: 138 us; the launch traced here: 137 us
  waiting for transfers between devices  66.8 us (48%)
  blocking collectives  30.2 us (22%)
  between operations  13.6 us (10%)
  starting transfers between devices  10.1 us (7%)
  matrix products  5.75 us (4%)
  Pallas kernels  5.5 us (4%)
  local copies, waits for them, and re-layouts  3.28 us (2%)
  other arithmetic  2.1 us (2%)
    all_gather x1, waiting for transfers between devices, body(): weight = lax.all_gather(out_weight, SEQ, axis=1, tiled=True)  59.3 us
    all_to_all x1, blocking collectives, body(): blocks = lax.all_to_all(blocks, CH, 0, 0)  30.2 us
    dot_general x1, matrix products, body(): jnp.dot(gated, weight, preferred_element_type=jnp.float32)  5.75 us
    ppermute x4, starting transfers between devices, shift(): lax.ppermute(value, axis, [(i, (i + step) % size) for i in range(size)])  5.26 us
    ppermute x1, starting transfers between devices, incoming_state(): earlier = lax.ppermute(total, 'yh', [(0, 1)])  4.82 us
    ppermute x4, waiting for transfers between devices, shift(): lax.ppermute(value, axis, [(i, (i + step) % size) for i in range(size)])  4.72 us
    pallas_call x1, Pallas kernels, gate(): pl.pallas_call(gated_kernel, out_shape=jax.ShapeDtypeStruct(keys.shape, j...  3.78 us
    unnamed x23, local copies, waits for them, and re-layouts  3.09 us
  transfers between devices with their start and end apart: 6, of which 5 were waited for; matrix products, arithmetic and copies ran while one was open for 1% of the time, Pallas kernels for 4%

commit v1 on v0

--- a/solution.py
+++ b/solution.py
@@ -1,3 +1,5 @@
+import functools
+
 import jax
 import jax.numpy as jnp
 from jax import lax
@@ -11,6 +13,7 @@
 SIZES = {"yh": 2, "x": 4, "core": 2, "z": 4, "yl": 2}
 LANES = 128
 ROWS = 8
+CUT = 40
 
 
 def shift(value, axis, step):
@@ -93,14 +96,17 @@
     )(keys, values, queries, rate, gain, skip, state)
 
 
-def incoming_state(own, rate, steps):
+def incoming_state(own, rate, steps, join, last_join):
     core, x, yh = (lax.axis_index(name) for name in ("core", "x", "yh"))
     other = shift(own, "core", 1)
     first = jnp.where(core == 0, own, other)
     second = jnp.where(core == 0, other, own)
     hop = rate * jnp.float32(steps)
     pair = jnp.exp(-hop) * first + second
-    ring = [pair] + [shift(pair, "x", j) for j in (1, 2, 3)]
+    next_pair = shift(pair, "x", 1)
+    pair, next_pair = join(pair, next_pair)
+    both = shift(jnp.stack([pair, next_pair]), "x", 2)
+    ring = [pair, next_pair, both[0], both[1]]
     before = jnp.zeros_like(own)
     total = jnp.zeros_like(own)
     for j in range(4):
@@ -108,28 +114,124 @@
         total = total + jnp.exp(-hop * (2 * (3 - source)).astype(jnp.float32)) * ring[j]
         if j:
             before = before + jnp.where(x >= j, jnp.exp(-hop * (2.0 * (j - 1))), 0.0) * ring[j]
-    earlier = lax.ppermute(total, "yh", [(0, 1)])
+    earlier = last_join(lax.ppermute(total, "yh", [(0, 1)]))
     before = before + jnp.where(yh == 1, jnp.exp(-hop * (2 * x).astype(jnp.float32)), 0.0) * earlier
     return jnp.where(core == 0, before, jnp.exp(-hop) * before + first)
 
 
 def by_mode(array):
     return array.T.reshape(array.shape[1], ROWS, LANES)
+
+
+def first_weights(own):
+    return shift(own, "x", 1), shift(own, "x", 3), shift(own, "yh", 1)
+
+
+def second_weights(left, right, far):
+    cut = far.shape[0] * CUT // 64
+    core = lax.axis_index("core")
+    opposite = lax.ppermute(
+        jnp.where(core == 0, left, right),
+        ("x", "core"),
+        [(2 * i + c, 2 * ((i + 1 - 2 * c) % 4) + c) for i in range(4) for c in range(2)],
+    )
+    tops = shift(jnp.stack([left[:cut], right[:cut]]), "yh", 1)
+    return opposite, tops, shift(far[cut:], "x", 1), shift(far[cut:], "x", 3)
+
+
+def third_weights(opposite, far):
+    half = far.shape[0] // 2
+    return shift(opposite[:half], "yh", 1), shift(far[half:], "x", 2)
+
+
+def project_kernel(pieces, first_ref, second_ref, slot_ref, *refs):
+    near_ref, far_ref = refs[-2:]
+    refs = refs[:-2]
+    position = 0
+    for block, count in enumerate(pieces):
+        sums = [None, None]
+        row = 0
+        for ref in refs[position : position + count]:
+            rows = ref.shape[0]
+            for half, rows_ref in enumerate((first_ref, second_ref)):
+                term = jnp.dot(rows_ref[:, row : row + rows], ref[...], preferred_element_type=jnp.float32)
+                sums[half] = term if sums[half] is None else sums[half] + term
+            row += rows
+        position += count
+        turn, side = slot_ref[0, block], slot_ref[1, block]
+        near_ref[side, turn] = sums[0].astype(jnp.bfloat16)
+        far_ref[turn, side] = sums[1].astype(jnp.bfloat16)
+
+
+def project(first, second, blocks, slots):
+    flat = [piece for block in blocks for piece in block]
+    rows, columns = first.shape[0], flat[0].shape[1]
+    return pl.pallas_call(
+        functools.partial(project_kernel, [len(block) for block in blocks]),
+        out_shape=(
+            jax.ShapeDtypeStruct((2, 4, rows, columns), jnp.bfloat16),
+            jax.ShapeDtypeStruct((4, 2, rows, columns), jnp.bfloat16),
+        ),
+        in_specs=[pl.BlockSpec(memory_space=pltpu.VMEM)] * 2
+        + [pl.BlockSpec(memory_space=pltpu.SMEM)]
+        + [pl.BlockSpec(memory_space=pltpu.VMEM)] * len(flat),
+        compiler_params=pltpu.CompilerParams(vmem_limit_bytes=40 * 1024 * 1024),
+        cost_estimate=pl.CostEstimate(flops=2200000000, bytes_accessed=7000000, transcendentals=0),
+        name="project",
+    )(first, second, slots, *flat)
+
+
+def add_up(*terms):
+    total = terms[0].astype(jnp.float32)
+    for term in terms[1:]:
+        total = total + term.astype(jnp.float32)
+    return total.astype(jnp.bfloat16)
 
 
 def body(keys, values, queries, decay, residue, skip, out_weight):
     steps = keys.shape[0]
     seq_len = steps * 16
-    weight = lax.all_gather(out_weight, SEQ, axis=1, tiled=True)
+    core, x, yh, z, yl = (lax.axis_index(name) for name in ("core", "x", "yh", "z", "yl"))
+    rounds = [first_weights(out_weight)]
     rate = by_mode(decay) / jnp.float32(seq_len)
     gain = by_mode(residue) * jnp.sqrt(rate)
     own = end_state(keys, values, rate)
-    state = incoming_state(own, rate, steps)
+
+    def join(*values):
+        values, rounds[0] = lax.optimization_barrier((values, rounds[0]))
+        rounds.append(second_weights(*rounds[0]))
+        return values
+
+    def last_join(value):
+        value, rounds[1] = lax.optimization_barrier((value, rounds[1]))
+        rounds.append(third_weights(rounds[1][0], rounds[0][2]))
+        return value
+
+    state = incoming_state(own, rate, steps, join, last_join)
+    (left, right, far), (opposite, tops, left_end, right_end), far_opposite = rounds
+    blocks = [[out_weight], [left], [opposite], [right]]
+    blocks += [[far], [tops[0], left_end], list(far_opposite), [tops[1], right_end]]
     gated = gate(keys, values, queries, rate, gain, skip.reshape(ROWS, LANES), state)
-    partial = jnp.dot(gated, weight, preferred_element_type=jnp.float32).astype(jnp.bfloat16)
-    blocks = partial.reshape(steps, 8, partial.shape[1] // 8).transpose(1, 0, 2)
-    blocks = lax.all_to_all(blocks, CH, 0, 0)
-    return blocks.astype(jnp.float32).sum(0).astype(jnp.bfloat16)
+    other = shift(gated, "core", 1)
+    first = jnp.where(core == 0, gated, other)
+    second = jnp.where(core == 0, other, gated)
+    column = [(yh ^ side) * 4 + (x - j) % 4 for side in (0, 1) for j in range(4)]
+    slots = jnp.stack(
+        [
+            jnp.stack([(c // 2 - z) % 4 for c in column]),
+            jnp.stack([c % 2 ^ yl for c in column]),
+        ]
+    ).astype(jnp.int32)
+    near, far = project(first, second, blocks, slots)
+    pair = add_up(near[0], shift(near[1], "yl", 1))
+    ring = add_up(far[0], *[shift(far[j], "z", j) for j in (1, 3, 2)])
+    top = add_up(pair[0], *[shift(pair[j], "z", j) for j in (1, 3, 2)])
+    end = add_up(ring[0], shift(ring[1], "yl", 1))
+    mine = jnp.where(core == 0, top, end)
+    got = shift(jnp.where(core == 0, end, top), "core", 1)
+    return jnp.where(
+        core == 0, jnp.concatenate([mine, got], 1), jnp.concatenate([got, mine], 1)
+    )
 
 
 def solution(mesh):

time: 138 us -> 91.4 us (0.66)
  waiting for transfers between devices: 66.8 us -> 33.5 us
  starting transfers between devices: 10.1 us -> 40.5 us
  blocking collectives: 30.2 us -> 0 us
  between operations: 13.6 us -> 0.36 us
  matrix products: 5.75 us -> 0 us
  Pallas kernels: 5.5 us -> 8.54 us
  local copies, waits for them, and re-layouts: 3.28 us -> 4.74 us
    all_gather x1 -> x0, waiting for transfers between devices: 59.3 us -> none  [body(): weight = lax.all_gather(out_weight, SEQ, axis=1, tiled=True)]
    ppermute x4 -> x21, starting transfers between devices: 5.26 us -> 36.4 us  [shift(): lax.ppermute(value, axis, [(i, (i + step) % size) for i in range(size)])]
    all_to_all x1 -> x0, blocking collectives: 30.2 us -> none  [body(): blocks = lax.all_to_all(blocks, CH, 0, 0)]
    ppermute x4 -> x21, waiting for transfers between devices: 4.72 us -> 28.4 us  [shift(): lax.ppermute(value, axis, [(i, (i + step) % size) for i in range(size)])]
    dot_general x1 -> x0, matrix products: 5.75 us -> none  [body(): jnp.dot(gated, weight, preferred_element_type=jnp.float32)]
    pallas_call x0 -> x1, Pallas kernels: none -> 3.05 us  [project(): pl.pallas_call(functools.partial(project_kernel, [len(block) for block in...]
    ppermute x1 -> x2, waiting for transfers between devices: 2.15 us -> 5.12 us  [the longest x1 5.12 us: incoming_state(): earlier = last_join(lax.ppermute(total, 'yh', [(0, 1)]))]
    select_n x0 -> x5, other arithmetic: none -> 2.22 us  [the longest x1 1.18 us: body(): second = jnp.where(core == 0, other, gated)]
  transfers between devices with their start and end apart: 6 -> 23, of which waited for: 5 -> 13; matrix products, arithmetic and copies ran while one was open for 1% -> 3% of each run, Pallas kernels for 4% -> 2%
where the time goes in v1:
time: 91.4 us; the launch traced here: 91.1 us
  starting transfers between devices  40.5 us (44%)
  waiting for transfers between devices  33.5 us (37%)
  Pallas kernels  8.54 us (9%)
  local copies, waits for them, and re-layouts  4.74 us (5%)
  other arithmetic  3.41 us (4%)
    ppermute x21, starting transfers between devices, shift(): lax.ppermute(value, axis, [(i, (i + step) % size) for i in range(size)])  36.4 us
    ppermute x21, waiting for transfers between devices, shift(): lax.ppermute(value, axis, [(i, (i + step) % size) for i in range(size)])  28.4 us
    ppermute x1, waiting for transfers between devices, incoming_state(): earlier = last_join(lax.ppermute(total, 'yh', [(0, 1)]))  5.12 us
    unnamed x45, local copies, waits for them, and re-layouts  4.31 us
    pallas_call x1, Pallas kernels, gate(): pl.pallas_call(gated_kernel, out_shape=jax.ShapeDtypeStruct(keys.shape, j...  3.78 us
    pallas_call x1, Pallas kernels, project(): pl.pallas_call(functools.partial(project_kernel, [len(block) for block in...  3.05 us
    ppermute x1, starting transfers between devices, incoming_state(): earlier = last_join(lax.ppermute(total, 'yh', [(0, 1)]))  2.75 us
  transfers between devices with their start and end apart: 23, of which 13 were waited for; matrix products, arithmetic and copies ran while one was open for 3% of the time, Pallas kernels for 2%

profile of v1, /device:TPU:1, one launch (start us, length us, event | category | flops | bytes accessed | tf_op | source)
XLA Modules:
  0.0 91.1 jit_solution(16595950788817685233)
XLA Ops:
  0.0 3.3 %collective-permute-start.3 = (bf16[1024,256]{1,0:T(8,128)(2,1)}, bf16[1024,256]{1,0:T(8,128)(2,1)S(1)}, u32[]{:S(2)}, u32[]{:S(2)}) collective-permute-start(bf16[1024,256]{1,0:T(8,128)(2,1)} %refs_0_.1), channel_id=1, source_target_pairs={{0,48},{16,0},{32,16},{48,32},{1,49},{17,1},{33,17},{49,33},{2,50}... | collective-permute-start | bytes 1572872 | tf_op jit(solution)/shard_map/ppermute | solution.py:21
  3.3 2.9 %collective-permute-start.4 = (bf16[1024,256]{1,0:T(8,128)(2,1)}, bf16[1024,256]{1,0:T(8,128)(2,1)S(1)}, u32[]{:S(2)}, u32[]{:S(2)}) collective-permute-start(bf16[1024,256]{1,0:T(8,128)(2,1)} %refs_0_.1), channel_id=1, source_target_pairs={{0,64},{64,0},{1,65},{65,1},{2,66},{66,2},{3,67},{67,3},{4,68},{68... | collective-permute-start | bytes 1572872 | tf_op jit(solution)/shard_map/ppermute | solution.py:21
  6.2 0.7 select_bitcast_fusion.3
  7.0 1.0 %copy-done.1 = bf16[256,1024]{1,0:T(8,128)(2,1)S(1)} copy-done((bf16[256,1024]{1,0:T(8,128)(2,1)S(1)}, bf16[256,1024]{1,0:T(8,128)(2,1)}, u32[]{:S(2)}) %copy-start.1) | copy-done | bytes 524312
  8.0 1.7 %end_state.1 = f32[16,8,128]{2,1,0:T(8,128)S(1)} custom-call(bf16[256,1024]{1,0:T(8,128)(2,1)S(1)} %copy-done, bf16[256,1024]{1,0:T(8,128)(2,1)S(1)} %copy-done.1, f32[16,8,128]{2,1,0:T(8,128)S(1)} %bitcast.169), custom_call_target="tpu_custom_call" | custom-call | flops 9000000 | bytes 1200000 | tf_op jit(solution)/shard_map/end_state/pallas_call | solution.py:77
  9.8 1.3 %collective-permute-start = (f32[16,8,128]{2,1,0:T(8,128)S(1)}, f32[16,8,128]{2,1,0:T(8,128)S(1)}, u32[]{:S(2)}, u32[]{:S(2)}) collective-permute-start(f32[16,8,128]{2,1,0:T(8,128)S(1)} %end_state.1), channel_id=1, source_target_pairs={{0,8},{8,0},{1,9},{9,1},{2,10},{10,2},{3,11},{11,3},{4,12},{12,4},... | collective-permute-start | bytes 196616 | tf_op jit(solution)/shard_map/ppermute | solution.py:21
  11.1 0.9 collective-permute-done
  12.0 0.6 copy-done.13
  12.6 0.5 collective-permute-start.1
  13.2 5.5 %collective-permute-done.1 = f32[16,8,128]{2,1,0:T(8,128)S(1)} collective-permute-done((f32[16,8,128]{2,1,0:T(8,128)S(1)}, f32[16,8,128]{2,1,0:T(8,128)S(1)}, u32[]{:S(2)}, u32[]{:S(2)}) %collective-permute-start.1) | collective-permute-done | bytes 65568 | tf_op jit(solution)/shard_map/ppermute | solution.py:21
  18.6 0.4 collective-permute-start.5
  19.2 3.0 %collective-permute-start.8 = (bf16[2,640,256]{2,1,0:T(8,128)(2,1)S(1)}, bf16[2,640,256]{2,1,0:T(8,128)(2,1)S(1)}, u32[]{:S(2)}, u32[]{:S(2)}) collective-permute-start(bf16[2,640,256]{2,1,0:T(8,128)(2,1)S(1)} %pad_maximum_fusion), channel_id=1, source_target_pairs={{0,64},{64,0},{1,65},{65,1},{2,66},{66,2},{3,67},{67,3},{4,68},{68... | collective-permute-start | bytes 1966088 | tf_op jit(solution)/shard_map/ppermute | solution.py:21
  22.2 1.3 %collective-permute-start.7 = (bf16[1024,256]{1,0:T(8,128)(2,1)S(1)}, bf16[1024,256]{1,0:T(8,128)(2,1)S(1)}, u32[]{:S(2)}, u32[]{:S(2)}) collective-permute-start(bf16[1024,256]{1,0:T(8,128)(2,1)S(1)} %broadcast_select_fusion), channel_id=1, source_target_pairs={{0,16},{8,56},{16,32},{24,8},{32,48},{40,24},{48,0},{56,40},{1,17}... | collective-permute-start | bytes 1572872 | tf_op jit(solution)/shard_map/ppermute | solution.py:133
  23.5 0.8 copy-done.12
  24.5 1.8 %collective-permute-start.10 = (bf16[384,256]{1,0:T(8,128)(2,1)S(1)}, bf16[384,256]{1,0:T(8,128)(2,1)S(1)}, u32[]{:S(2)}, u32[]{:S(2)}) collective-permute-start(bf16[384,256]{1,0:T(8,128)(2,1)S(1)} %slice.68), channel_id=1, source_target_pairs={{0,48},{16,0},{32,16},{48,32},{1,49},{17,1},{33,17},{49,33},{2,50}... | collective-permute-start | bytes 589832 | tf_op jit(solution)/shard_map/ppermute | solution.py:21
  26.3 2.7 %collective-permute-start.6 = (f32[16,8,128]{2,1,0:T(8,128)S(1)}, f32[16,8,128]{2,1,0:T(8,128)S(1)}, u32[]{:S(2)}, u32[]{:S(2)}) collective-permute-start(f32[16,8,128]{2,1,0:T(8,128)S(1)} %fusion.8), channel_id=1, source_target_pairs={{0,64},{1,65},{2,66},{3,67},{4,68},{5,69},{6,70},{7,71},{8,72},{9,... | collective-permute-start | bytes 196616 | tf_op jit(solution)/shard_map/ppermute | solution.py:117
  29.1 0.8 copy-done.10
  30.0 5.1 %collective-permute-done.6 = f32[16,8,128]{2,1,0:T(8,128)S(1)} collective-permute-done((f32[16,8,128]{2,1,0:T(8,128)S(1)}, f32[16,8,128]{2,1,0:T(8,128)S(1)}, u32[]{:S(2)}, u32[]{:S(2)}) %collective-permute-start.6) | collective-permute-done | bytes 65568 | tf_op jit(solution)/shard_map/ppermute | solution.py:117
  35.1 0.5 collective-permute-done.10.refs_10_
  35.8 0.6 copy-done.6
  36.4 0.2 copy-done.8
  36.6 3.8 %gated.1 = bf16[256,1024]{1,0:T(8,128)(2,1)S(1)} custom-call(bf16[256,1024]{1,0:T(8,128)(2,1)S(1)} %copy-done, bf16[256,1024]{1,0:T(8,128)(2,1)S(1)} %copy-done.2, bf16[256,1024]{1,0:T(8,128)(2,1)S(1)} %copy-done.3, f32[16,8,128]{2,1,0:T(8,128)S(1)} %bitcast.170, f32[16,8,128]{2,1,0:T(8,128)S(1)} %bitcast_multiply_fusion.10.gain_ref, ...), custom_call_target="tpu_custom_call" | custom-call | flops 18000000 | bytes 2500000 | tf_op jit(solution)/shard_map/gated/pallas_call | solution.py:89
  40.4 4.0 %collective-permute-start.11 = (bf16[256,1024]{1,0:T(8,128)(2,1)S(1)}, bf16[256,1024]{1,0:T(8,128)(2,1)}, u32[]{:S(2)}, u32[]{:S(2)}) collective-permute-start(bf16[256,1024]{1,0:T(8,128)(2,1)S(1)} %gated.1), channel_id=1, source_target_pairs={{0,8},{8,0},{1,9},{9,1},{2,10},{10,2},{3,11},{11,3},{4,12},{12,4},... | collective-permute-start | bytes 1572872 | tf_op jit(solution)/shard_map/ppermute | solution.py:21
  44.6 1.6 %collective-permute-start.13 = (bf16[512,256]{1,0:T(8,128)(2,1)S(1)}, bf16[512,256]{1,0:T(8,128)(2,1)S(1)}, u32[]{:S(2)}, u32[]{:S(2)}) collective-permute-start(bf16[512,256]{1,0:T(8,128)(2,1)S(1)} %slice.71), channel_id=1, source_target_pairs={{0,32},{16,48},{32,0},{48,16},{1,33},{17,49},{33,1},{49,17},{2,34}... | collective-permute-start | bytes 786440 | tf_op jit(solution)/shard_map/ppermute | solution.py:21
  46.3 3.8 %collective-permute-start.12 = (bf16[512,256]{1,0:T(8,128)(2,1)S(1)}, bf16[512,256]{1,0:T(8,128)(2,1)S(1)}, u32[]{:S(2)}, u32[]{:S(2)}) collective-permute-start(bf16[512,256]{1,0:T(8,128)(2,1)S(1)} %slice.70), channel_id=1, source_target_pairs={{0,64},{64,0},{1,65},{65,1},{2,66},{66,2},{3,67},{67,3},{4,68},{68... | collective-permute-start | bytes 786440 | tf_op jit(solution)/shard_map/ppermute | solution.py:21
  50.1 1.2 %broadcast_select_fusion.1 = (bf16[256,1024]{1,0:T(8,128)(2,1)S(1)}, bf16[256,1024]{1,0:T(8,128)(2,1)S(1)}) fusion(bf16[256,1024]{1,0:T(8,128)(2,1)} %collective-permute-done.11, bf16[256,1024]{1,0:T(8,128)(2,1)S(1)} %gated.1, pred[]{:T(512)S(6)} %eq.43), kind=kLoop, calls=%fused_computation.9 | loop fusion | flops 524288 | bytes 2097153 | tf_op jit(solution)/shard_map/jit(_where)/select_n | solution.py:217
  51.3 2.3 %collective-permute-done.13.refs_8_ = bf16[512,256]{1,0:T(8,128)(2,1)S(1)} collective-permute-done((bf16[512,256]{1,0:T(8,128)(2,1)S(1)}, bf16[512,256]{1,0:T(8,128)(2,1)S(1)}, u32[]{:S(2)}, u32[]{:S(2)}) %collective-permute-start.13) | collective-permute-done | bytes 262176 | tf_op jit(solution)/shard_map/ppermute | solution.py:21
  53.6 2.4 %collective-permute-done.12.refs_7_ = bf16[512,256]{1,0:T(8,128)(2,1)S(1)} collective-permute-done((bf16[512,256]{1,0:T(8,128)(2,1)S(1)}, bf16[512,256]{1,0:T(8,128)(2,1)S(1)}, u32[]{:S(2)}, u32[]{:S(2)}) %collective-permute-start.12) | collective-permute-done | bytes 262176 | tf_op jit(solution)/shard_map/ppermute | solution.py:21
  56.0 3.0 %project.1 = (bf16[2,4,256,256]{3,2,1,0:T(8,128)(2,1)S(1)}, bf16[4,2,256,256]{3,2,1,0:T(8,128)(2,1)S(1)}) custom-call(bf16[256,1024]{1,0:T(8,128)(2,1)S(1)} %get-tuple-element.35.first_ref, bf16[256,1024]{1,0:T(8,128)(2,1)S(1)} %get-tuple-element.34.second_ref, s32[2,8]{1,0:T(2,128)S(1)} %pad_add_fusion.slot_ref, bf16[1024,256]{1,0:T(8,128)(2,1)S(1)} %copy-done.5, ...), custom_call_target="tpu_custom_call" | custom-call | flops 2200000000 | bytes 7000000 | tf_op jit(solution)/shard_map/project/pallas_call | solution.py:169
  59.1 1.7 %collective-permute-start.18 = (bf16[2,256,256]{2,1,0:T(8,128)(2,1)S(1)}, bf16[2,256,256]{2,1,0:T(8,128)(2,1)S(1)}, u32[]{:S(2)}, u32[]{:S(2)}) collective-permute-start(bf16[2,256,256]{2,1,0:T(8,128)(2,1)S(1)} %get-tuple-element.31), channel_id=1, source_target_pairs={{0,2},{2,4},{4,6},{6,0},{1,3},{3,5},{5,7},{7,1},{8,10},{10,12},{12... | collective-permute-start | bytes 786440 | tf_op jit(solution)/shard_map/ppermute | solution.py:21
  60.9 3.3 %collective-permute-start.20 = (bf16[2,256,256]{2,1,0:T(8,128)(2,1)S(1)}, bf16[2,256,256]{2,1,0:T(8,128)(2,1)S(1)}, u32[]{:S(2)}, u32[]{:S(2)}) collective-permute-start(bf16[2,256,256]{2,1,0:T(8,128)(2,1)S(1)} %get-tuple-element.32), channel_id=1, source_target_pairs={{0,4},{2,6},{4,0},{6,2},{1,5},{3,7},{5,1},{7,3},{8,12},{10,14},{12... | collective-permute-start | bytes 786440 | tf_op jit(solution)/shard_map/ppermute | solution.py:21
  64.2 0.7 collective-permute-start.19
  64.9 0.5 collective-permute-start.14
  65.4 2.9 %collective-permute-done.18 = bf16[2,256,256]{2,1,0:T(8,128)(2,1)S(1)} collective-permute-done((bf16[2,256,256]{2,1,0:T(8,128)(2,1)S(1)}, bf16[2,256,256]{2,1,0:T(8,128)(2,1)S(1)}, u32[]{:S(2)}, u32[]{:S(2)}) %collective-permute-start.18) | collective-permute-done | bytes 262176 | tf_op jit(solution)/shard_map/ppermute | solution.py:21
  68.3 6.5 %collective-permute-done.20 = bf16[2,256,256]{2,1,0:T(8,128)(2,1)S(1)} collective-permute-done((bf16[2,256,256]{2,1,0:T(8,128)(2,1)S(1)}, bf16[2,256,256]{2,1,0:T(8,128)(2,1)S(1)}, u32[]{:S(2)}, u32[]{:S(2)}) %collective-permute-start.20) | collective-permute-done | bytes 262176 | tf_op jit(solution)/shard_map/ppermute | solution.py:21
  74.8 0.2 collective-permute-done.19
  75.0 0.1 fusion.3
  75.2 0.5 collective-permute-start.21
  75.6 0.6 collective-permute-done.14
  76.3 0.1 fusion
  76.5 1.5 %collective-permute-start.15 = (bf16[256,256]{1,0:T(8,128)(2,1)S(1)}, bf16[256,256]{1,0:T(8,128)(2,1)S(1)}, u32[]{:S(2)}, u32[]{:S(2)}) collective-permute-start(bf16[256,256]{1,0:T(8,128)(2,1)S(1)} %get-tuple-element.38), channel_id=1, source_target_pairs={{0,2},{2,4},{4,6},{6,0},{1,3},{3,5},{5,7},{7,1},{8,10},{10,12},{12... | collective-permute-start | bytes 393224 | tf_op jit(solution)/shard_map/ppermute | solution.py:21
  78.0 2.5 %collective-permute-start.17 = (bf16[256,256]{1,0:T(8,128)(2,1)S(1)}, bf16[256,256]{1,0:T(8,128)(2,1)S(1)}, u32[]{:S(2)}, u32[]{:S(2)}) collective-permute-start(bf16[256,256]{1,0:T(8,128)(2,1)S(1)} %get-tuple-element.39), channel_id=1, source_target_pairs={{0,4},{2,6},{4,0},{6,2},{1,5},{3,7},{5,1},{7,3},{8,12},{10,14},{12... | collective-permute-start | bytes 393224 | tf_op jit(solution)/shard_map/ppermute | solution.py:21
  80.5 1.2 %collective-permute-done.15 = bf16[256,256]{1,0:T(8,128)(2,1)S(1)} collective-permute-done((bf16[256,256]{1,0:T(8,128)(2,1)S(1)}, bf16[256,256]{1,0:T(8,128)(2,1)S(1)}, u32[]{:S(2)}, u32[]{:S(2)}) %collective-permute-start.15) | collective-permute-done | bytes 131104 | tf_op jit(solution)/shard_map/ppermute | solution.py:21
  81.7 4.4 %collective-permute-done.17 = bf16[256,256]{1,0:T(8,128)(2,1)S(1)} collective-permute-done((bf16[256,256]{1,0:T(8,128)(2,1)S(1)}, bf16[256,256]{1,0:T(8,128)(2,1)S(1)}, u32[]{:S(2)}, u32[]{:S(2)}) %collective-permute-start.17) | collective-permute-done | bytes 131104 | tf_op jit(solution)/shard_map/ppermute | solution.py:21
  86.1 0.1 broadcast_select_fusion.4
  86.2 3.0 %collective-permute-start.22 = (bf16[256,256]{1,0:T(8,128)(2,1)S(1)}, bf16[256,256]{1,0:T(8,128)(2,1)S(1)}, u32[]{:S(2)}, u32[]{:S(2)}) collective-permute-start(bf16[256,256]{1,0:T(8,128)(2,1)S(1)} %broadcast_select_fusion.3), channel_id=1, source_target_pairs={{0,8},{8,0},{1,9},{9,1},{2,10},{10,2},{3,11},{11,3},{4,12},{12,4},... | collective-permute-start | bytes 393224 | tf_op jit(solution)/shard_map/ppermute | solution.py:21
  89.2 1.0 %collective-permute-done.22 = bf16[256,256]{1,0:T(8,128)(2,1)S(1)} collective-permute-done((bf16[256,256]{1,0:T(8,128)(2,1)S(1)}, bf16[256,256]{1,0:T(8,128)(2,1)S(1)}, u32[]{:S(2)}, u32[]{:S(2)}) %collective-permute-start.22) | collective-permute-done | bytes 131104 | tf_op jit(solution)/shard_map/ppermute | solution.py:21
  90.2 0.8 maximum_select_fusion
  (72 shorter events, 1.0 us)
Async XLA Ops:
  0.0 6.2 %copy-start.15 = (f32[1024,16]{0,1:T(8,128)S(1)}, f32[1024,16]{0,1:T(8,128)}, u32[]{:S(2)}) copy-start(f32[1024,16]{0,1:T(8,128)} %param.10) | copy-start | bytes 196612
  0.0 7.0 %copy-start = (bf16[256,1024]{1,0:T(8,128)(2,1)S(1)}, bf16[256,1024]{1,0:T(8,128)(2,1)}, u32[]{:S(2)}) copy-start(bf16[256,1024]{1,0:T(8,128)(2,1)} %keys_ref.3) | copy-start | bytes 1572868
  0.0 18.6 %collective-permute-start.3 = (bf16[1024,256]{1,0:T(8,128)(2,1)}, bf16[1024,256]{1,0:T(8,128)(2,1)S(1)}, u32[]{:S(2)}, u32[]{:S(2)}) collective-permute-start(bf16[1024,256]{1,0:T(8,128)(2,1)} %refs_0_.1), channel_id=1, source_target_pairs={{0,48},{16,0},{32,16},{48,32},{1,49},{17,1},{33,17},{49,33},{2,50}... | collective-permute-start | bytes 1572872 | tf_op jit(solution)/shard_map/ppermute | solution.py:21
  3.3 15.3 %collective-permute-start.2 = (bf16[1024,256]{1,0:T(8,128)(2,1)}, bf16[1024,256]{1,0:T(8,128)(2,1)S(1)}, u32[]{:S(2)}, u32[]{:S(2)}) collective-permute-start(bf16[1024,256]{1,0:T(8,128)(2,1)} %refs_0_.1), channel_id=1, source_target_pairs={{0,16},{16,32},{32,48},{48,0},{1,17},{17,33},{33,49},{49,1},{2,18}... | collective-permute-start | bytes 1572872 | tf_op jit(solution)/shard_map/ppermute | solution.py:21
  3.3 15.3 %collective-permute-start.4 = (bf16[1024,256]{1,0:T(8,128)(2,1)}, bf16[1024,256]{1,0:T(8,128)(2,1)S(1)}, u32[]{:S(2)}, u32[]{:S(2)}) collective-permute-start(bf16[1024,256]{1,0:T(8,128)(2,1)} %refs_0_.1), channel_id=1, source_target_pairs={{0,64},{64,0},{1,65},{65,1},{2,66},{66,2},{3,67},{67,3},{4,68},{68... | collective-permute-start | bytes 1572872 | tf_op jit(solution)/shard_map/ppermute | solution.py:21
  7.0 1.0 %copy-start.1 = (bf16[256,1024]{1,0:T(8,128)(2,1)S(1)}, bf16[256,1024]{1,0:T(8,128)(2,1)}, u32[]{:S(2)}) copy-start(bf16[256,1024]{1,0:T(8,128)(2,1)} %values_ref.3) | copy-start | bytes 1572868
  9.8 2.2 %collective-permute-start = (f32[16,8,128]{2,1,0:T(8,128)S(1)}, f32[16,8,128]{2,1,0:T(8,128)S(1)}, u32[]{:S(2)}, u32[]{:S(2)}) collective-permute-start(f32[16,8,128]{2,1,0:T(8,128)S(1)} %end_state.1), channel_id=1, source_target_pairs={{0,8},{8,0},{1,9},{9,1},{2,10},{10,2},{3,11},{11,3},{4,12},{12,4},... | collective-permute-start | bytes 196616 | tf_op jit(solution)/shard_map/ppermute | solution.py:21
  12.0 0.6 copy-start.13
  12.6 6.0 %collective-permute-start.1 = (f32[16,8,128]{2,1,0:T(8,128)S(1)}, f32[16,8,128]{2,1,0:T(8,128)S(1)}, u32[]{:S(2)}, u32[]{:S(2)}) collective-permute-start(f32[16,8,128]{2,1,0:T(8,128)S(1)} %fusion.14), channel_id=1, source_target_pairs={{0,16},{16,32},{32,48},{48,0},{1,17},{17,33},{33,49},{49,1},{2,18}... | collective-permute-start | bytes 196616 | tf_op jit(solution)/shard_map/ppermute | solution.py:21
  18.6 7.6 %collective-permute-start.5 = (f32[2,16,8,128]{3,2,1,0:T(8,128)S(1)}, f32[2,16,8,128]{3,2,1,0:T(8,128)S(1)}, u32[]{:S(2)}, u32[]{:S(2)}) collective-permute-start(f32[2,16,8,128]{3,2,1,0:T(8,128)S(1)} %pad_maximum_fusion.1), channel_id=1, source_target_pairs={{0,32},{16,48},{32,0},{48,16},{1,33},{17,49},{33,1},{49,17},{2,34}... | collective-permute-start | bytes 393224 | tf_op jit(solution)/shard_map/ppermute | solution.py:21
  19.2 4.3 %copy-start.16 = (f32[1024,16]{0,1:T(8,128)S(1)}, f32[1024,16]{0,1:T(8,128)}, u32[]{:S(2)}) copy-start(f32[1024,16]{0,1:T(8,128)} %param.11) | copy-start | bytes 196612
  19.2 16.5 %collective-permute-start.8 = (bf16[2,640,256]{2,1,0:T(8,128)(2,1)S(1)}, bf16[2,640,256]{2,1,0:T(8,128)(2,1)S(1)}, u32[]{:S(2)}, u32[]{:S(2)}) collective-permute-start(bf16[2,640,256]{2,1,0:T(8,128)(2,1)S(1)} %pad_maximum_fusion), channel_id=1, source_target_pairs={{0,64},{64,0},{1,65},{65,1},{2,66},{66,2},{3,67},{67,3},{4,68},{68... | collective-permute-start | bytes 1966088 | tf_op jit(solution)/shard_map/ppermute | solution.py:21
  22.2 13.5 %collective-permute-start.7 = (bf16[1024,256]{1,0:T(8,128)(2,1)S(1)}, bf16[1024,256]{1,0:T(8,128)(2,1)S(1)}, u32[]{:S(2)}, u32[]{:S(2)}) collective-permute-start(bf16[1024,256]{1,0:T(8,128)(2,1)S(1)} %broadcast_select_fusion), channel_id=1, source_target_pairs={{0,16},{8,56},{16,32},{24,8},{32,48},{40,24},{48,0},{56,40},{1,17}... | collective-permute-start | bytes 1572872 | tf_op jit(solution)/shard_map/ppermute | solution.py:133
  23.5 0.8 copy-start.12
  24.5 11.2 %collective-permute-start.10 = (bf16[384,256]{1,0:T(8,128)(2,1)S(1)}, bf16[384,256]{1,0:T(8,128)(2,1)S(1)}, u32[]{:S(2)}, u32[]{:S(2)}) collective-permute-start(bf16[384,256]{1,0:T(8,128)(2,1)S(1)} %slice.68), channel_id=1, source_target_pairs={{0,48},{16,0},{32,16},{48,32},{1,49},{17,1},{33,17},{49,33},{2,50}... | collective-permute-start | bytes 589832 | tf_op jit(solution)/shard_map/ppermute | solution.py:21
  26.2 9.4 %collective-permute-start.9 = (bf16[384,256]{1,0:T(8,128)(2,1)S(1)}, bf16[384,256]{1,0:T(8,128)(2,1)S(1)}, u32[]{:S(2)}, u32[]{:S(2)}) collective-permute-start(bf16[384,256]{1,0:T(8,128)(2,1)S(1)} %slice.68), channel_id=1, source_target_pairs={{0,16},{16,32},{32,48},{48,0},{1,17},{17,33},{33,49},{49,1},{2,18}... | collective-permute-start | bytes 589832 | tf_op jit(solution)/shard_map/ppermute | solution.py:21
  26.3 2.8 %copy-start.11 = (f32[2,8,8,128]{3,1,2,0:T(8,128)S(1)}, f32[2,8,8,128]{3,1,2,0:T(8,128)}, u32[]{:S(2)}) copy-start(f32[2,8,8,128]{3,1,2,0:T(8,128)} %get-tuple-element.41) | copy-start | bytes 196612
  26.3 8.8 %collective-permute-start.6 = (f32[16,8,128]{2,1,0:T(8,128)S(1)}, f32[16,8,128]{2,1,0:T(8,128)S(1)}, u32[]{:S(2)}, u32[]{:S(2)}) collective-permute-start(f32[16,8,128]{2,1,0:T(8,128)S(1)} %fusion.8), channel_id=1, source_target_pairs={{0,64},{1,65},{2,66},{3,67},{4,68},{5,69},{6,70},{7,71},{8,72},{9,... | collective-permute-start | bytes 196616 | tf_op jit(solution)/shard_map/ppermute | solution.py:117
  29.1 0.8 copy-start.10
  29.9 5.8 %copy-start.14 = (f32[16,8,128]{2,1,0:T(8,128)S(1)}, f32[16,8,128]{2,1,0:T(8,128)}, u32[]{:S(2)}) copy-start(f32[16,8,128]{2,1,0:T(8,128)} %copy-done.13) | copy-start | bytes 196612
  30.0 6.6 %copy-start.2 = (bf16[256,1024]{1,0:T(8,128)(2,1)S(1)}, bf16[256,1024]{1,0:T(8,128)(2,1)}, u32[]{:S(2)}) copy-start(bf16[256,1024]{1,0:T(8,128)(2,1)} %values_ref.3) | copy-start | bytes 1572868
  30.0 6.6 %copy-start.3 = (bf16[256,1024]{1,0:T(8,128)(2,1)S(1)}, bf16[256,1024]{1,0:T(8,128)(2,1)}, u32[]{:S(2)}) copy-start(bf16[256,1024]{1,0:T(8,128)(2,1)} %queries_ref.1) | copy-start | bytes 1572868
  35.7 0.7 copy-start.6
  35.7 0.9 copy-start.8
  35.7 0.9 copy-start.4
  40.4 9.8 %collective-permute-start.11 = (bf16[256,1024]{1,0:T(8,128)(2,1)S(1)}, bf16[256,1024]{1,0:T(8,128)(2,1)}, u32[]{:S(2)}, u32[]{:S(2)}) collective-permute-start(bf16[256,1024]{1,0:T(8,128)(2,1)S(1)} %gated.1), channel_id=1, source_target_pairs={{0,8},{8,0},{1,9},{9,1},{2,10},{10,2},{3,11},{11,3},{4,12},{12,4},... | collective-permute-start | bytes 1572872 | tf_op jit(solution)/shard_map/ppermute | solution.py:21
  44.4 5.7 %copy-start.9 = (bf16[2,640,256]{2,1,0:T(8,128)(2,1)S(1)}, bf16[2,640,256]{2,1,0:T(8,128)(2,1)}, u32[]{:S(2)}) copy-start(bf16[2,640,256]{2,1,0:T(8,128)(2,1)} %copy-done.8) | copy-start | bytes 1966084
  44.6 9.0 %collective-permute-start.13 = (bf16[512,256]{1,0:T(8,128)(2,1)S(1)}, bf16[512,256]{1,0:T(8,128)(2,1)S(1)}, u32[]{:S(2)}, u32[]{:S(2)}) collective-permute-start(bf16[512,256]{1,0:T(8,128)(2,1)S(1)} %slice.71), channel_id=1, source_target_pairs={{0,32},{16,48},{32,0},{48,16},{1,33},{17,49},{33,1},{49,17},{2,34}... | collective-permute-start | bytes 786440 | tf_op jit(solution)/shard_map/ppermute | solution.py:21
  46.3 9.8 %collective-permute-start.12 = (bf16[512,256]{1,0:T(8,128)(2,1)S(1)}, bf16[512,256]{1,0:T(8,128)(2,1)S(1)}, u32[]{:S(2)}, u32[]{:S(2)}) collective-permute-start(bf16[512,256]{1,0:T(8,128)(2,1)S(1)} %slice.70), channel_id=1, source_target_pairs={{0,64},{64,0},{1,65},{65,1},{2,66},{66,2},{3,67},{67,3},{4,68},{68... | collective-permute-start | bytes 786440 | tf_op jit(solution)/shard_map/ppermute | solution.py:21
  50.1 5.9 %copy-start.5 = (bf16[1024,256]{1,0:T(8,128)(2,1)S(1)}, bf16[1024,256]{1,0:T(8,128)(2,1)}, u32[]{:S(2)}) copy-start(bf16[1024,256]{1,0:T(8,128)(2,1)} %refs_0_.1) | copy-start | bytes 1572868
  50.1 5.9 %copy-start.7 = (bf16[384,256]{1,0:T(8,128)(2,1)S(1)}, bf16[384,256]{1,0:T(8,128)(2,1)}, u32[]{:S(2)}) copy-start(bf16[384,256]{1,0:T(8,128)(2,1)} %copy-done.6) | copy-start | bytes 589828
  59.1 9.2 %collective-permute-start.18 = (bf16[2,256,256]{2,1,0:T(8,128)(2,1)S(1)}, bf16[2,256,256]{2,1,0:T(8,128)(2,1)S(1)}, u32[]{:S(2)}, u32[]{:S(2)}) collective-permute-start(bf16[2,256,256]{2,1,0:T(8,128)(2,1)S(1)} %get-tuple-element.31), channel_id=1, source_target_pairs={{0,2},{2,4},{4,6},{6,0},{1,3},{3,5},{5,7},{7,1},{8,10},{10,12},{12... | collective-permute-start | bytes 786440 | tf_op jit(solution)/shard_map/ppermute | solution.py:21
  60.9 13.9 %collective-permute-start.20 = (bf16[2,256,256]{2,1,0:T(8,128)(2,1)S(1)}, bf16[2,256,256]{2,1,0:T(8,128)(2,1)S(1)}, u32[]{:S(2)}, u32[]{:S(2)}) collective-permute-start(bf16[2,256,256]{2,1,0:T(8,128)(2,1)S(1)} %get-tuple-element.32), channel_id=1, source_target_pairs={{0,4},{2,6},{4,0},{6,2},{1,5},{3,7},{5,1},{7,3},{8,12},{10,14},{12... | collective-permute-start | bytes 786440 | tf_op jit(solution)/shard_map/ppermute | solution.py:21
  64.2 10.8 %collective-permute-start.19 = (bf16[2,256,256]{2,1,0:T(8,128)(2,1)S(1)}, bf16[2,256,256]{2,1,0:T(8,128)(2,1)S(1)}, u32[]{:S(2)}, u32[]{:S(2)}) collective-permute-start(bf16[2,256,256]{2,1,0:T(8,128)(2,1)S(1)} %get-tuple-element.33), channel_id=1, source_target_pairs={{0,6},{2,0},{4,2},{6,4},{1,7},{3,1},{5,3},{7,5},{8,14},{10,8},{12,... | collective-permute-start | bytes 786440 | tf_op jit(solution)/shard_map/ppermute | solution.py:21
  64.9 11.4 %collective-permute-start.14 = (bf16[4,256,256]{2,1,0:T(8,128)(2,1)S(1)}, bf16[4,256,256]{2,1,0:T(8,128)(2,1)S(1)}, u32[]{:S(2)}, u32[]{:S(2)}) collective-permute-start(bf16[4,256,256]{2,1,0:T(8,128)(2,1)S(1)} %slice_bitcast_fusion), channel_id=1, source_target_pairs={{0,1},{1,0},{2,3},{3,2},{4,5},{5,4},{6,7},{7,6},{8,9},{9,8},{10,11... | collective-permute-start | bytes 1572872 | tf_op jit(solution)/shard_map/ppermute | solution.py:21
  75.2 5.3 %collective-permute-start.21 = (bf16[256,256]{1,0:T(8,128)(2,1)S(1)}, bf16[256,256]{1,0:T(8,128)(2,1)S(1)}, u32[]{:S(2)}, u32[]{:S(2)}) collective-permute-start(bf16[256,256]{1,0:T(8,128)(2,1)S(1)} %slice_bitcast_fusion.8), channel_id=1, source_target_pairs={{0,1},{1,0},{2,3},{3,2},{4,5},{5,4},{6,7},{7,6},{8,9},{9,8},{10,11... | collective-permute-start | bytes 393224 | tf_op jit(solution)/shard_map/ppermute | solution.py:21
  76.5 5.2 %collective-permute-start.15 = (bf16[256,256]{1,0:T(8,128)(2,1)S(1)}, bf16[256,256]{1,0:T(8,128)(2,1)S(1)}, u32[]{:S(2)}, u32[]{:S(2)}) collective-permute-start(bf16[256,256]{1,0:T(8,128)(2,1)S(1)} %get-tuple-element.38), channel_id=1, source_target_pairs={{0,2},{2,4},{4,6},{6,0},{1,3},{3,5},{5,7},{7,1},{8,10},{10,12},{12... | collective-permute-start | bytes 393224 | tf_op jit(solution)/shard_map/ppermute | solution.py:21
  78.0 8.1 %collective-permute-start.17 = (bf16[256,256]{1,0:T(8,128)(2,1)S(1)}, bf16[256,256]{1,0:T(8,128)(2,1)S(1)}, u32[]{:S(2)}, u32[]{:S(2)}) collective-permute-start(bf16[256,256]{1,0:T(8,128)(2,1)S(1)} %get-tuple-element.39), channel_id=1, source_target_pairs={{0,4},{2,6},{4,0},{6,2},{1,5},{3,7},{5,1},{7,3},{8,12},{10,14},{12... | collective-permute-start | bytes 393224 | tf_op jit(solution)/shard_map/ppermute | solution.py:21
  80.5 5.6 %collective-permute-start.16 = (bf16[256,256]{1,0:T(8,128)(2,1)S(1)}, bf16[256,256]{1,0:T(8,128)(2,1)S(1)}, u32[]{:S(2)}, u32[]{:S(2)}) collective-permute-start(bf16[256,256]{1,0:T(8,128)(2,1)S(1)} %get-tuple-element.40), channel_id=1, source_target_pairs={{0,6},{2,0},{4,2},{6,4},{1,7},{3,1},{5,3},{7,5},{8,14},{10,8},{12,... | collective-permute-start | bytes 393224 | tf_op jit(solution)/shard_map/ppermute | solution.py:21
  86.2 4.0 %collective-permute-start.22 = (bf16[256,256]{1,0:T(8,128)(2,1)S(1)}, bf16[256,256]{1,0:T(8,128)(2,1)S(1)}, u32[]{:S(2)}, u32[]{:S(2)}) collective-permute-start(bf16[256,256]{1,0:T(8,128)(2,1)S(1)} %broadcast_select_fusion.3), channel_id=1, source_target_pairs={{0,8},{8,0},{1,9},{9,1},{2,10},{10,2},{3,11},{11,3},{4,12},{12,4},... | collective-permute-start | bytes 393224 | tf_op jit(solution)/shard_map/ppermute | solution.py:21

commit v2 on v0

v2 whole, which is shorter than its diff:
```python
import functools

import jax
import jax.numpy as jnp
from jax import lax
from jax.experimental import pallas as pl
from jax.experimental.pallas import tpu as pltpu
from jax.sharding import Mesh, PartitionSpec as P

SEQ = ("yh", "x", "core")
CH = ("z", "yl")
ALL = SEQ + CH
SIZES = {"yh": 2, "x": 4, "core": 2, "z": 4, "yl": 2}
LANES = 128
CUT = 32
ROWS = 8


def shift(value, axis, step):
    size = SIZES[axis]
    return lax.ppermute(value, axis, [(i, (i + step) % size) for i in range(size)])


def spread_rows(keys_ref, values_ref, z_ref):
    steps = keys_ref.shape[0]
    for block in range(ROWS):
        lanes = pl.ds(block * LANES, LANES)
        product = keys_ref[:, lanes].astype(jnp.float32) * values_ref[:, lanes].astype(jnp.float32)
        z_ref[pl.ds(block * steps, steps), :] = product.astype(jnp.bfloat16).astype(jnp.float32)


def spread_modes(array_ref, spread_ref):
    modes = array_ref.shape[0]
    for block in range(ROWS):
        spread_ref[pl.ds(block * modes, modes), :] = array_ref[:, pl.ds(block * LANES, LANES)]
    return [spread_ref[pl.ds(n, ROWS, stride=modes), :] for n in range(modes)]


def end_state_kernel(
    seq_len, keys_ref, values_ref, decay_ref, residue_ref, state_ref, rate_ref, gain_ref, z_ref, spread_ref
):
    steps = keys_ref.shape[0]
    modes = decay_ref.shape[0]
    spread_rows(keys_ref, values_ref, z_ref)
    rate = [decay * jnp.float32(1.0 / seq_len) for decay in spread_modes(decay_ref, spread_ref)]
    keep = [jnp.exp(-r) for r in rate]
    for n in range(modes):
        rate_ref[n] = rate[n]

    def step(t, states):
        z = z_ref[pl.ds(t, ROWS, stride=steps), :]
        return tuple(keep[n] * states[n] + z for n in range(modes))

    start = tuple(jnp.zeros((ROWS, LANES), jnp.float32) for _ in range(modes))
    states = lax.fori_loop(0, steps, step, start, unroll=8)
    for n in range(modes):
        state_ref[n] = states[n]
    residue = spread_modes(residue_ref, spread_ref)
    for n in range(modes):
        gain_ref[n] = residue[n] * jnp.sqrt(rate_ref[n])


def local_kernel(keys_ref, values_ref, rate_ref, gain_ref, skip_ref, y_ref, z_ref):
    steps = keys_ref.shape[0]
    modes = rate_ref.shape[0]
    spread_rows(keys_ref, values_ref, z_ref)
    keep = [jnp.exp(-rate_ref[n]) for n in range(modes)]
    gain = [gain_ref[n] for n in range(modes)]
    skip = skip_ref[...]

    def step(t, states):
        at = pl.ds(t, ROWS, stride=steps)
        z = z_ref[at, :]
        states = tuple(keep[n] * states[n] + z for n in range(modes))
        y_ref[at, :] = tree_sum([gain[n] * states[n] for n in range(modes)] + [skip * z])
        return states

    start = tuple(jnp.zeros((ROWS, LANES), jnp.float32) for _ in range(modes))
    lax.fori_loop(0, steps, step, start, unroll=4)


def gated_kernel(queries_ref, y_ref, rate_ref, gain_ref, state_ref, out_ref, sum_ref):
    steps = queries_ref.shape[0]
    modes = rate_ref.shape[0]
    keep = [jnp.exp(-rate_ref[n]) for n in range(modes)]

    def step(t, terms):
        at = pl.ds(t, ROWS, stride=steps)
        terms = tuple(keep[n] * terms[n] for n in range(modes))
        sum_ref[at, :] = y_ref[at, :] + tree_sum(list(terms))
        return terms

    lax.fori_loop(0, steps, step, tuple(gain_ref[n] * state_ref[n] for n in range(modes)), unroll=8)
    for block in range(ROWS):
        lanes = pl.ds(block * LANES, LANES)
        y = sum_ref[pl.ds(block * steps, steps), :]
        out_ref[:, lanes] = (queries_ref[:, lanes].astype(jnp.float32) * y).astype(jnp.bfloat16)


def tree_sum(terms):
    while len(terms) > 1:
        terms = [sum(terms[i + 1 : i + 2], terms[i]) for i in range(0, len(terms), 2)]
    return terms[0]


def end_state(keys, values, decay, residue, seq_len):
    steps = keys.shape[0]
    modes = decay.shape[1]
    by_mode = jax.ShapeDtypeStruct((modes, ROWS, LANES), jnp.float32)
    return pl.pallas_call(
        functools.partial(end_state_kernel, seq_len),
        out_shape=(by_mode,) * 3,
        scratch_shapes=[
            pltpu.VMEM((ROWS * steps, LANES), jnp.float32),
            pltpu.VMEM((ROWS * modes, LANES), jnp.float32),
        ],
        compiler_params=pltpu.CompilerParams(vmem_limit_bytes=32 * 1024 * 1024),
        cost_estimate=pl.CostEstimate(flops=9000000, bytes_accessed=1200000, transcendentals=0),
        name="end_state",
    )(keys, values, decay.T, residue.T)


def local_part(keys, values, rate, gain, skip):
    steps = keys.shape[0]
    return pl.pallas_call(
        local_kernel,
        out_shape=jax.ShapeDtypeStruct((ROWS * steps, LANES), jnp.float32),
        scratch_shapes=[pltpu.VMEM((ROWS * steps, LANES), jnp.float32)],
        compiler_params=pltpu.CompilerParams(vmem_limit_bytes=32 * 1024 * 1024),
        cost_estimate=pl.CostEstimate(flops=0, bytes_accessed=0, transcendentals=0),
        name="local_part",
    )(keys, values, rate, gain, skip)


def gate(queries, local, rate, gain, state):
    return pl.pallas_call(
        gated_kernel,
        out_shape=jax.ShapeDtypeStruct(queries.shape, jnp.bfloat16),
        scratch_shapes=[pltpu.VMEM(local.shape, jnp.float32)],
        compiler_params=pltpu.CompilerParams(vmem_limit_bytes=32 * 1024 * 1024),
        cost_estimate=pl.CostEstimate(flops=0, bytes_accessed=0, transcendentals=0),
        name="gated",
    )(queries, local, rate, gain, state)


def incoming_state(own, rate, steps, local):
    core, x, yh = (lax.axis_index(name) for name in ("core", "x", "yh"))
    other = shift(own, "core", 1)
    first = jnp.where(core == 0, own, other)
    second = jnp.where(core == 0, other, own)
    hop = rate * jnp.float32(steps)
    pair = jnp.exp(-hop) * first + second
    half = own.shape[0] // 2
    mine = lax.dynamic_slice_in_dim(pair, core * half, half, 0)
    my_hop = lax.dynamic_slice_in_dim(hop, core * half, half, 0)
    pairs = lax.all_to_all(jnp.broadcast_to(mine[None], (8, *mine.shape)), ("yh", "x"), 0, 0)
    pairs, local = lax.optimization_barrier((pairs, local))
    place = yh * 4 + x
    before = jnp.zeros_like(mine)
    for j in range(8):
        weight = jnp.exp(-my_hop * (2 * jnp.maximum(place - 1 - j, 0)).astype(jnp.float32))
        before = before + jnp.where(j < place, weight, 0.0) * pairs[j]
    rest = shift(before, "core", 1)
    before = jnp.where(core == 0, jnp.concatenate([before, rest]), jnp.concatenate([rest, before]))
    return jnp.where(core == 0, before, jnp.exp(-hop) * before + first), local


def both_ways(value, step):
    return lax.ppermute(
        value,
        ("x", "core"),
        [(2 * i + c, 2 * ((i + (1 - 2 * c) * step) % 4) + c) for i in range(4) for c in range(2)],
    )


def first_weights(own):
    return both_ways(own, 1), both_ways(own, -1), shift(own, "yh", 1)


def second_weights(ahead, behind, far):
    cut = far.shape[0] * CUT // 64
    onward = both_ways(jnp.concatenate([ahead, far[:cut]]), 1)
    across = shift(jnp.concatenate([behind, ahead[cut:]]), "yh", 1)
    return shift(far, "x", 2), onward, across


def project_early_kernel(gated_ref, *refs):
    for block, ref in enumerate(refs[:-1]):
        term = jnp.dot(gated_ref[...], ref[...], preferred_element_type=jnp.float32)
        refs[-1][block] = term.astype(jnp.bfloat16)


def project_early(gated, weights):
    return pl.pallas_call(
        project_early_kernel,
        out_shape=jax.ShapeDtypeStruct((len(weights), gated.shape[0], weights[0].shape[1]), jnp.bfloat16),
        compiler_params=pltpu.CompilerParams(vmem_limit_bytes=32 * 1024 * 1024),
        cost_estimate=pl.CostEstimate(flops=0, bytes_accessed=0, transcendentals=0),
        name="project_early",
    )(gated, *weights)


def project_kernel(gated_ref, other_ref, place_ref, early_ref, *refs):
    first_refs, (onward_ref, across_ref, out_ref) = refs[:-3], refs[-3:]
    count = gated_ref.shape[1]
    cut = onward_ref.shape[0] - count
    core = place_ref[2, 0]

    def late(rows_ref):
        yield jnp.dot(rows_ref[...], onward_ref[:count, :], preferred_element_type=jnp.float32)
        yield jnp.dot(rows_ref[...], across_ref[:count, :], preferred_element_type=jnp.float32)
        yield jnp.dot(
            rows_ref[:, :cut], onward_ref[count:, :], preferred_element_type=jnp.float32
        ) + jnp.dot(rows_ref[:, cut:], across_ref[count:, :], preferred_element_type=jnp.float32)

    def put(half, block, term):
        out_ref[half, place_ref[1, block], place_ref[0, block]] = term.astype(jnp.bfloat16)

    for block, ref in enumerate(first_refs):
        put(core, block, early_ref[block])
        put(1 - core, block, jnp.dot(other_ref[...], ref[...], preferred_element_type=jnp.float32))
    for half, rows_ref in ((core, gated_ref), (1 - core, other_ref)):
        for block, term in enumerate(late(rows_ref)):
            put(half, len(first_refs) + block, term)


def project(gated, other, places, early, first, onward, across):
    return pl.pallas_call(
        project_kernel,
        out_shape=jax.ShapeDtypeStruct((2, 2, 4, *early.shape[1:]), jnp.bfloat16),
        in_specs=[pl.BlockSpec(memory_space=pltpu.VMEM)] * 2
        + [pl.BlockSpec(memory_space=pltpu.SMEM)]
        + [pl.BlockSpec(memory_space=pltpu.VMEM)] * (len(first) + 3),
        compiler_params=pltpu.CompilerParams(vmem_limit_bytes=32 * 1024 * 1024),
        cost_estimate=pl.CostEstimate(flops=1500000000, bytes_accessed=7000000, transcendentals=0),
        name="project",
    )(gated, other, places, early, *first, onward, across)


def add_up(*terms):
    total = terms[0].astype(jnp.float32)
    for term in terms[1:]:
        total = total + term.astype(jnp.float32)
    return total.astype(jnp.bfloat16)


def body(keys, values, queries, decay, residue, skip, out_weight):
    steps = keys.shape[0]
    seq_len = steps * 16
    core, x, yh, z, yl = (lax.axis_index(name) for name in ("core", "x", "yh", "z", "yl"))
    first = first_weights(out_weight)
    own, rate, gain = end_state(keys, values, decay, residue, seq_len)
    first, late_gain = lax.optimization_barrier((first, gain))
    local = local_part(keys, values, rate, late_gain, skip.reshape(ROWS, LANES))
    state, local = incoming_state(own, rate, steps, local)
    far_opposite, onward, across = second_weights(*first)
    state, far_opposite = lax.optimization_barrier((state, far_opposite))
    gated = gate(queries, local, rate, gain, state)
    other = shift(gated, "core", 1)
    ahead, behind = 2 * core - 1, 1 - 2 * core
    column = [yh * 4 + (x + j) % 4 for j in (0, ahead, behind)] + [(yh ^ 1) * 4 + x]
    column += [(yh ^ 1) * 4 + (x + 2) % 4, yh * 4 + (x + 2) % 4]
    column += [(yh ^ 1) * 4 + (x + j) % 4 for j in (behind, ahead)]
    places = [[(c // 2 - z) % 4 for c in column], [c % 2 ^ yl for c in column], [core] * 8]
    places = jnp.stack([jnp.stack(row) for row in places]).astype(jnp.int32)
    first = (out_weight, *first, far_opposite)
    near, away = project(gated, other, places, project_early(gated, first), first, onward, across)
    ring = add_up(away[:, 0], *[shift(away[:, j], "z", j) for j in (2, 1, 3)])
    pair = add_up(near[0], shift(near[1], "yl", 1))
    top = add_up(pair[0], *[shift(pair[j], "z", j) for j in (2, 1, 3)])
    end = add_up(ring[0], shift(ring[1], "yl", 1))
    mine = jnp.where(core == 0, top, end)
    got = shift(jnp.where(core == 0, end, top), "core", 1)
    return jnp.where(
        core == 0, jnp.concatenate([mine, got], 1), jnp.concatenate([got, mine], 1)
    )


def solution(mesh):
    fine = Mesh(
        mesh.devices.reshape(tuple(SIZES[name] for name in ALL)),
        ALL,
    )
    return jax.shard_map(
        body,
        mesh=fine,
        in_specs=(
            P(SEQ, CH),
            P(SEQ, CH),
            P(SEQ, CH),
            P(CH, None),
            P(CH, None),
            P(CH),
            P(CH, SEQ),
        ),
        out_specs=P(SEQ, CH),
        check_vma=False,
    )
```

time: 138 us -> 80.9 us (0.59)
  waiting for transfers between devices: 66.8 us -> 18.3 us
  blocking collectives: 30.2 us -> 0 us
  starting transfers between devices: 10.1 us -> 35.7 us
  between operations: 13.6 us -> 0.24 us
  Pallas kernels: 5.5 us -> 11.4 us
  matrix products: 5.75 us -> 0 us
  local copies, waits for them, and re-layouts: 3.28 us -> 8.93 us
  other arithmetic: 2.1 us -> 5.58 us
    all_gather x1 -> x0, waiting for transfers between devices: 59.3 us -> none  [body(): weight = lax.all_gather(out_weight, SEQ, axis=1, tiled=True)]
    all_to_all x1 -> x0, blocking collectives: 30.2 us -> none  [body(): blocks = lax.all_to_all(blocks, CH, 0, 0)]
    ppermute x4 -> x15, starting transfers between devices: 5.26 us -> 27.9 us  [shift(): lax.ppermute(value, axis, [(i, (i + step) % size) for i in range(size)])]
    ppermute x4 -> x15, waiting for transfers between devices: 4.72 us -> 18.3 us  [shift(): lax.ppermute(value, axis, [(i, (i + step) % size) for i in range(size)])]
    pallas_call x2 -> x5, Pallas kernels: 5.5 us -> 11.4 us  [the longest x1 3.69 us: local_part(): pl.pallas_call(local_kernel, out_shape=jax.ShapeDtypeStruct((ROWS * steps...]
    dot_general x1 -> x0, matrix products: 5.75 us -> none  [body(): jnp.dot(gated, weight, preferred_element_type=jnp.float32)]
    unnamed x23 -> x24, local copies, waits for them, and re-layouts: 3.09 us -> 7.73 us
    all_to_all x0 -> x1, starting transfers between devices: none -> 4.23 us  [incoming_state(): lax.all_to_all(jnp.broadcast_to(mine[None], (8, *mine.shape)), ('yh', 'x'...]
  transfers between devices with their start and end apart: 6 -> 19, of which waited for: 5 -> 9; matrix products, arithmetic and copies ran while one was open for 1% -> 7% of each run, Pallas kernels for 4% -> 10%
where the time goes in v2:
time: 80.9 us; the launch traced here: 80.2 us
  starting transfers between devices  35.7 us (44%)
  waiting for transfers between devices  18.3 us (23%)
  Pallas kernels  11.4 us (14%)
  local copies, waits for them, and re-layouts  8.93 us (11%)
  other arithmetic  5.58 us (7%)
    ppermute x15, starting transfers between devices, shift(): lax.ppermute(value, axis, [(i, (i + step) % size) for i in range(size)])  27.9 us
    ppermute x15, waiting for transfers between devices, shift(): lax.ppermute(value, axis, [(i, (i + step) % size) for i in range(size)])  18.3 us
    unnamed x24, local copies, waits for them, and re-layouts  7.73 us
    all_to_all x1, starting transfers between devices, incoming_state(): lax.all_to_all(jnp.broadcast_to(mine[None], (8, *mine.shape)), ('yh', 'x'...  4.23 us
    pallas_call x1, Pallas kernels, local_part(): pl.pallas_call(local_kernel, out_shape=jax.ShapeDtypeStruct((ROWS * steps...  3.69 us
    ppermute x3, starting transfers between devices, both_ways(): lax.ppermute(value, ('x', 'core'), [(2 * i + c, 2 * ((i + (1 - 2 * c) * s...  3.56 us
    pallas_call x1, Pallas kernels, project(): pl.pallas_call(project_kernel, out_shape=jax.ShapeDtypeStruct((2, 2, 4, *...  3.27 us
    pallas_call x1, Pallas kernels, end_state(): pl.pallas_call(functools.partial(end_state_kernel, seq_len), out_shape=(b...  1.82 us
  transfers between devices with their start and end apart: 19, of which 9 were waited for; matrix products, arithmetic and copies ran while one was open for 7% of the time, Pallas kernels for 10%

profile of v2, /device:TPU:1, one launch (start us, length us, event | category | flops | bytes accessed | tf_op | source)
XLA Modules:
  0.0 80.2 jit_solution(7602553609248486204)
XLA Ops:
  0.0 3.7 %collective-permute-start.3 = (bf16[1024,256]{1,0:T(8,128)(2,1)}, bf16[1024,256]{1,0:T(8,128)(2,1)S(1)}, u32[]{:S(2)}, u32[]{:S(2)}) collective-permute-start(bf16[1024,256]{1,0:T(8,128)(2,1)} %refs_0_.3), channel_id=1, source_target_pairs={{0,64},{64,0},{1,65},{65,1},{2,66},{66,2},{3,67},{67,3},{4,68},{68... | collective-permute-start | bytes 1572872 | tf_op jit(solution)/shard_map/ppermute | solution.py:21
  3.7 1.2 %collective-permute-start.2 = (bf16[1024,256]{1,0:T(8,128)(2,1)}, bf16[1024,256]{1,0:T(8,128)(2,1)S(1)}, u32[]{:S(2)}, u32[]{:S(2)}) collective-permute-start(bf16[1024,256]{1,0:T(8,128)(2,1)} %refs_0_.3), channel_id=1, source_target_pairs={{0,48},{8,24},{16,0},{24,40},{32,16},{40,56},{48,32},{56,8},{1,49}... | collective-permute-start | bytes 1572872 | tf_op jit(solution)/shard_map/ppermute | solution.py:169
  5.0 1.5 %collective-permute-start.1 = (bf16[1024,256]{1,0:T(8,128)(2,1)}, bf16[1024,256]{1,0:T(8,128)(2,1)S(1)}, u32[]{:S(2)}, u32[]{:S(2)}) collective-permute-start(bf16[1024,256]{1,0:T(8,128)(2,1)} %refs_0_.3), channel_id=1, source_target_pairs={{0,16},{8,56},{16,32},{24,8},{32,48},{40,24},{48,0},{56,40},{1,17}... | collective-permute-start | bytes 1572872 | tf_op jit(solution)/shard_map/ppermute | solution.py:169
  6.4 1.0 %copy-done = bf16[256,1024]{1,0:T(8,128)(2,1)S(1)} copy-done((bf16[256,1024]{1,0:T(8,128)(2,1)S(1)}, bf16[256,1024]{1,0:T(8,128)(2,1)}, u32[]{:S(2)}) %copy-start) | copy-done | bytes 524312
  7.5 1.0 %copy-done.2 = bf16[256,1024]{1,0:T(8,128)(2,1)S(1)} copy-done((bf16[256,1024]{1,0:T(8,128)(2,1)S(1)}, bf16[256,1024]{1,0:T(8,128)(2,1)}, u32[]{:S(2)}) %copy-start.2) | copy-done | bytes 524312
  8.5 0.8 %copy-done.8 = f32[1024,16]{0,1:T(8,128)S(1)} copy-done((f32[1024,16]{0,1:T(8,128)S(1)}, f32[1024,16]{0,1:T(8,128)}, u32[]{:S(2)}) %copy-start.8) | copy-done | bytes 65560
  9.3 0.8 %copy-done.9 = f32[1024,16]{0,1:T(8,128)S(1)} copy-done((f32[1024,16]{0,1:T(8,128)S(1)}, f32[1024,16]{0,1:T(8,128)}, u32[]{:S(2)}) %copy-start.9) | copy-done | bytes 65560
  10.2 1.8 %end_state.1 = (f32[16,8,128]{2,1,0:T(8,128)S(1)}, f32[16,8,128]{2,1,0:T(8,128)S(1)}, f32[16,8,128]{2,1,0:T(8,128)S(1)}) custom-call(bf16[256,1024]{1,0:T(8,128)(2,1)S(1)} %copy-done, bf16[256,1024]{1,0:T(8,128)(2,1)S(1)} %copy-done.2, f32[16,1024]{1,0:T(8,128)S(1)} %bitcast.115, f32[16,1024]{1,0:T(8,128)S(1)} %bitcast.116), custom_call_target="tpu_custom_call" | custom-call | flops 9000000 | bytes 1200000 | tf_op jit(solution)/shard_map/end_state/pallas_call | solution.py:110
  12.0 1.1 %collective-permute-start = (f32[16,8,128]{2,1,0:T(8,128)S(1)}, f32[16,8,128]{2,1,0:T(8,128)S(1)}, u32[]{:S(2)}, u32[]{:S(2)}) collective-permute-start(f32[16,8,128]{2,1,0:T(8,128)S(1)} %get-tuple-element.17), channel_id=1, source_target_pairs={{0,8},{8,0},{1,9},{9,1},{2,10},{10,2},{3,11},{11,3},{4,12},{12,4},... | collective-permute-start | bytes 196616 | tf_op jit(solution)/shard_map/ppermute | solution.py:21
  13.1 0.6 broadcast_multiply_fusion
  13.8 0.3 collective-permute-done
  14.1 0.7 broadcast_in_dim.17
  14.8 4.2 %all-to-all-start = ((f32[8,8,8,128]{3,2,1,0:T(8,128)}), f32[8,8,8,128]{3,2,1,0:T(8,128)S(1)}, u32[]{:S(2)}, u32[]{:S(2)}) async-start(f32[8,8,8,128]{3,2,1,0:T(8,128)} %broadcast_in_dim.17), calls=%async_computation | async-start | bytes 524288 | tf_op jit(solution)/shard_map/all_to_all | solution.py:156
  19.1 3.0 %collective-permute-start.5 = (bf16[1024,256]{1,0:T(8,128)(2,1)S(1)}, bf16[1024,256]{1,0:T(8,128)(2,1)S(1)}, u32[]{:S(2)}, u32[]{:S(2)}) collective-permute-start(bf16[1024,256]{1,0:T(8,128)(2,1)S(1)} %collective-permute-done.3.refs_3_), channel_id=1, source_target_pairs={{0,32},{16,48},{32,0},{48,16},{1,33},{17,49},{33,1},{49,17},{2,34}... | collective-permute-start | bytes 1572872 | tf_op jit(solution)/shard_map/ppermute | solution.py:21
  22.2 0.9 %pad_maximum_fusion = bf16[1536,256]{1,0:T(8,128)(2,1)} fusion(bf16[512,256]{1,0:T(8,128)(2,1)S(1)} %slice.78, bf16[1024,256]{1,0:T(8,128)(2,1)S(1)} %collective-permute-done.1.refs_1_), kind=kLoop, calls=%fused_computation.3 | loop fusion | flops 1572864 | bytes 1572864 | tf_op jit(solution)/shard_map/concatenate | solution.py:182
  23.1 0.9 %collective-permute-start.7 = (bf16[1536,256]{1,0:T(8,128)(2,1)}, bf16[1536,256]{1,0:T(8,128)(2,1)}, u32[]{:S(2)}, u32[]{:S(2)}) collective-permute-start(bf16[1536,256]{1,0:T(8,128)(2,1)} %pad_maximum_fusion), channel_id=1, source_target_pairs={{0,16},{8,56},{16,32},{24,8},{32,48},{40,24},{48,0},{56,40},{1,17}... | collective-permute-start | bytes 2359304 | tf_op jit(solution)/shard_map/ppermute | solution.py:169
  24.0 0.9 %pad_maximum_fusion.1 = bf16[1536,256]{1,0:T(8,128)(2,1)} fusion(bf16[512,256]{1,0:T(8,128)(2,1)S(1)} %slice.79, bf16[1024,256]{1,0:T(8,128)(2,1)S(1)} %collective-permute-done.2.refs_2_), kind=kLoop, calls=%fused_computation.4 | loop fusion | flops 1572864 | bytes 1572864 | tf_op jit(solution)/shard_map/concatenate | solution.py:183
  25.0 2.7 %collective-permute-start.8 = (bf16[1536,256]{1,0:T(8,128)(2,1)}, bf16[1536,256]{1,0:T(8,128)(2,1)}, u32[]{:S(2)}, u32[]{:S(2)}) collective-permute-start(bf16[1536,256]{1,0:T(8,128)(2,1)} %pad_maximum_fusion.1), channel_id=1, source_target_pairs={{0,64},{64,0},{1,65},{65,1},{2,66},{66,2},{3,67},{67,3},{4,68},{68... | collective-permute-start | bytes 2359304 | tf_op jit(solution)/shard_map/ppermute | solution.py:21
  27.7 3.7 %local_part.1.y_ref = f32[2048,128]{1,0:T(8,128)S(1)} custom-call(bf16[256,1024]{1,0:T(8,128)(2,1)S(1)} %copy-done.1, bf16[256,1024]{1,0:T(8,128)(2,1)S(1)} %copy-done.3, f32[16,8,128]{2,1,0:T(8,128)S(1)} %get-tuple-element.16.rate_ref, f32[16,8,128]{2,1,0:T(8,128)S(1)} %get-tuple-element.19.gain_ref, f32[8,128]{1,0:T(8,128)S(1)} %bitcast.117), custom_call_target="tpu_custom_call" | custom-call | tf_op jit(solution)/shard_map/local_part/pallas_call | solution.py:125
  31.4 0.8 %fusion.9 = f32[8,8,128]{2,1,0:T(8,128)S(1)} fusion(f32[8,8,8,128]{3,2,1,0:T(8,128)S(1)} %all-to-all-done, f32[16,8,128]{2,1,0:T(8,128)} %get-tuple-element.35, s32[]{:T(128)S(6)} %select_n.213, f32[]{:T(128)S(6)} %convert_element_type.91, f32[]{:T(128)S(6)} %convert_element_type.90, f32[]{:T(128)S(6)} %convert_element_type.89, f32[]{:T(128)S(6)} %convert_element_type.88, ...), kind=kLoop, calls=%fused_computation.37 | loop fusion | flops 262144 | bytes 327724 | tf_op jit(solution)/shard_map/add | solution.py:162
  32.2 1.2 %collective-permute-start.4 = (f32[8,8,128]{2,1,0:T(8,128)S(1)}, f32[8,8,128]{2,1,0:T(8,128)S(1)}, u32[]{:S(2)}, u32[]{:S(2)}) collective-permute-start(f32[8,8,128]{2,1,0:T(8,128)S(1)} %fusion.9), channel_id=1, source_target_pairs={{0,8},{8,0},{1,9},{9,1},{2,10},{10,2},{3,11},{11,3},{4,12},{12,4},... | collective-permute-start | bytes 98312 | tf_op jit(solution)/shard_map/ppermute | solution.py:21
  33.4 0.9 %collective-permute-done.4 = f32[8,8,128]{2,1,0:T(8,128)S(1)} collective-permute-done((f32[8,8,128]{2,1,0:T(8,128)S(1)}, f32[8,8,128]{2,1,0:T(8,128)S(1)}, u32[]{:S(2)}, u32[]{:S(2)}) %collective-permute-start.4) | collective-permute-done | bytes 32800 | tf_op jit(solution)/shard_map/ppermute | solution.py:21
  34.3 0.9 %add_select_fusion.state_ref = f32[16,8,128]{2,1,0:T(8,128)S(1)} fusion(f32[16,8,128]{2,1,0:T(8,128)} %copy-done.11, f32[8,8,128]{2,1,0:T(8,128)S(1)} %fusion.9, f32[8,8,128]{2,1,0:T(8,128)S(1)} %collective-permute-done.4, pred[]{:T(512)S(6)} %eq.33, f32[16,8,128]{2,1,0:T(8,128)S(1)} %get-tuple-element.16.rate_ref), kind=kLoop, calls=%fused_computation.31 | loop fusion | flops 131072 | bytes 262145 | tf_op jit(solution)/shard_map/jit(_where)/select_n | solution.py:165
  35.1 1.3 %collective-permute-done.5.refs_4_ = bf16[1024,256]{1,0:T(8,128)(2,1)S(1)} collective-permute-done((bf16[1024,256]{1,0:T(8,128)(2,1)S(1)}, bf16[1024,256]{1,0:T(8,128)(2,1)S(1)}, u32[]{:S(2)}, u32[]{:S(2)}) %collective-permute-start.5) | collective-permute-done | bytes 524320 | tf_op jit(solution)/shard_map/ppermute | solution.py:21
  36.5 0.8 %copy-done.5 = bf16[1024,256]{1,0:T(8,128)(2,1)} copy-done((bf16[1024,256]{1,0:T(8,128)(2,1)}, bf16[1024,256]{1,0:T(8,128)(2,1)S(1)}, u32[]{:S(2)}) %copy-start.5) | copy-done | bytes 524312
  37.3 1.0 %copy-done.7 = bf16[256,1024]{1,0:T(8,128)(2,1)S(1)} copy-done((bf16[256,1024]{1,0:T(8,128)(2,1)S(1)}, bf16[256,1024]{1,0:T(8,128)(2,1)}, u32[]{:S(2)}) %copy-start.7) | copy-done | bytes 524312
  38.4 1.8 %gated.1.gated_ref = bf16[256,1024]{1,0:T(8,128)(2,1)S(1)} custom-call(bf16[256,1024]{1,0:T(8,128)(2,1)S(1)} %copy-done.7, f32[2048,128]{1,0:T(8,128)S(1)} %local_part.1.y_ref, f32[16,8,128]{2,1,0:T(8,128)S(1)} %get-tuple-element.16.rate_ref, f32[16,8,128]{2,1,0:T(8,128)S(1)} %get-tuple-element.19.gain_ref, f32[16,8,128]{2,1,0:T(8,128)S(1)} %add_select_fusion.state_ref), custom_call_target="tpu_custom_call" | custom-call | tf_op jit(solution)/shard_map/gated/pallas_call | solution.py:136
  40.2 1.5 %collective-permute-start.6 = (bf16[256,1024]{1,0:T(8,128)(2,1)S(1)}, bf16[256,1024]{1,0:T(8,128)(2,1)}, u32[]{:S(2)}, u32[]{:S(2)}) collective-permute-start(bf16[256,1024]{1,0:T(8,128)(2,1)S(1)} %gated.1.gated_ref), channel_id=1, source_target_pairs={{0,8},{8,0},{1,9},{9,1},{2,10},{10,2},{3,11},{11,3},{4,12},{12,4},... | collective-permute-start | bytes 1572872 | tf_op jit(solution)/shard_map/ppermute | solution.py:21
  42.0 1.0 %copy-done.4 = bf16[1024,256]{1,0:T(8,128)(2,1)S(1)} copy-done((bf16[1024,256]{1,0:T(8,128)(2,1)S(1)}, bf16[1024,256]{1,0:T(8,128)(2,1)}, u32[]{:S(2)}) %copy-start.4) | copy-done | bytes 524312
  43.1 1.0 %copy-done.6 = bf16[1024,256]{1,0:T(8,128)(2,1)S(1)} copy-done((bf16[1024,256]{1,0:T(8,128)(2,1)S(1)}, bf16[1024,256]{1,0:T(8,128)(2,1)}, u32[]{:S(2)}) %copy-start.6) | copy-done | bytes 524312
  44.1 0.8 %project_early.1.early_ref = bf16[5,256,256]{2,1,0:T(8,128)(2,1)S(1)} custom-call(bf16[256,1024]{1,0:T(8,128)(2,1)S(1)} %gated.1.gated_ref, bf16[1024,256]{1,0:T(8,128)(2,1)S(1)} %copy-done.4, bf16[1024,256]{1,0:T(8,128)(2,1)S(1)} %collective-permute-done.1.refs_1_, bf16[1024,256]{1,0:T(8,128)(2,1)S(1)} %collective-permute-done.2.refs_2_, ...), custom_call_target="tpu_custom_call" | custom-call | tf_op jit(solution)/shard_map/project_early/pallas_call | solution.py:194
  45.0 3.3 %project.1 = bf16[2,2,4,256,256]{4,3,2,1,0:T(8,128)(2,1)S(1)} custom-call(bf16[256,1024]{1,0:T(8,128)(2,1)S(1)} %gated.1.gated_ref, bf16[256,1024]{1,0:T(8,128)(2,1)} %collective-permute-done.6.other_ref, s32[3,8]{1,0:T(4,128)S(1)} %add_add_fusion.place_ref, bf16[5,256,256]{2,1,0:T(8,128)(2,1)S(1)} %project_early.1.early_ref, ...), custom_call_target="tpu_custom_call" | custom-call | flops 1500000000 | bytes 7000000 | tf_op jit(solution)/shard_map/project/pallas_call | solution.py:228
  48.4 3.7 %collective-permute-start.13 = (bf16[2,256,256]{2,1,0:T(8,128)(2,1)S(1)}, bf16[2,256,256]{2,1,0:T(8,128)(2,1)S(1)}, u32[]{:S(2)}, u32[]{:S(2)}) collective-permute-start(bf16[2,256,256]{2,1,0:T(8,128)(2,1)S(1)} %get-tuple-element.29), channel_id=1, source_target_pairs={{0,4},{2,6},{4,0},{6,2},{1,5},{3,7},{5,1},{7,3},{8,12},{10,14},{12... | collective-permute-start | bytes 786440 | tf_op jit(solution)/shard_map/ppermute | solution.py:21
  52.1 0.4 collective-permute-start.15
  52.5 1.0 %collective-permute-start.14 = (bf16[2,256,256]{2,1,0:T(8,128)(2,1)S(1)}, bf16[2,256,256]{2,1,0:T(8,128)(2,1)S(1)}, u32[]{:S(2)}, u32[]{:S(2)}) collective-permute-start(bf16[2,256,256]{2,1,0:T(8,128)(2,1)S(1)} %get-tuple-element.31), channel_id=1, source_target_pairs={{0,2},{2,4},{4,6},{6,0},{1,3},{3,5},{5,7},{7,1},{8,10},{10,12},{12... | collective-permute-start | bytes 786440 | tf_op jit(solution)/shard_map/ppermute | solution.py:21
  53.6 1.2 %collective-permute-start.9 = (bf16[4,256,256]{2,1,0:T(8,128)(2,1)S(1)}, bf16[4,256,256]{2,1,0:T(8,128)(2,1)S(1)}, u32[]{:S(2)}, u32[]{:S(2)}) collective-permute-start(bf16[4,256,256]{2,1,0:T(8,128)(2,1)S(1)} %slice_bitcast_fusion.1), channel_id=1, source_target_pairs={{0,1},{1,0},{2,3},{3,2},{4,5},{5,4},{6,7},{7,6},{8,9},{9,8},{10,11... | collective-permute-start | bytes 1572872 | tf_op jit(solution)/shard_map/ppermute | solution.py:21
  54.7 2.2 %collective-permute-done.13 = bf16[2,256,256]{2,1,0:T(8,128)(2,1)S(1)} collective-permute-done((bf16[2,256,256]{2,1,0:T(8,128)(2,1)S(1)}, bf16[2,256,256]{2,1,0:T(8,128)(2,1)S(1)}, u32[]{:S(2)}, u32[]{:S(2)}) %collective-permute-start.13) | collective-permute-done | bytes 262176 | tf_op jit(solution)/shard_map/ppermute | solution.py:21
  57.0 7.2 %collective-permute-done.15 = bf16[2,256,256]{2,1,0:T(8,128)(2,1)S(1)} collective-permute-done((bf16[2,256,256]{2,1,0:T(8,128)(2,1)S(1)}, bf16[2,256,256]{2,1,0:T(8,128)(2,1)S(1)}, u32[]{:S(2)}, u32[]{:S(2)}) %collective-permute-start.15) | collective-permute-done | bytes 262176 | tf_op jit(solution)/shard_map/ppermute | solution.py:21
  64.3 1.2 %collective-permute-start.16 = (bf16[256,256]{1,0:T(8,128)(2,1)S(1)}, bf16[256,256]{1,0:T(8,128)(2,1)S(1)}, u32[]{:S(2)}, u32[]{:S(2)}) collective-permute-start(bf16[256,256]{1,0:T(8,128)(2,1)S(1)} %slice_bitcast_fusion.7), channel_id=1, source_target_pairs={{0,1},{1,0},{2,3},{3,2},{4,5},{5,4},{6,7},{7,6},{8,9},{9,8},{10,11... | collective-permute-start | bytes 393224 | tf_op jit(solution)/shard_map/ppermute | solution.py:21
  65.6 3.2 %collective-permute-start.10 = (bf16[256,256]{1,0:T(8,128)(2,1)S(1)}, bf16[256,256]{1,0:T(8,128)(2,1)S(1)}, u32[]{:S(2)}, u32[]{:S(2)}) collective-permute-start(bf16[256,256]{1,0:T(8,128)(2,1)S(1)} %get-tuple-element.32), channel_id=1, source_target_pairs={{0,4},{2,6},{4,0},{6,2},{1,5},{3,7},{5,1},{7,3},{8,12},{10,14},{12... | collective-permute-start | bytes 393224 | tf_op jit(solution)/shard_map/ppermute | solution.py:21
  68.9 0.5 collective-permute-start.12
  69.4 1.0 %collective-permute-start.11 = (bf16[256,256]{1,0:T(8,128)(2,1)S(1)}, bf16[256,256]{1,0:T(8,128)(2,1)S(1)}, u32[]{:S(2)}, u32[]{:S(2)}) collective-permute-start(bf16[256,256]{1,0:T(8,128)(2,1)S(1)} %get-tuple-element.34), channel_id=1, source_target_pairs={{0,2},{2,4},{4,6},{6,0},{1,3},{3,5},{5,7},{7,1},{8,10},{10,12},{12... | collective-permute-start | bytes 393224 | tf_op jit(solution)/shard_map/ppermute | solution.py:21
  70.4 0.9 %collective-permute-done.10 = bf16[256,256]{1,0:T(8,128)(2,1)S(1)} collective-permute-done((bf16[256,256]{1,0:T(8,128)(2,1)S(1)}, bf16[256,256]{1,0:T(8,128)(2,1)S(1)}, u32[]{:S(2)}, u32[]{:S(2)}) %collective-permute-start.10) | collective-permute-done | bytes 131104 | tf_op jit(solution)/shard_map/ppermute | solution.py:21
  71.3 4.1 %collective-permute-done.12 = bf16[256,256]{1,0:T(8,128)(2,1)S(1)} collective-permute-done((bf16[256,256]{1,0:T(8,128)(2,1)S(1)}, bf16[256,256]{1,0:T(8,128)(2,1)S(1)}, u32[]{:S(2)}, u32[]{:S(2)}) %collective-permute-start.12) | collective-permute-done | bytes 131104 | tf_op jit(solution)/shard_map/ppermute | solution.py:21
  75.4 0.4 collective-permute-done.11
  76.0 2.4 %collective-permute-start.17 = (bf16[256,256]{1,0:T(8,128)(2,1)S(1)}, bf16[256,256]{1,0:T(8,128)(2,1)S(1)}, u32[]{:S(2)}, u32[]{:S(2)}) collective-permute-start(bf16[256,256]{1,0:T(8,128)(2,1)S(1)} %broadcast_select_fusion), channel_id=1, source_target_pairs={{0,8},{8,0},{1,9},{9,1},{2,10},{10,2},{3,11},{11,3},{4,12},{12,4},... | collective-permute-start | bytes 393224 | tf_op jit(solution)/shard_map/ppermute | solution.py:21
  78.4 1.0 %collective-permute-done.17 = bf16[256,256]{1,0:T(8,128)(2,1)S(1)} collective-permute-done((bf16[256,256]{1,0:T(8,128)(2,1)S(1)}, bf16[256,256]{1,0:T(8,128)(2,1)S(1)}, u32[]{:S(2)}, u32[]{:S(2)}) %collective-permute-start.17) | collective-permute-done | bytes 131104 | tf_op jit(solution)/shard_map/ppermute | solution.py:21
  79.4 0.8 %maximum_select_fusion = bf16[256,512]{1,0:T(8,128)(2,1)} fusion(bf16[256,256]{1,0:T(8,128)(2,1)S(1)} %collective-permute-done.17, bf16[256,256]{1,0:T(8,128)(2,1)S(1)} %get-tuple-element.27, pred[]{:T(512)S(6)} %eq.33), kind=kLoop, calls=%fused_computation.15 | loop fusion | flops 1179648 | bytes 524289 | tf_op jit(solution)/shard_map/jit(_where)/select_n | solution.py:274
  (43 shorter events, 1.1 us)
Async XLA Ops:
  0.0 19.0 %collective-permute-start.3 = (bf16[1024,256]{1,0:T(8,128)(2,1)}, bf16[1024,256]{1,0:T(8,128)(2,1)S(1)}, u32[]{:S(2)}, u32[]{:S(2)}) collective-permute-start(bf16[1024,256]{1,0:T(8,128)(2,1)} %refs_0_.3), channel_id=1, source_target_pairs={{0,64},{64,0},{1,65},{65,1},{2,66},{66,2},{3,67},{67,3},{4,68},{68... | collective-permute-start | bytes 1572872 | tf_op jit(solution)/shard_map/ppermute | solution.py:21
  3.7 15.3 %collective-permute-start.2 = (bf16[1024,256]{1,0:T(8,128)(2,1)}, bf16[1024,256]{1,0:T(8,128)(2,1)S(1)}, u32[]{:S(2)}, u32[]{:S(2)}) collective-permute-start(bf16[1024,256]{1,0:T(8,128)(2,1)} %refs_0_.3), channel_id=1, source_target_pairs={{0,48},{8,24},{16,0},{24,40},{32,16},{40,56},{48,32},{56,8},{1,49}... | collective-permute-start | bytes 1572872 | tf_op jit(solution)/shard_map/ppermute | solution.py:169
  5.0 14.1 %collective-permute-start.1 = (bf16[1024,256]{1,0:T(8,128)(2,1)}, bf16[1024,256]{1,0:T(8,128)(2,1)S(1)}, u32[]{:S(2)}, u32[]{:S(2)}) collective-permute-start(bf16[1024,256]{1,0:T(8,128)(2,1)} %refs_0_.3), channel_id=1, source_target_pairs={{0,16},{8,56},{16,32},{24,8},{32,48},{40,24},{48,0},{56,40},{1,17}... | collective-permute-start | bytes 1572872 | tf_op jit(solution)/shard_map/ppermute | solution.py:169
  6.4 1.0 %copy-start = (bf16[256,1024]{1,0:T(8,128)(2,1)S(1)}, bf16[256,1024]{1,0:T(8,128)(2,1)}, u32[]{:S(2)}) copy-start(bf16[256,1024]{1,0:T(8,128)(2,1)} %keys_ref.3) | copy-start | bytes 1572868
  7.5 1.0 %copy-start.2 = (bf16[256,1024]{1,0:T(8,128)(2,1)S(1)}, bf16[256,1024]{1,0:T(8,128)(2,1)}, u32[]{:S(2)}) copy-start(bf16[256,1024]{1,0:T(8,128)(2,1)} %values_ref.3) | copy-start | bytes 1572868
  8.5 0.8 %copy-start.8 = (f32[1024,16]{0,1:T(8,128)S(1)}, f32[1024,16]{0,1:T(8,128)}, u32[]{:S(2)}) copy-start(f32[1024,16]{0,1:T(8,128)} %param.10) | copy-start | bytes 196612
  9.3 0.8 %copy-start.9 = (f32[1024,16]{0,1:T(8,128)S(1)}, f32[1024,16]{0,1:T(8,128)}, u32[]{:S(2)}) copy-start(f32[1024,16]{0,1:T(8,128)} %param.11) | copy-start | bytes 196612
  12.0 2.0 %collective-permute-start = (f32[16,8,128]{2,1,0:T(8,128)S(1)}, f32[16,8,128]{2,1,0:T(8,128)S(1)}, u32[]{:S(2)}, u32[]{:S(2)}) collective-permute-start(f32[16,8,128]{2,1,0:T(8,128)S(1)} %get-tuple-element.17), channel_id=1, source_target_pairs={{0,8},{8,0},{1,9},{9,1},{2,10},{10,2},{3,11},{11,3},{4,12},{12,4},... | collective-permute-start | bytes 196616 | tf_op jit(solution)/shard_map/ppermute | solution.py:21
  14.0 5.0 %copy-start.11 = (f32[16,8,128]{2,1,0:T(8,128)}, f32[16,8,128]{2,1,0:T(8,128)S(1)}, u32[]{:S(2)}) copy-start(f32[16,8,128]{2,1,0:T(8,128)S(1)} %broadcast_select_fusion.2) | copy-start | bytes 196612
  14.8 16.6 %all-to-all-start = ((f32[8,8,8,128]{3,2,1,0:T(8,128)}), f32[8,8,8,128]{3,2,1,0:T(8,128)S(1)}, u32[]{:S(2)}, u32[]{:S(2)}) async-start(f32[8,8,8,128]{3,2,1,0:T(8,128)} %broadcast_in_dim.17), calls=%async_computation | async-start | bytes 524288 | tf_op jit(solution)/shard_map/all_to_all | solution.py:156
  19.1 17.4 %collective-permute-start.5 = (bf16[1024,256]{1,0:T(8,128)(2,1)S(1)}, bf16[1024,256]{1,0:T(8,128)(2,1)S(1)}, u32[]{:S(2)}, u32[]{:S(2)}) collective-permute-start(bf16[1024,256]{1,0:T(8,128)(2,1)S(1)} %collective-permute-done.3.refs_3_), channel_id=1, source_target_pairs={{0,32},{16,48},{32,0},{48,16},{1,33},{17,49},{33,1},{49,17},{2,34}... | collective-permute-start | bytes 1572872 | tf_op jit(solution)/shard_map/ppermute | solution.py:21
  22.2 5.5 %copy-start.1 = (bf16[256,1024]{1,0:T(8,128)(2,1)S(1)}, bf16[256,1024]{1,0:T(8,128)(2,1)}, u32[]{:S(2)}) copy-start(bf16[256,1024]{1,0:T(8,128)(2,1)} %keys_ref.3) | copy-start | bytes 1572868
  22.2 5.5 %copy-start.3 = (bf16[256,1024]{1,0:T(8,128)(2,1)S(1)}, bf16[256,1024]{1,0:T(8,128)(2,1)}, u32[]{:S(2)}) copy-start(bf16[256,1024]{1,0:T(8,128)(2,1)} %values_ref.3) | copy-start | bytes 1572868
  22.2 5.5 %copy-start.10 = (f32[1024]{0:T(1024)S(1)}, f32[1024]{0:T(1024)}, u32[]{:S(2)}) copy-start(f32[1024]{0:T(1024)} %param.12) | copy-start | bytes 12292
  23.1 21.8 %collective-permute-start.7 = (bf16[1536,256]{1,0:T(8,128)(2,1)}, bf16[1536,256]{1,0:T(8,128)(2,1)}, u32[]{:S(2)}, u32[]{:S(2)}) collective-permute-start(bf16[1536,256]{1,0:T(8,128)(2,1)} %pad_maximum_fusion), channel_id=1, source_target_pairs={{0,16},{8,56},{16,32},{24,8},{32,48},{40,24},{48,0},{56,40},{1,17}... | collective-permute-start | bytes 2359304 | tf_op jit(solution)/shard_map/ppermute | solution.py:169
  25.0 20.0 %collective-permute-start.8 = (bf16[1536,256]{1,0:T(8,128)(2,1)}, bf16[1536,256]{1,0:T(8,128)(2,1)}, u32[]{:S(2)}, u32[]{:S(2)}) collective-permute-start(bf16[1536,256]{1,0:T(8,128)(2,1)} %pad_maximum_fusion.1), channel_id=1, source_target_pairs={{0,64},{64,0},{1,65},{65,1},{2,66},{66,2},{3,67},{67,3},{4,68},{68... | collective-permute-start | bytes 2359304 | tf_op jit(solution)/shard_map/ppermute | solution.py:21
  32.2 2.1 %collective-permute-start.4 = (f32[8,8,128]{2,1,0:T(8,128)S(1)}, f32[8,8,128]{2,1,0:T(8,128)S(1)}, u32[]{:S(2)}, u32[]{:S(2)}) collective-permute-start(f32[8,8,128]{2,1,0:T(8,128)S(1)} %fusion.9), channel_id=1, source_target_pairs={{0,8},{8,0},{1,9},{9,1},{2,10},{10,2},{3,11},{11,3},{4,12},{12,4},... | collective-permute-start | bytes 98312 | tf_op jit(solution)/shard_map/ppermute | solution.py:21
  36.5 0.8 %copy-start.5 = (bf16[1024,256]{1,0:T(8,128)(2,1)}, bf16[1024,256]{1,0:T(8,128)(2,1)S(1)}, u32[]{:S(2)}) copy-start(bf16[1024,256]{1,0:T(8,128)(2,1)S(1)} %collective-permute-done.5.refs_4_) | copy-start | bytes 1572868
  37.3 1.0 %copy-start.7 = (bf16[256,1024]{1,0:T(8,128)(2,1)S(1)}, bf16[256,1024]{1,0:T(8,128)(2,1)}, u32[]{:S(2)}) copy-start(bf16[256,1024]{1,0:T(8,128)(2,1)} %queries_ref.1) | copy-start | bytes 1572868
  40.2 4.8 %collective-permute-start.6 = (bf16[256,1024]{1,0:T(8,128)(2,1)S(1)}, bf16[256,1024]{1,0:T(8,128)(2,1)}, u32[]{:S(2)}, u32[]{:S(2)}) collective-permute-start(bf16[256,1024]{1,0:T(8,128)(2,1)S(1)} %gated.1.gated_ref), channel_id=1, source_target_pairs={{0,8},{8,0},{1,9},{9,1},{2,10},{10,2},{3,11},{11,3},{4,12},{12,4},... | collective-permute-start | bytes 1572872 | tf_op jit(solution)/shard_map/ppermute | solution.py:21
  42.0 1.0 %copy-start.4 = (bf16[1024,256]{1,0:T(8,128)(2,1)S(1)}, bf16[1024,256]{1,0:T(8,128)(2,1)}, u32[]{:S(2)}) copy-start(bf16[1024,256]{1,0:T(8,128)(2,1)} %refs_0_.3) | copy-start | bytes 1572868
  43.1 1.0 %copy-start.6 = (bf16[1024,256]{1,0:T(8,128)(2,1)S(1)}, bf16[1024,256]{1,0:T(8,128)(2,1)}, u32[]{:S(2)}) copy-start(bf16[1024,256]{1,0:T(8,128)(2,1)} %copy-done.5) | copy-start | bytes 1572868
  48.4 8.6 %collective-permute-start.13 = (bf16[2,256,256]{2,1,0:T(8,128)(2,1)S(1)}, bf16[2,256,256]{2,1,0:T(8,128)(2,1)S(1)}, u32[]{:S(2)}, u32[]{:S(2)}) collective-permute-start(bf16[2,256,256]{2,1,0:T(8,128)(2,1)S(1)} %get-tuple-element.29), channel_id=1, source_target_pairs={{0,4},{2,6},{4,0},{6,2},{1,5},{3,7},{5,1},{7,3},{8,12},{10,14},{12... | collective-permute-start | bytes 786440 | tf_op jit(solution)/shard_map/ppermute | solution.py:21
  52.1 12.0 %collective-permute-start.15 = (bf16[2,256,256]{2,1,0:T(8,128)(2,1)S(1)}, bf16[2,256,256]{2,1,0:T(8,128)(2,1)S(1)}, u32[]{:S(2)}, u32[]{:S(2)}) collective-permute-start(bf16[2,256,256]{2,1,0:T(8,128)(2,1)S(1)} %get-tuple-element.30), channel_id=1, source_target_pairs={{0,6},{2,0},{4,2},{6,4},{1,7},{3,1},{5,3},{7,5},{8,14},{10,8},{12,... | collective-permute-start | bytes 786440 | tf_op jit(solution)/shard_map/ppermute | solution.py:21
  52.5 11.6 %collective-permute-start.14 = (bf16[2,256,256]{2,1,0:T(8,128)(2,1)S(1)}, bf16[2,256,256]{2,1,0:T(8,128)(2,1)S(1)}, u32[]{:S(2)}, u32[]{:S(2)}) collective-permute-start(bf16[2,256,256]{2,1,0:T(8,128)(2,1)S(1)} %get-tuple-element.31), channel_id=1, source_target_pairs={{0,2},{2,4},{4,6},{6,0},{1,3},{3,5},{5,7},{7,1},{8,10},{10,12},{12... | collective-permute-start | bytes 786440 | tf_op jit(solution)/shard_map/ppermute | solution.py:21
  53.6 11.9 %collective-permute-start.9 = (bf16[4,256,256]{2,1,0:T(8,128)(2,1)S(1)}, bf16[4,256,256]{2,1,0:T(8,128)(2,1)S(1)}, u32[]{:S(2)}, u32[]{:S(2)}) collective-permute-start(bf16[4,256,256]{2,1,0:T(8,128)(2,1)S(1)} %slice_bitcast_fusion.1), channel_id=1, source_target_pairs={{0,1},{1,0},{2,3},{3,2},{4,5},{5,4},{6,7},{7,6},{8,9},{9,8},{10,11... | collective-permute-start | bytes 1572872 | tf_op jit(solution)/shard_map/ppermute | solution.py:21
  64.3 6.1 %collective-permute-start.16 = (bf16[256,256]{1,0:T(8,128)(2,1)S(1)}, bf16[256,256]{1,0:T(8,128)(2,1)S(1)}, u32[]{:S(2)}, u32[]{:S(2)}) collective-permute-start(bf16[256,256]{1,0:T(8,128)(2,1)S(1)} %slice_bitcast_fusion.7), channel_id=1, source_target_pairs={{0,1},{1,0},{2,3},{3,2},{4,5},{5,4},{6,7},{7,6},{8,9},{9,8},{10,11... | collective-permute-start | bytes 393224 | tf_op jit(solution)/shard_map/ppermute | solution.py:21
  65.6 5.6 %collective-permute-start.10 = (bf16[256,256]{1,0:T(8,128)(2,1)S(1)}, bf16[256,256]{1,0:T(8,128)(2,1)S(1)}, u32[]{:S(2)}, u32[]{:S(2)}) collective-permute-start(bf16[256,256]{1,0:T(8,128)(2,1)S(1)} %get-tuple-element.32), channel_id=1, source_target_pairs={{0,4},{2,6},{4,0},{6,2},{1,5},{3,7},{5,1},{7,3},{8,12},{10,14},{12... | collective-permute-start | bytes 393224 | tf_op jit(solution)/shard_map/ppermute | solution.py:21
  68.9 6.5 %collective-permute-start.12 = (bf16[256,256]{1,0:T(8,128)(2,1)S(1)}, bf16[256,256]{1,0:T(8,128)(2,1)S(1)}, u32[]{:S(2)}, u32[]{:S(2)}) collective-permute-start(bf16[256,256]{1,0:T(8,128)(2,1)S(1)} %get-tuple-element.33), channel_id=1, source_target_pairs={{0,6},{2,0},{4,2},{6,4},{1,7},{3,1},{5,3},{7,5},{8,14},{10,8},{12,... | collective-permute-start | bytes 393224 | tf_op jit(solution)/shard_map/ppermute | solution.py:21
  69.4 6.4 %collective-permute-start.11 = (bf16[256,256]{1,0:T(8,128)(2,1)S(1)}, bf16[256,256]{1,0:T(8,128)(2,1)S(1)}, u32[]{:S(2)}, u32[]{:S(2)}) collective-permute-start(bf16[256,256]{1,0:T(8,128)(2,1)S(1)} %get-tuple-element.34), channel_id=1, source_target_pairs={{0,2},{2,4},{4,6},{6,0},{1,3},{3,5},{5,7},{7,1},{8,10},{10,12},{12... | collective-permute-start | bytes 393224 | tf_op jit(solution)/shard_map/ppermute | solution.py:21
  76.0 3.4 %collective-permute-start.17 = (bf16[256,256]{1,0:T(8,128)(2,1)S(1)}, bf16[256,256]{1,0:T(8,128)(2,1)S(1)}, u32[]{:S(2)}, u32[]{:S(2)}) collective-permute-start(bf16[256,256]{1,0:T(8,128)(2,1)S(1)} %broadcast_select_fusion), channel_id=1, source_target_pairs={{0,8},{8,0},{1,9},{9,1},{2,10},{10,2},{3,11},{11,3},{4,12},{12,4},... | collective-permute-start | bytes 393224 | tf_op jit(solution)/shard_map/ppermute | solution.py:21

commit v3 on v2

--- a/solution.py
+++ b/solution.py
@@ -12,7 +12,7 @@
 ALL = SEQ + CH
 SIZES = {"yh": 2, "x": 4, "core": 2, "z": 4, "yl": 2}
 LANES = 128
-CUT = 32
+CUT = 24
 ROWS = 8
 
 
@@ -37,7 +37,7 @@
 
 
 def end_state_kernel(
-    seq_len, keys_ref, values_ref, decay_ref, residue_ref, state_ref, rate_ref, gain_ref, z_ref, spread_ref
+    seq_len, keys_ref, values_ref, decay_ref, state_ref, rate_ref, z_ref, spread_ref
 ):
     steps = keys_ref.shape[0]
     modes = decay_ref.shape[0]
@@ -55,17 +55,17 @@
     states = lax.fori_loop(0, steps, step, start, unroll=8)
     for n in range(modes):
         state_ref[n] = states[n]
-    residue = spread_modes(residue_ref, spread_ref)
-    for n in range(modes):
-        gain_ref[n] = residue[n] * jnp.sqrt(rate_ref[n])
-
-
-def local_kernel(keys_ref, values_ref, rate_ref, gain_ref, skip_ref, y_ref, z_ref):
+
+
+def local_kernel(keys_ref, values_ref, rate_ref, residue_ref, skip_ref, y_ref, gain_ref, z_ref, spread_ref):
     steps = keys_ref.shape[0]
     modes = rate_ref.shape[0]
     spread_rows(keys_ref, values_ref, z_ref)
     keep = [jnp.exp(-rate_ref[n]) for n in range(modes)]
-    gain = [gain_ref[n] for n in range(modes)]
+    residue = spread_modes(residue_ref, spread_ref)
+    gain = [residue[n] * jnp.sqrt(rate_ref[n]) for n in range(modes)]
+    for n in range(modes):
+        gain_ref[n] = gain[n]
     skip = skip_ref[...]
 
     def step(t, states):
@@ -103,13 +103,13 @@
     return terms[0]
 
 
-def end_state(keys, values, decay, residue, seq_len):
+def end_state(keys, values, decay, seq_len):
     steps = keys.shape[0]
     modes = decay.shape[1]
     by_mode = jax.ShapeDtypeStruct((modes, ROWS, LANES), jnp.float32)
     return pl.pallas_call(
         functools.partial(end_state_kernel, seq_len),
-        out_shape=(by_mode,) * 3,
+        out_shape=(by_mode,) * 2,
         scratch_shapes=[
             pltpu.VMEM((ROWS * steps, LANES), jnp.float32),
             pltpu.VMEM((ROWS * modes, LANES), jnp.float32),
@@ -117,19 +117,25 @@
         compiler_params=pltpu.CompilerParams(vmem_limit_bytes=32 * 1024 * 1024),
         cost_estimate=pl.CostEstimate(flops=9000000, bytes_accessed=1200000, transcendentals=0),
         name="end_state",
-    )(keys, values, decay.T, residue.T)
-
-
-def local_part(keys, values, rate, gain, skip):
+    )(keys, values, decay.T)
+
+
+def local_part(keys, values, rate, residue, skip):
     steps = keys.shape[0]
     return pl.pallas_call(
         local_kernel,
-        out_shape=jax.ShapeDtypeStruct((ROWS * steps, LANES), jnp.float32),
-        scratch_shapes=[pltpu.VMEM((ROWS * steps, LANES), jnp.float32)],
+        out_shape=(
+            jax.ShapeDtypeStruct((ROWS * steps, LANES), jnp.float32),
+            jax.ShapeDtypeStruct(rate.shape, jnp.float32),
+        ),
+        scratch_shapes=[
+            pltpu.VMEM((ROWS * steps, LANES), jnp.float32),
+            pltpu.VMEM((ROWS * rate.shape[0], LANES), jnp.float32),
+        ],
         compiler_params=pltpu.CompilerParams(vmem_limit_bytes=32 * 1024 * 1024),
         cost_estimate=pl.CostEstimate(flops=0, bytes_accessed=0, transcendentals=0),
         name="local_part",
-    )(keys, values, rate, gain, skip)
+    )(keys, values, rate, residue.T, skip)
 
 
 def gate(queries, local, rate, gain, state):
@@ -200,41 +206,43 @@
     )(gated, *weights)
 
 
-def project_kernel(gated_ref, other_ref, place_ref, early_ref, *refs):
+def late_blocks(rows_ref, onward_ref, across_ref):
+    count = rows_ref.shape[1]
+    cut = onward_ref.shape[0] - count
+    yield jnp.dot(rows_ref[...], onward_ref[:count, :], preferred_element_type=jnp.float32)
+    yield jnp.dot(rows_ref[...], across_ref[:count, :], preferred_element_type=jnp.float32)
+    yield jnp.dot(rows_ref[:, :cut], onward_ref[count:, :], preferred_element_type=jnp.float32) + jnp.dot(
+        rows_ref[:, cut:], across_ref[count:, :], preferred_element_type=jnp.float32
+    )
+
+
+def project_own_kernel(gated_ref, place_ref, early_ref, onward_ref, across_ref, out_ref):
+    early = early_ref.shape[0]
+    for block in range(early):
+        out_ref[place_ref[0, block], place_ref[1, block]] = early_ref[block]
+    for block, term in enumerate(late_blocks(gated_ref, onward_ref, across_ref), early):
+        out_ref[place_ref[0, block], place_ref[1, block]] = term.astype(jnp.bfloat16)
+
+
+def project_other_kernel(other_ref, place_ref, *refs):
     first_refs, (onward_ref, across_ref, out_ref) = refs[:-3], refs[-3:]
-    count = gated_ref.shape[1]
-    cut = onward_ref.shape[0] - count
-    core = place_ref[2, 0]
-
-    def late(rows_ref):
-        yield jnp.dot(rows_ref[...], onward_ref[:count, :], preferred_element_type=jnp.float32)
-        yield jnp.dot(rows_ref[...], across_ref[:count, :], preferred_element_type=jnp.float32)
-        yield jnp.dot(
-            rows_ref[:, :cut], onward_ref[count:, :], preferred_element_type=jnp.float32
-        ) + jnp.dot(rows_ref[:, cut:], across_ref[count:, :], preferred_element_type=jnp.float32)
-
-    def put(half, block, term):
-        out_ref[half, place_ref[1, block], place_ref[0, block]] = term.astype(jnp.bfloat16)
-
     for block, ref in enumerate(first_refs):
-        put(core, block, early_ref[block])
-        put(1 - core, block, jnp.dot(other_ref[...], ref[...], preferred_element_type=jnp.float32))
-    for half, rows_ref in ((core, gated_ref), (1 - core, other_ref)):
-        for block, term in enumerate(late(rows_ref)):
-            put(half, len(first_refs) + block, term)
-
-
-def project(gated, other, places, early, first, onward, across):
-    return pl.pallas_call(
-        project_kernel,
-        out_shape=jax.ShapeDtypeStruct((2, 2, 4, *early.shape[1:]), jnp.bfloat16),
-        in_specs=[pl.BlockSpec(memory_space=pltpu.VMEM)] * 2
-        + [pl.BlockSpec(memory_space=pltpu.SMEM)]
-        + [pl.BlockSpec(memory_space=pltpu.VMEM)] * (len(first) + 3),
-        compiler_params=pltpu.CompilerParams(vmem_limit_bytes=32 * 1024 * 1024),
-        cost_estimate=pl.CostEstimate(flops=1500000000, bytes_accessed=7000000, transcendentals=0),
-        name="project",
-    )(gated, other, places, early, *first, onward, across)
+        term = jnp.dot(other_ref[...], ref[...], preferred_element_type=jnp.float32)
+        out_ref[place_ref[1, block], place_ref[2, block]] = term.astype(jnp.bfloat16)
+    for block, term in enumerate(late_blocks(other_ref, onward_ref, across_ref), len(first_refs)):
+        out_ref[place_ref[1, block], place_ref[2, block]] = term.astype(jnp.bfloat16)
+
+
+def project(kernel, lead, rows, places, weights):
+    return pl.pallas_call(
+        kernel,
+        out_shape=jax.ShapeDtypeStruct((*lead, rows.shape[0], weights[-1].shape[1]), jnp.bfloat16),
+        in_specs=[pl.BlockSpec(memory_space=pltpu.VMEM), pl.BlockSpec(memory_space=pltpu.SMEM)]
+        + [pl.BlockSpec(memory_space=pltpu.VMEM)] * len(weights),
+        compiler_params=pltpu.CompilerParams(vmem_limit_bytes=32 * 1024 * 1024),
+        cost_estimate=pl.CostEstimate(flops=800000000, bytes_accessed=4000000, transcendentals=0),
+        name=kernel.__name__,
+    )(rows, places, *weights)
 
 
 def add_up(*terms):
@@ -249,9 +257,9 @@
     seq_len = steps * 16
     core, x, yh, z, yl = (lax.axis_index(name) for name in ("core", "x", "yh", "z", "yl"))
     first = first_weights(out_weight)
-    own, rate, gain = end_state(keys, values, decay, residue, seq_len)
-    first, late_gain = lax.optimization_barrier((first, gain))
-    local = local_part(keys, values, rate, late_gain, skip.reshape(ROWS, LANES))
+    own, rate = end_state(keys, values, decay, seq_len)
+    first, late_rate = lax.optimization_barrier((first, rate))
+    local, gain = local_part(keys, values, late_rate, residue, skip.reshape(ROWS, LANES))
     state, local = incoming_state(own, rate, steps, local)
     far_opposite, onward, across = second_weights(*first)
     state, far_opposite = lax.optimization_barrier((state, far_opposite))
@@ -261,18 +269,19 @@
     column = [yh * 4 + (x + j) % 4 for j in (0, ahead, behind)] + [(yh ^ 1) * 4 + x]
     column += [(yh ^ 1) * 4 + (x + 2) % 4, yh * 4 + (x + 2) % 4]
     column += [(yh ^ 1) * 4 + (x + j) % 4 for j in (behind, ahead)]
-    places = [[(c // 2 - z) % 4 for c in column], [c % 2 ^ yl for c in column], [core] * 8]
+    places = [[(c // 2 - z) % 4 for c in column], [c % 2 ^ yl for c in column], [c // 2 for c in column]]
     places = jnp.stack([jnp.stack(row) for row in places]).astype(jnp.int32)
     first = (out_weight, *first, far_opposite)
-    near, away = project(gated, other, places, project_early(gated, first), first, onward, across)
-    ring = add_up(away[:, 0], *[shift(away[:, j], "z", j) for j in (2, 1, 3)])
+    other, early = lax.optimization_barrier((other, project_early(gated, first)))
+    near = project(project_other_kernel, (2, 4), other, places, (*first, onward, across))
+    near, gated = lax.optimization_barrier((near, gated))
+    away = project(project_own_kernel, (4, 2), gated, places, (early, onward, across))
     pair = add_up(near[0], shift(near[1], "yl", 1))
-    top = add_up(pair[0], *[shift(pair[j], "z", j) for j in (2, 1, 3)])
-    end = add_up(ring[0], shift(ring[1], "yl", 1))
-    mine = jnp.where(core == 0, top, end)
-    got = shift(jnp.where(core == 0, end, top), "core", 1)
+    got = shift(add_up(*lax.all_to_all(pair, "z", 0, 0)), "core", 1)
+    ring = add_up(away[0], *[shift(away[j], "z", j) for j in (2, 1, 3)])
+    kept = add_up(ring[0], shift(ring[1], "yl", 1))
     return jnp.where(
-        core == 0, jnp.concatenate([mine, got], 1), jnp.concatenate([got, mine], 1)
+        core == 0, jnp.concatenate([kept, got], 1), jnp.concatenate([got, kept], 1)
     )
 
 

time: 80.9 us -> 78.5 us (0.970)
  waiting for transfers between devices: 18.3 us -> 15.5 us
  local copies, waits for them, and re-layouts: 8.93 us -> 7.5 us
  starting transfers between devices: 35.7 us -> 36.9 us
  Pallas kernels: 11.4 us -> 12.4 us
    ppermute x15 -> x12, waiting for transfers between devices: 18.3 us -> 7.05 us  [shift(): lax.ppermute(value, axis, [(i, (i + step) % size) for i in range(size)])]
    all_to_all x0 -> x1, waiting for transfers between devices: none -> 5.19 us  [body(): got = shift(add_up(*lax.all_to_all(pair, 'z', 0, 0)), 'core', 1)]
    all_to_all x0 -> x1, starting transfers between devices: none -> 5.03 us  [body(): got = shift(add_up(*lax.all_to_all(pair, 'z', 0, 0)), 'core', 1)]
    ppermute x15 -> x12, starting transfers between devices: 27.9 us -> 24.1 us  [shift(): lax.ppermute(value, axis, [(i, (i + step) % size) for i in range(size)])]
    ppermute x3, waiting for transfers between devices: 0.01 us -> 3.22 us  [both_ways(): lax.ppermute(value, ('x', 'core'), [(2 * i + c, 2 * ((i + (1 - 2 * c) * s...]
    unnamed x24 -> x32, local copies, waits for them, and re-layouts: 7.73 us -> 6.39 us
    pallas_call x2 -> x3, Pallas kernels: 6.96 us -> 7.97 us  [the longest x2 4.33 us: project(): pl.pallas_call(kernel, out_shape=jax.ShapeDtypeStruct((*lead, rows.shape[...]
    select_n x1, other arithmetic: 0.86 us -> 0.02 us  [incoming_state(): return (jnp.where(core == 0, before, jnp.exp(-hop) * before + first), local)]
  transfers between devices with their start and end apart: 19 -> 17, of which waited for: 9 -> 9; matrix products, arithmetic and copies ran while one was open for 7% -> 7% of each run, Pallas kernels for 10% -> 13%
where the time goes in v3:
time: 78.5 us; the launch traced here: 77.9 us
  starting transfers between devices  36.9 us (47%)
  waiting for transfers between devices  15.5 us (20%)
  Pallas kernels  12.4 us (16%)
  local copies, waits for them, and re-layouts  7.5 us (10%)
  other arithmetic  5.48 us (7%)
    ppermute x12, starting transfers between devices, shift(): lax.ppermute(value, axis, [(i, (i + step) % size) for i in range(size)])  24.1 us
    ppermute x12, waiting for transfers between devices, shift(): lax.ppermute(value, axis, [(i, (i + step) % size) for i in range(size)])  7.05 us
    unnamed x32, local copies, waits for them, and re-layouts  6.39 us
    all_to_all x1, waiting for transfers between devices, body(): got = shift(add_up(*lax.all_to_all(pair, 'z', 0, 0)), 'core', 1)  5.19 us
    all_to_all x1, starting transfers between devices, body(): got = shift(add_up(*lax.all_to_all(pair, 'z', 0, 0)), 'core', 1)  5.03 us
    pallas_call x2, Pallas kernels, project(): pl.pallas_call(kernel, out_shape=jax.ShapeDtypeStruct((*lead, rows.shape[...  4.33 us
    all_to_all x1, starting transfers between devices, incoming_state(): lax.all_to_all(jnp.broadcast_to(mine[None], (8, *mine.shape)), ('yh', 'x'...  4.23 us
    pallas_call x1, Pallas kernels, local_part(): pl.pallas_call(local_kernel, out_shape=(jax.ShapeDtypeStruct((ROWS * step...  3.64 us
  transfers between devices with their start and end apart: 17, of which 9 were waited for; matrix products, arithmetic and copies ran while one was open for 7% of the time, Pallas kernels for 13%

profile of v3, /device:TPU:1, one launch (start us, length us, event | category | flops | bytes accessed | tf_op | source)
XLA Modules:
  0.0 77.9 jit_solution(7624671559476543566)
XLA Ops:
  0.0 3.7 %collective-permute-start.3 = (bf16[1024,256]{1,0:T(8,128)(2,1)}, bf16[1024,256]{1,0:T(8,128)(2,1)S(1)}, u32[]{:S(2)}, u32[]{:S(2)}) collective-permute-start(bf16[1024,256]{1,0:T(8,128)(2,1)} %refs_0_.3), channel_id=1, source_target_pairs={{0,64},{64,0},{1,65},{65,1},{2,66},{66,2},{3,67},{67,3},{4,68},{68... | collective-permute-start | bytes 1572872 | tf_op jit(solution)/shard_map/ppermute | solution.py:21
  3.7 1.2 %collective-permute-start.2 = (bf16[1024,256]{1,0:T(8,128)(2,1)}, bf16[1024,256]{1,0:T(8,128)(2,1)S(1)}, u32[]{:S(2)}, u32[]{:S(2)}) collective-permute-start(bf16[1024,256]{1,0:T(8,128)(2,1)} %refs_0_.3), channel_id=1, source_target_pairs={{0,48},{8,24},{16,0},{24,40},{32,16},{40,56},{48,32},{56,8},{1,49}... | collective-permute-start | bytes 1572872 | tf_op jit(solution)/shard_map/ppermute | solution.py:175
  5.0 1.5 %collective-permute-start.1 = (bf16[1024,256]{1,0:T(8,128)(2,1)}, bf16[1024,256]{1,0:T(8,128)(2,1)S(1)}, u32[]{:S(2)}, u32[]{:S(2)}) collective-permute-start(bf16[1024,256]{1,0:T(8,128)(2,1)} %refs_0_.3), channel_id=1, source_target_pairs={{0,16},{8,56},{16,32},{24,8},{32,48},{40,24},{48,0},{56,40},{1,17}... | collective-permute-start | bytes 1572872 | tf_op jit(solution)/shard_map/ppermute | solution.py:175
  6.4 1.0 %copy-done = bf16[256,1024]{1,0:T(8,128)(2,1)S(1)} copy-done((bf16[256,1024]{1,0:T(8,128)(2,1)S(1)}, bf16[256,1024]{1,0:T(8,128)(2,1)}, u32[]{:S(2)}) %copy-start) | copy-done | bytes 524312
  7.5 1.0 %copy-done.2 = bf16[256,1024]{1,0:T(8,128)(2,1)S(1)} copy-done((bf16[256,1024]{1,0:T(8,128)(2,1)S(1)}, bf16[256,1024]{1,0:T(8,128)(2,1)}, u32[]{:S(2)}) %copy-start.2) | copy-done | bytes 524312
  8.5 0.8 %copy-done.11 = f32[1024,16]{0,1:T(8,128)S(1)} copy-done((f32[1024,16]{0,1:T(8,128)S(1)}, f32[1024,16]{0,1:T(8,128)}, u32[]{:S(2)}) %copy-start.11) | copy-done | bytes 65560
  9.3 1.8 %end_state.1 = (f32[16,8,128]{2,1,0:T(8,128)S(1)}, f32[16,8,128]{2,1,0:T(8,128)S(1)}) custom-call(bf16[256,1024]{1,0:T(8,128)(2,1)S(1)} %copy-done, bf16[256,1024]{1,0:T(8,128)(2,1)S(1)} %copy-done.2, f32[16,1024]{1,0:T(8,128)S(1)} %bitcast.99), custom_call_target="tpu_custom_call" | custom-call | flops 9000000 | bytes 1200000 | tf_op jit(solution)/shard_map/end_state/pallas_call | solution.py:110
  11.1 1.1 %collective-permute-start = (f32[16,8,128]{2,1,0:T(8,128)S(1)}, f32[16,8,128]{2,1,0:T(8,128)S(1)}, u32[]{:S(2)}, u32[]{:S(2)}) collective-permute-start(f32[16,8,128]{2,1,0:T(8,128)S(1)} %get-tuple-element.22), channel_id=1, source_target_pairs={{0,8},{8,0},{1,9},{9,1},{2,10},{10,2},{3,11},{11,3},{4,12},{12,4},... | collective-permute-start | bytes 196616 | tf_op jit(solution)/shard_map/ppermute | solution.py:21
  12.3 0.6 broadcast_multiply_fusion
  12.9 0.3 collective-permute-done
  13.2 0.7 broadcast_in_dim.17
  13.9 4.2 %all-to-all-start = ((f32[8,8,8,128]{3,2,1,0:T(8,128)}), f32[8,8,8,128]{3,2,1,0:T(8,128)S(1)}, u32[]{:S(2)}, u32[]{:S(2)}) async-start(f32[8,8,8,128]{3,2,1,0:T(8,128)} %broadcast_in_dim.17), calls=%async_computation | async-start | bytes 524288 | tf_op jit(solution)/shard_map/all_to_all | solution.py:162
  18.2 0.7 collective-permute-done.1.refs_1_
  19.0 2.3 %collective-permute-start.5 = (bf16[1024,256]{1,0:T(8,128)(2,1)S(1)}, bf16[1024,256]{1,0:T(8,128)(2,1)S(1)}, u32[]{:S(2)}, u32[]{:S(2)}) collective-permute-start(bf16[1024,256]{1,0:T(8,128)(2,1)S(1)} %collective-permute-done.3.refs_3_), channel_id=1, source_target_pairs={{0,32},{16,48},{32,0},{48,16},{1,33},{17,49},{33,1},{49,17},{2,34}... | collective-permute-start | bytes 1572872 | tf_op jit(solution)/shard_map/ppermute | solution.py:21
  21.3 0.9 %pad_maximum_fusion = bf16[1664,256]{1,0:T(8,128)(2,1)} fusion(bf16[640,256]{1,0:T(8,128)(2,1)S(1)} %slice.63, bf16[1024,256]{1,0:T(8,128)(2,1)S(1)} %collective-permute-done.2.refs_2_), kind=kLoop, calls=%fused_computation.2 | loop fusion | flops 1703936 | bytes 1703936 | tf_op jit(solution)/shard_map/concatenate | solution.py:189
  22.3 2.7 %collective-permute-start.8 = (bf16[1664,256]{1,0:T(8,128)(2,1)}, bf16[1664,256]{1,0:T(8,128)(2,1)S(1)}, u32[]{:S(2)}, u32[]{:S(2)}) collective-permute-start(bf16[1664,256]{1,0:T(8,128)(2,1)} %pad_maximum_fusion), channel_id=1, source_target_pairs={{0,64},{64,0},{1,65},{65,1},{2,66},{66,2},{3,67},{67,3},{4,68},{68... | collective-permute-start | bytes 2555912 | tf_op jit(solution)/shard_map/ppermute | solution.py:21
  25.0 3.6 %local_part.1 = (f32[2048,128]{1,0:T(8,128)S(1)}, f32[16,8,128]{2,1,0:T(8,128)S(1)}) custom-call(bf16[256,1024]{1,0:T(8,128)(2,1)S(1)} %copy-done.1, bf16[256,1024]{1,0:T(8,128)(2,1)S(1)} %copy-done.3, f32[16,8,128]{2,1,0:T(8,128)S(1)} %get-tuple-element.23.rate_ref, f32[16,1024]{1,0:T(8,128)S(1)} %bitcast.100, f32[8,128]{1,0:T(8,128)S(1)} %bitcast.101), custom_call_target="tpu_custom_call" | custom-call | tf_op jit(solution)/shard_map/local_part/pallas_call | solution.py:125
  28.6 1.0 %copy-done.8 = f32[2048,128]{1,0:T(8,128)} copy-done((f32[2048,128]{1,0:T(8,128)}, f32[2048,128]{1,0:T(8,128)S(1)}, u32[]{:S(2)}) %copy-start.8) | copy-done | bytes 1048600
  29.6 0.6 copy-done.13
  30.2 0.9 %fusion.7 = f32[8,8,128]{2,1,0:T(8,128)S(1)} fusion(f32[8,8,8,128]{3,2,1,0:T(8,128)S(1)} %all-to-all-done, f32[16,8,128]{2,1,0:T(8,128)} %get-tuple-element.40, s32[]{:T(128)S(6)} %select_n.208, f32[]{:T(128)S(6)} %convert_element_type.90, f32[]{:T(128)S(6)} %convert_element_type.89, f32[]{:T(128)S(6)} %convert_element_type.88, f32[]{:T(128)S(6)} %convert_element_type.87, ...), kind=kLoop, calls=%fused_computation.27 | loop fusion | flops 262144 | bytes 327724 | tf_op jit(solution)/shard_map/add | solution.py:168
  31.2 1.6 %collective-permute-start.4 = (f32[8,8,128]{2,1,0:T(8,128)S(1)}, f32[8,8,128]{2,1,0:T(8,128)S(1)}, u32[]{:S(2)}, u32[]{:S(2)}) collective-permute-start(f32[8,8,128]{2,1,0:T(8,128)S(1)} %fusion.7), channel_id=1, source_target_pairs={{0,8},{8,0},{1,9},{9,1},{2,10},{10,2},{3,11},{11,3},{4,12},{12,4},... | collective-permute-start | bytes 98312 | tf_op jit(solution)/shard_map/ppermute | solution.py:21
  32.7 0.9 %pad_maximum_fusion.1 = bf16[1408,256]{1,0:T(8,128)(2,1)} fusion(bf16[384,256]{1,0:T(8,128)(2,1)S(1)} %slice.62, bf16[1024,256]{1,0:T(8,128)(2,1)S(1)} %collective-permute-done.1.refs_1_), kind=kLoop, calls=%fused_computation.3 | loop fusion | flops 1441792 | bytes 1441792 | tf_op jit(solution)/shard_map/concatenate | solution.py:188
  33.6 0.9 %collective-permute-start.7 = (bf16[1408,256]{1,0:T(8,128)(2,1)}, bf16[1408,256]{1,0:T(8,128)(2,1)}, u32[]{:S(2)}, u32[]{:S(2)}) collective-permute-start(bf16[1408,256]{1,0:T(8,128)(2,1)} %pad_maximum_fusion.1), channel_id=1, source_target_pairs={{0,16},{8,56},{16,32},{24,8},{32,48},{40,24},{48,0},{56,40},{1,17}... | collective-permute-start | bytes 2162696 | tf_op jit(solution)/shard_map/ppermute | solution.py:175
  34.6 1.0 %collective-permute-done.5.refs_4_ = bf16[1024,256]{1,0:T(8,128)(2,1)S(1)} collective-permute-done((bf16[1024,256]{1,0:T(8,128)(2,1)S(1)}, bf16[1024,256]{1,0:T(8,128)(2,1)S(1)}, u32[]{:S(2)}, u32[]{:S(2)}) %collective-permute-start.5) | collective-permute-done | bytes 524320 | tf_op jit(solution)/shard_map/ppermute | solution.py:21
  35.5 0.8 %copy-done.5 = bf16[1024,256]{1,0:T(8,128)(2,1)} copy-done((bf16[1024,256]{1,0:T(8,128)(2,1)}, bf16[1024,256]{1,0:T(8,128)(2,1)S(1)}, u32[]{:S(2)}) %copy-start.5) | copy-done | bytes 524312
  36.3 1.8 %gated.1.gated_ref = bf16[256,1024]{1,0:T(8,128)(2,1)S(1)} custom-call(bf16[256,1024]{1,0:T(8,128)(2,1)S(1)} %copy-done.10, f32[2048,128]{1,0:T(8,128)S(1)} %copy-done.9, f32[16,8,128]{2,1,0:T(8,128)S(1)} %get-tuple-element.23.rate_ref, f32[16,8,128]{2,1,0:T(8,128)S(1)} %copy-done.14, f32[16,8,128]{2,1,0:T(8,128)S(1)} %add_select_fusion.state_ref), custom_call_target="tpu_custom_call" | custom-call | tf_op jit(solution)/shard_map/gated/pallas_call | solution.py:142
  38.1 1.6 %collective-permute-start.6 = (bf16[256,1024]{1,0:T(8,128)(2,1)S(1)}, bf16[256,1024]{1,0:T(8,128)(2,1)}, u32[]{:S(2)}, u32[]{:S(2)}) collective-permute-start(bf16[256,1024]{1,0:T(8,128)(2,1)S(1)} %gated.1.gated_ref), channel_id=1, source_target_pairs={{0,8},{8,0},{1,9},{9,1},{2,10},{10,2},{3,11},{11,3},{4,12},{12,4},... | collective-permute-start | bytes 1572872 | tf_op jit(solution)/shard_map/ppermute | solution.py:21
  39.7 0.1 stack.101
  40.0 1.0 %copy-done.6 = bf16[1024,256]{1,0:T(8,128)(2,1)S(1)} copy-done((bf16[1024,256]{1,0:T(8,128)(2,1)S(1)}, bf16[1024,256]{1,0:T(8,128)(2,1)}, u32[]{:S(2)}) %copy-start.6) | copy-done | bytes 524312
  41.0 0.8 %project_early.1.early_ref = bf16[5,256,256]{2,1,0:T(8,128)(2,1)S(1)} custom-call(bf16[256,1024]{1,0:T(8,128)(2,1)S(1)} %gated.1.gated_ref, bf16[1024,256]{1,0:T(8,128)(2,1)S(1)} %copy-done.4, bf16[1024,256]{1,0:T(8,128)(2,1)S(1)} %collective-permute-done.1.refs_1_, bf16[1024,256]{1,0:T(8,128)(2,1)S(1)} %collective-permute-done.2.refs_2_, ...), custom_call_target="tpu_custom_call" | custom-call | tf_op jit(solution)/shard_map/project_early/pallas_call | solution.py:200
  41.9 2.5 %collective-permute-done.7.refs_5_.onward_ref = bf16[1408,256]{1,0:T(8,128)(2,1)} collective-permute-done((bf16[1408,256]{1,0:T(8,128)(2,1)}, bf16[1408,256]{1,0:T(8,128)(2,1)}, u32[]{:S(2)}, u32[]{:S(2)}) %collective-permute-start.7) | collective-permute-done | bytes 720928 | tf_op jit(solution)/shard_map/ppermute | solution.py:175
  44.4 0.2 collective-permute-done.8.refs_6_.across_ref
  44.6 2.6 %project_other_kernel.1 = bf16[2,4,256,256]{3,2,1,0:T(8,128)(2,1)S(1)} custom-call(bf16[256,1024]{1,0:T(8,128)(2,1)} %collective-permute-done.6.other_ref, s32[3,8]{1,0:T(4,128)S(1)} %pad_add_fusion.place_ref, bf16[1024,256]{1,0:T(8,128)(2,1)S(1)} %copy-done.4, bf16[1024,256]{1,0:T(8,128)(2,1)S(1)} %collective-permute-done.1.refs_1_, ...), custom_call_target="tpu_custom_call" | custom-call | flops 800000000 | bytes 4000000 | tf_op jit(solution)/shard_map/project_other_kernel/pallas_call | solution.py:237
  47.3 1.3 %collective-permute-start.13 = (bf16[4,256,256]{2,1,0:T(8,128)(2,1)S(1)}, bf16[4,256,256]{2,1,0:T(8,128)(2,1)S(1)}, u32[]{:S(2)}, u32[]{:S(2)}) collective-permute-start(bf16[4,256,256]{2,1,0:T(8,128)(2,1)S(1)} %slice_bitcast_fusion), channel_id=1, source_target_pairs={{0,1},{1,0},{2,3},{3,2},{4,5},{5,4},{6,7},{7,6},{8,9},{9,8},{10,11... | collective-permute-start | bytes 1572872 | tf_op jit(solution)/shard_map/ppermute | solution.py:21
  48.5 1.7 %project_own_kernel.1 = bf16[4,2,256,256]{3,2,1,0:T(8,128)(2,1)S(1)} custom-call(bf16[256,1024]{1,0:T(8,128)(2,1)S(1)} %gated.1.gated_ref, s32[3,8]{1,0:T(4,128)S(1)} %pad_add_fusion.place_ref, bf16[5,256,256]{2,1,0:T(8,128)(2,1)S(1)} %project_early.1.early_ref, bf16[1408,256]{1,0:T(8,128)(2,1)} %collective-permute-done.7.refs_5_.onward_ref, ...), custom_call_target="tpu_custom_call" | custom-call | flops 800000000 | bytes 4000000 | tf_op jit(solution)/shard_map/project_own_kernel/pallas_call | solution.py:237
  50.3 3.7 %collective-permute-start.9 = (bf16[2,256,256]{2,1,0:T(8,128)(2,1)S(1)}, bf16[2,256,256]{2,1,0:T(8,128)(2,1)S(1)}, u32[]{:S(2)}, u32[]{:S(2)}) collective-permute-start(bf16[2,256,256]{2,1,0:T(8,128)(2,1)S(1)} %get-tuple-element.37), channel_id=1, source_target_pairs={{0,4},{2,6},{4,0},{6,2},{1,5},{3,7},{5,1},{7,3},{8,12},{10,14},{12... | collective-permute-start | bytes 786440 | tf_op jit(solution)/shard_map/ppermute | solution.py:21
  54.0 0.4 collective-permute-start.11
  54.4 1.0 %collective-permute-start.10 = (bf16[2,256,256]{2,1,0:T(8,128)(2,1)S(1)}, bf16[2,256,256]{2,1,0:T(8,128)(2,1)S(1)}, u32[]{:S(2)}, u32[]{:S(2)}) collective-permute-start(bf16[2,256,256]{2,1,0:T(8,128)(2,1)S(1)} %get-tuple-element.39), channel_id=1, source_target_pairs={{0,2},{2,4},{4,6},{6,0},{1,3},{3,5},{5,7},{7,1},{8,10},{10,12},{12... | collective-permute-start | bytes 786440 | tf_op jit(solution)/shard_map/ppermute | solution.py:21
  55.5 3.4 %collective-permute-done.13 = bf16[4,256,256]{2,1,0:T(8,128)(2,1)S(1)} collective-permute-done((bf16[4,256,256]{2,1,0:T(8,128)(2,1)S(1)}, bf16[4,256,256]{2,1,0:T(8,128)(2,1)S(1)}, u32[]{:S(2)}, u32[]{:S(2)}) %collective-permute-start.13) | collective-permute-done | bytes 524320 | tf_op jit(solution)/shard_map/ppermute | solution.py:21
  58.9 0.9 %fusion = bf16[4,256,256]{2,1,0:T(8,128)(2,1)} fusion(bf16[4,256,256]{2,1,0:T(8,128)(2,1)S(1)} %collective-permute-done.13, bf16[2,4,256,256]{3,2,1,0:T(8,128)(2,1)S(1)} %project_other_kernel.1), kind=kLoop, calls=%fused_computation.1 | loop fusion | flops 1048576 | bytes 1572864 | tf_op jit(solution)/shard_map/convert_element_type | solution.py:252
  59.8 5.0 %all-to-all-start.1 = ((bf16[4,256,256]{2,1,0:T(8,128)(2,1)}), bf16[4,256,256]{2,1,0:T(8,128)(2,1)S(1)}, u32[]{:S(2)}, u32[]{:S(2)}) async-start(bf16[4,256,256]{2,1,0:T(8,128)(2,1)} %fusion), calls=%async_computation.1 | async-start | bytes 1048576 | tf_op jit(solution)/shard_map/all_to_all | solution.py:280
  64.9 1.2 %collective-permute-done.11 = bf16[2,256,256]{2,1,0:T(8,128)(2,1)S(1)} collective-permute-done((bf16[2,256,256]{2,1,0:T(8,128)(2,1)S(1)}, bf16[2,256,256]{2,1,0:T(8,128)(2,1)S(1)}, u32[]{:S(2)}, u32[]{:S(2)}) %collective-permute-start.11) | collective-permute-done | bytes 262176 | tf_op jit(solution)/shard_map/ppermute | solution.py:21
  66.1 0.1 fusion.3
  66.2 0.4 collective-permute-start.12
  66.6 5.2 %all-to-all-done.1 = bf16[4,256,256]{2,1,0:T(8,128)(2,1)S(1)} async-done(((bf16[4,256,256]{2,1,0:T(8,128)(2,1)}), bf16[4,256,256]{2,1,0:T(8,128)(2,1)S(1)}, u32[]{:S(2)}, u32[]{:S(2)}) %all-to-all-start.1) | async-done | bytes 524320 | tf_op jit(solution)/shard_map/all_to_all | solution.py:280
  71.9 4.3 %collective-permute-start.14 = (bf16[256,256]{1,0:T(8,128)(2,1)S(1)}, bf16[256,256]{1,0:T(8,128)(2,1)S(1)}, u32[]{:S(2)}, u32[]{:S(2)}) collective-permute-start(bf16[256,256]{1,0:T(8,128)(2,1)S(1)} %fusion.5), channel_id=1, source_target_pairs={{0,8},{8,0},{1,9},{9,1},{2,10},{10,2},{3,11},{11,3},{4,12},{12,4},... | collective-permute-start | bytes 393224 | tf_op jit(solution)/shard_map/ppermute | solution.py:21
  76.2 0.9 %collective-permute-done.14 = bf16[256,256]{1,0:T(8,128)(2,1)S(1)} collective-permute-done((bf16[256,256]{1,0:T(8,128)(2,1)S(1)}, bf16[256,256]{1,0:T(8,128)(2,1)S(1)}, u32[]{:S(2)}, u32[]{:S(2)}) %collective-permute-start.14) | collective-permute-done | bytes 131104 | tf_op jit(solution)/shard_map/ppermute | solution.py:21
  77.1 0.8 %maximum_select_fusion = bf16[256,512]{1,0:T(8,128)(2,1)} fusion(bf16[256,256]{1,0:T(8,128)(2,1)S(1)} %collective-permute-done.14, bf16[256,256]{1,0:T(8,128)(2,1)S(1)} %fusion.4, pred[]{:T(512)S(6)} %eq.31), kind=kLoop, calls=%fused_computation.13 | loop fusion | flops 1179648 | bytes 524289 | tf_op jit(solution)/shard_map/jit(_where)/select_n | solution.py:283
  (46 shorter events, 0.5 us)
Async XLA Ops:
  0.0 18.2 %collective-permute-start.3 = (bf16[1024,256]{1,0:T(8,128)(2,1)}, bf16[1024,256]{1,0:T(8,128)(2,1)S(1)}, u32[]{:S(2)}, u32[]{:S(2)}) collective-permute-start(bf16[1024,256]{1,0:T(8,128)(2,1)} %refs_0_.3), channel_id=1, source_target_pairs={{0,64},{64,0},{1,65},{65,1},{2,66},{66,2},{3,67},{67,3},{4,68},{68... | collective-permute-start | bytes 1572872 | tf_op jit(solution)/shard_map/ppermute | solution.py:21
  3.7 14.4 %collective-permute-start.2 = (bf16[1024,256]{1,0:T(8,128)(2,1)}, bf16[1024,256]{1,0:T(8,128)(2,1)S(1)}, u32[]{:S(2)}, u32[]{:S(2)}) collective-permute-start(bf16[1024,256]{1,0:T(8,128)(2,1)} %refs_0_.3), channel_id=1, source_target_pairs={{0,48},{8,24},{16,0},{24,40},{32,16},{40,56},{48,32},{56,8},{1,49}... | collective-permute-start | bytes 1572872 | tf_op jit(solution)/shard_map/ppermute | solution.py:175
  5.0 13.9 %collective-permute-start.1 = (bf16[1024,256]{1,0:T(8,128)(2,1)}, bf16[1024,256]{1,0:T(8,128)(2,1)S(1)}, u32[]{:S(2)}, u32[]{:S(2)}) collective-permute-start(bf16[1024,256]{1,0:T(8,128)(2,1)} %refs_0_.3), channel_id=1, source_target_pairs={{0,16},{8,56},{16,32},{24,8},{32,48},{40,24},{48,0},{56,40},{1,17}... | collective-permute-start | bytes 1572872 | tf_op jit(solution)/shard_map/ppermute | solution.py:175
  6.4 1.0 %copy-start = (bf16[256,1024]{1,0:T(8,128)(2,1)S(1)}, bf16[256,1024]{1,0:T(8,128)(2,1)}, u32[]{:S(2)}) copy-start(bf16[256,1024]{1,0:T(8,128)(2,1)} %keys_ref.3) | copy-start | bytes 1572868
  7.5 1.0 %copy-start.2 = (bf16[256,1024]{1,0:T(8,128)(2,1)S(1)}, bf16[256,1024]{1,0:T(8,128)(2,1)}, u32[]{:S(2)}) copy-start(bf16[256,1024]{1,0:T(8,128)(2,1)} %values_ref.3) | copy-start | bytes 1572868
  8.5 0.8 %copy-start.11 = (f32[1024,16]{0,1:T(8,128)S(1)}, f32[1024,16]{0,1:T(8,128)}, u32[]{:S(2)}) copy-start(f32[1024,16]{0,1:T(8,128)} %param.10) | copy-start | bytes 196612
  11.1 2.0 %collective-permute-start = (f32[16,8,128]{2,1,0:T(8,128)S(1)}, f32[16,8,128]{2,1,0:T(8,128)S(1)}, u32[]{:S(2)}, u32[]{:S(2)}) collective-permute-start(f32[16,8,128]{2,1,0:T(8,128)S(1)} %get-tuple-element.22), channel_id=1, source_target_pairs={{0,8},{8,0},{1,9},{9,1},{2,10},{10,2},{3,11},{11,3},{4,12},{12,4},... | collective-permute-start | bytes 196616 | tf_op jit(solution)/shard_map/ppermute | solution.py:21
  13.9 16.3 %all-to-all-start = ((f32[8,8,8,128]{3,2,1,0:T(8,128)}), f32[8,8,8,128]{3,2,1,0:T(8,128)S(1)}, u32[]{:S(2)}, u32[]{:S(2)}) async-start(f32[8,8,8,128]{3,2,1,0:T(8,128)} %broadcast_in_dim.17), calls=%async_computation | async-start | bytes 524288 | tf_op jit(solution)/shard_map/all_to_all | solution.py:162
  18.9 6.0 %copy-start.1 = (bf16[256,1024]{1,0:T(8,128)(2,1)S(1)}, bf16[256,1024]{1,0:T(8,128)(2,1)}, u32[]{:S(2)}) copy-start(bf16[256,1024]{1,0:T(8,128)(2,1)} %keys_ref.3) | copy-start | bytes 1572868
  18.9 6.0 %copy-start.3 = (bf16[256,1024]{1,0:T(8,128)(2,1)S(1)}, bf16[256,1024]{1,0:T(8,128)(2,1)}, u32[]{:S(2)}) copy-start(bf16[256,1024]{1,0:T(8,128)(2,1)} %values_ref.3) | copy-start | bytes 1572868
  18.9 6.0 %copy-start.12 = (f32[1024,16]{0,1:T(8,128)S(1)}, f32[1024,16]{0,1:T(8,128)}, u32[]{:S(2)}) copy-start(f32[1024,16]{0,1:T(8,128)} %param.11) | copy-start | bytes 196612
  19.0 6.0 %copy-start.15 = (f32[1024]{0:T(1024)S(1)}, f32[1024]{0:T(1024)}, u32[]{:S(2)}) copy-start(f32[1024]{0:T(1024)} %param.12) | copy-start | bytes 12292
  19.0 16.5 %collective-permute-start.5 = (bf16[1024,256]{1,0:T(8,128)(2,1)S(1)}, bf16[1024,256]{1,0:T(8,128)(2,1)S(1)}, u32[]{:S(2)}, u32[]{:S(2)}) collective-permute-start(bf16[1024,256]{1,0:T(8,128)(2,1)S(1)} %collective-permute-done.3.refs_3_), channel_id=1, source_target_pairs={{0,32},{16,48},{32,0},{48,16},{1,33},{17,49},{33,1},{49,17},{2,34}... | collective-permute-start | bytes 1572872 | tf_op jit(solution)/shard_map/ppermute | solution.py:21
  22.3 22.4 %collective-permute-start.8 = (bf16[1664,256]{1,0:T(8,128)(2,1)}, bf16[1664,256]{1,0:T(8,128)(2,1)S(1)}, u32[]{:S(2)}, u32[]{:S(2)}) collective-permute-start(bf16[1664,256]{1,0:T(8,128)(2,1)} %pad_maximum_fusion), channel_id=1, source_target_pairs={{0,64},{64,0},{1,65},{65,1},{2,66},{66,2},{3,67},{67,3},{4,68},{68... | collective-permute-start | bytes 2555912 | tf_op jit(solution)/shard_map/ppermute | solution.py:21
  28.6 1.0 %copy-start.8 = (f32[2048,128]{1,0:T(8,128)}, f32[2048,128]{1,0:T(8,128)S(1)}, u32[]{:S(2)}) copy-start(f32[2048,128]{1,0:T(8,128)S(1)} %get-tuple-element.25.y_ref) | copy-start | bytes 3145732
  29.6 0.6 copy-start.13
  30.2 6.1 %copy-start.9 = (f32[2048,128]{1,0:T(8,128)S(1)}, f32[2048,128]{1,0:T(8,128)}, u32[]{:S(2)}) copy-start(f32[2048,128]{1,0:T(8,128)} %copy-done.8) | copy-start | bytes 3145732
  30.2 6.1 %copy-start.10 = (bf16[256,1024]{1,0:T(8,128)(2,1)S(1)}, bf16[256,1024]{1,0:T(8,128)(2,1)}, u32[]{:S(2)}) copy-start(bf16[256,1024]{1,0:T(8,128)(2,1)} %queries_ref.1) | copy-start | bytes 1572868
  30.2 6.1 %copy-start.14 = (f32[16,8,128]{2,1,0:T(8,128)S(1)}, f32[16,8,128]{2,1,0:T(8,128)}, u32[]{:S(2)}) copy-start(f32[16,8,128]{2,1,0:T(8,128)} %copy-done.13) | copy-start | bytes 196612
  31.2 3.3 %collective-permute-start.4 = (f32[8,8,128]{2,1,0:T(8,128)S(1)}, f32[8,8,128]{2,1,0:T(8,128)S(1)}, u32[]{:S(2)}, u32[]{:S(2)}) collective-permute-start(f32[8,8,128]{2,1,0:T(8,128)S(1)} %fusion.7), channel_id=1, source_target_pairs={{0,8},{8,0},{1,9},{9,1},{2,10},{10,2},{3,11},{11,3},{4,12},{12,4},... | collective-permute-start | bytes 98312 | tf_op jit(solution)/shard_map/ppermute | solution.py:21
  33.6 10.7 %collective-permute-start.7 = (bf16[1408,256]{1,0:T(8,128)(2,1)}, bf16[1408,256]{1,0:T(8,128)(2,1)}, u32[]{:S(2)}, u32[]{:S(2)}) collective-permute-start(bf16[1408,256]{1,0:T(8,128)(2,1)} %pad_maximum_fusion.1), channel_id=1, source_target_pairs={{0,16},{8,56},{16,32},{24,8},{32,48},{40,24},{48,0},{56,40},{1,17}... | collective-permute-start | bytes 2162696 | tf_op jit(solution)/shard_map/ppermute | solution.py:175
  35.5 0.8 %copy-start.5 = (bf16[1024,256]{1,0:T(8,128)(2,1)}, bf16[1024,256]{1,0:T(8,128)(2,1)S(1)}, u32[]{:S(2)}) copy-start(bf16[1024,256]{1,0:T(8,128)(2,1)S(1)} %collective-permute-done.5.refs_4_) | copy-start | bytes 1572868
  36.3 3.7 %copy-start.4 = (bf16[1024,256]{1,0:T(8,128)(2,1)S(1)}, bf16[1024,256]{1,0:T(8,128)(2,1)}, u32[]{:S(2)}) copy-start(bf16[1024,256]{1,0:T(8,128)(2,1)} %refs_0_.3) | copy-start | bytes 1572868
  38.1 3.8 %collective-permute-start.6 = (bf16[256,1024]{1,0:T(8,128)(2,1)S(1)}, bf16[256,1024]{1,0:T(8,128)(2,1)}, u32[]{:S(2)}, u32[]{:S(2)}) collective-permute-start(bf16[256,1024]{1,0:T(8,128)(2,1)S(1)} %gated.1.gated_ref), channel_id=1, source_target_pairs={{0,8},{8,0},{1,9},{9,1},{2,10},{10,2},{3,11},{11,3},{4,12},{12,4},... | collective-permute-start | bytes 1572872 | tf_op jit(solution)/shard_map/ppermute | solution.py:21
  40.0 1.0 %copy-start.6 = (bf16[1024,256]{1,0:T(8,128)(2,1)S(1)}, bf16[1024,256]{1,0:T(8,128)(2,1)}, u32[]{:S(2)}) copy-start(bf16[1024,256]{1,0:T(8,128)(2,1)} %copy-done.5) | copy-start | bytes 1572868
  41.0 3.6 %copy-start.7 = (bf16[1024,256]{1,0:T(8,128)(2,1)S(1)}, bf16[1024,256]{1,0:T(8,128)(2,1)}, u32[]{:S(2)}) copy-start(bf16[1024,256]{1,0:T(8,128)(2,1)} %copy-done.5) | copy-start | bytes 1572868
  47.3 11.6 %collective-permute-start.13 = (bf16[4,256,256]{2,1,0:T(8,128)(2,1)S(1)}, bf16[4,256,256]{2,1,0:T(8,128)(2,1)S(1)}, u32[]{:S(2)}, u32[]{:S(2)}) collective-permute-start(bf16[4,256,256]{2,1,0:T(8,128)(2,1)S(1)} %slice_bitcast_fusion), channel_id=1, source_target_pairs={{0,1},{1,0},{2,3},{3,2},{4,5},{5,4},{6,7},{7,6},{8,9},{9,8},{10,11... | collective-permute-start | bytes 1572872 | tf_op jit(solution)/shard_map/ppermute | solution.py:21
  50.3 14.5 %collective-permute-start.9 = (bf16[2,256,256]{2,1,0:T(8,128)(2,1)S(1)}, bf16[2,256,256]{2,1,0:T(8,128)(2,1)S(1)}, u32[]{:S(2)}, u32[]{:S(2)}) collective-permute-start(bf16[2,256,256]{2,1,0:T(8,128)(2,1)S(1)} %get-tuple-element.37), channel_id=1, source_target_pairs={{0,4},{2,6},{4,0},{6,2},{1,5},{3,7},{5,1},{7,3},{8,12},{10,14},{12... | collective-permute-start | bytes 786440 | tf_op jit(solution)/shard_map/ppermute | solution.py:21
  54.0 12.1 %collective-permute-start.11 = (bf16[2,256,256]{2,1,0:T(8,128)(2,1)S(1)}, bf16[2,256,256]{2,1,0:T(8,128)(2,1)S(1)}, u32[]{:S(2)}, u32[]{:S(2)}) collective-permute-start(bf16[2,256,256]{2,1,0:T(8,128)(2,1)S(1)} %get-tuple-element.38), channel_id=1, source_target_pairs={{0,6},{2,0},{4,2},{6,4},{1,7},{3,1},{5,3},{7,5},{8,14},{10,8},{12,... | collective-permute-start | bytes 786440 | tf_op jit(solution)/shard_map/ppermute | solution.py:21
  54.4 11.6 %collective-permute-start.10 = (bf16[2,256,256]{2,1,0:T(8,128)(2,1)S(1)}, bf16[2,256,256]{2,1,0:T(8,128)(2,1)S(1)}, u32[]{:S(2)}, u32[]{:S(2)}) collective-permute-start(bf16[2,256,256]{2,1,0:T(8,128)(2,1)S(1)} %get-tuple-element.39), channel_id=1, source_target_pairs={{0,2},{2,4},{4,6},{6,0},{1,3},{3,5},{5,7},{7,1},{8,10},{10,12},{12... | collective-permute-start | bytes 786440 | tf_op jit(solution)/shard_map/ppermute | solution.py:21
  59.8 12.0 %all-to-all-start.1 = ((bf16[4,256,256]{2,1,0:T(8,128)(2,1)}), bf16[4,256,256]{2,1,0:T(8,128)(2,1)S(1)}, u32[]{:S(2)}, u32[]{:S(2)}) async-start(bf16[4,256,256]{2,1,0:T(8,128)(2,1)} %fusion), calls=%async_computation.1 | async-start | bytes 1048576 | tf_op jit(solution)/shard_map/all_to_all | solution.py:280
  66.2 9.9 %collective-permute-start.12 = (bf16[256,256]{1,0:T(8,128)(2,1)S(1)}, bf16[256,256]{1,0:T(8,128)(2,1)S(1)}, u32[]{:S(2)}, u32[]{:S(2)}) collective-permute-start(bf16[256,256]{1,0:T(8,128)(2,1)S(1)} %slice_bitcast_fusion.5), channel_id=1, source_target_pairs={{0,1},{1,0},{2,3},{3,2},{4,5},{5,4},{6,7},{7,6},{8,9},{9,8},{10,11... | collective-permute-start | bytes 393224 | tf_op jit(solution)/shard_map/ppermute | solution.py:21
  71.9 5.3 %collective-permute-start.14 = (bf16[256,256]{1,0:T(8,128)(2,1)S(1)}, bf16[256,256]{1,0:T(8,128)(2,1)S(1)}, u32[]{:S(2)}, u32[]{:S(2)}) collective-permute-start(bf16[256,256]{1,0:T(8,128)(2,1)S(1)} %fusion.5), channel_id=1, source_target_pairs={{0,8},{8,0},{1,9},{9,1},{2,10},{10,2},{3,11},{11,3},{4,12},{12,4},... | collective-permute-start | bytes 393224 | tf_op jit(solution)/shard_map/ppermute | solution.py:21

commit v4 on v3

--- a/solution.py
+++ b/solution.py
@@ -12,7 +12,7 @@
 ALL = SEQ + CH
 SIZES = {"yh": 2, "x": 4, "core": 2, "z": 4, "yl": 2}
 LANES = 128
-CUT = 24
+CUT = 26
 ROWS = 8
 
 
@@ -250,6 +250,20 @@
     for term in terms[1:]:
         total = total + term.astype(jnp.float32)
     return total.astype(jnp.bfloat16)
+
+
+def add_kernel(left_ref, right_ref, out_ref):
+    out_ref[...] = (left_ref[...].astype(jnp.float32) + right_ref[...].astype(jnp.float32)).astype(jnp.bfloat16)
+
+
+def add_pair(left, right):
+    return pl.pallas_call(
+        add_kernel,
+        out_shape=jax.ShapeDtypeStruct(left.shape, left.dtype),
+        compiler_params=pltpu.CompilerParams(vmem_limit_bytes=32 * 1024 * 1024),
+        cost_estimate=pl.CostEstimate(flops=0, bytes_accessed=1500000, transcendentals=0),
+        name="add_pair",
+    )(left, right)
 
 
 def body(keys, values, queries, decay, residue, skip, out_weight):
@@ -276,7 +290,7 @@
     near = project(project_other_kernel, (2, 4), other, places, (*first, onward, across))
     near, gated = lax.optimization_barrier((near, gated))
     away = project(project_own_kernel, (4, 2), gated, places, (early, onward, across))
-    pair = add_up(near[0], shift(near[1], "yl", 1))
+    pair = add_pair(near[0], shift(near[1], "yl", 1))
     got = shift(add_up(*lax.all_to_all(pair, "z", 0, 0)), "core", 1)
     ring = add_up(away[0], *[shift(away[j], "z", j) for j in (2, 1, 3)])
     kept = add_up(ring[0], shift(ring[1], "yl", 1))

time: 78.5 us -> 78.5 us (level)
  other arithmetic: 5.48 us -> 4.57 us
  Pallas kernels: 12.4 us -> 13.3 us
    convert_element_type x3 -> x2, other arithmetic: 1.08 us -> 0.17 us  [add_up(): return total.astype(jnp.bfloat16)]
    pallas_call x0 -> x1, Pallas kernels: none -> 0.9 us  [add_pair(): pl.pallas_call(add_kernel, out_shape=jax.ShapeDtypeStruct(left.shape, lef...]
    unnamed x32 -> x36, local copies, waits for them, and re-layouts: 6.39 us -> 6.42 us
  transfers between devices with their start and end apart: 17 -> 17, of which waited for: 9 -> 8; matrix products, arithmetic and copies ran while one was open for 7% -> 6% of each run, Pallas kernels for 13% -> 14%
where the time goes in v4:
time: 78.5 us; the launch traced here: 78 us
  starting transfers between devices  37.1 us (47%)
  waiting for transfers between devices  15.2 us (19%)
  Pallas kernels  13.3 us (17%)
  local copies, waits for them, and re-layouts  7.56 us (10%)
  other arithmetic  4.57 us (6%)
    ppermute x12, starting transfers between devices, shift(): lax.ppermute(value, axis, [(i, (i + step) % size) for i in range(size)])  24.3 us
    ppermute x12, waiting for transfers between devices, shift(): lax.ppermute(value, axis, [(i, (i + step) % size) for i in range(size)])  6.7 us
    unnamed x36, local copies, waits for them, and re-layouts  6.42 us
    all_to_all x1, starting transfers between devices, body(): got = shift(add_up(*lax.all_to_all(pair, 'z', 0, 0)), 'core', 1)  5.02 us
    all_to_all x1, waiting for transfers between devices, body(): got = shift(add_up(*lax.all_to_all(pair, 'z', 0, 0)), 'core', 1)  5.02 us
    pallas_call x2, Pallas kernels, project(): pl.pallas_call(kernel, out_shape=jax.ShapeDtypeStruct((*lead, rows.shape[...  4.35 us
    all_to_all x1, starting transfers between devices, incoming_state(): lax.all_to_all(jnp.broadcast_to(mine[None], (8, *mine.shape)), ('yh', 'x'...  4.23 us
    pallas_call x1, Pallas kernels, local_part(): pl.pallas_call(local_kernel, out_shape=(jax.ShapeDtypeStruct((ROWS * step...  3.64 us
  transfers between devices with their start and end apart: 17, of which 8 were waited for; matrix products, arithmetic and copies ran while one was open for 6% of the time, Pallas kernels for 14%

profile of v4, /device:TPU:1, one launch (start us, length us, event | category | flops | bytes accessed | tf_op | source)
XLA Modules:
  0.0 78.0 jit_solution(16784002885874907984)
XLA Ops:
  0.0 3.7 %collective-permute-start.3 = (bf16[1024,256]{1,0:T(8,128)(2,1)}, bf16[1024,256]{1,0:T(8,128)(2,1)S(1)}, u32[]{:S(2)}, u32[]{:S(2)}) collective-permute-start(bf16[1024,256]{1,0:T(8,128)(2,1)} %refs_0_.3), channel_id=1, source_target_pairs={{0,64},{64,0},{1,65},{65,1},{2,66},{66,2},{3,67},{67,3},{4,68},{68... | collective-permute-start | bytes 1572872 | tf_op jit(solution)/shard_map/ppermute | solution.py:21
  3.7 1.2 %collective-permute-start.2 = (bf16[1024,256]{1,0:T(8,128)(2,1)}, bf16[1024,256]{1,0:T(8,128)(2,1)S(1)}, u32[]{:S(2)}, u32[]{:S(2)}) collective-permute-start(bf16[1024,256]{1,0:T(8,128)(2,1)} %refs_0_.3), channel_id=1, source_target_pairs={{0,48},{8,24},{16,0},{24,40},{32,16},{40,56},{48,32},{56,8},{1,49}... | collective-permute-start | bytes 1572872 | tf_op jit(solution)/shard_map/ppermute | solution.py:175
  5.0 1.5 %collective-permute-start.1 = (bf16[1024,256]{1,0:T(8,128)(2,1)}, bf16[1024,256]{1,0:T(8,128)(2,1)S(1)}, u32[]{:S(2)}, u32[]{:S(2)}) collective-permute-start(bf16[1024,256]{1,0:T(8,128)(2,1)} %refs_0_.3), channel_id=1, source_target_pairs={{0,16},{8,56},{16,32},{24,8},{32,48},{40,24},{48,0},{56,40},{1,17}... | collective-permute-start | bytes 1572872 | tf_op jit(solution)/shard_map/ppermute | solution.py:175
  6.4 1.0 %copy-done = bf16[256,1024]{1,0:T(8,128)(2,1)S(1)} copy-done((bf16[256,1024]{1,0:T(8,128)(2,1)S(1)}, bf16[256,1024]{1,0:T(8,128)(2,1)}, u32[]{:S(2)}) %copy-start) | copy-done | bytes 524312
  7.5 1.0 %copy-done.2 = bf16[256,1024]{1,0:T(8,128)(2,1)S(1)} copy-done((bf16[256,1024]{1,0:T(8,128)(2,1)S(1)}, bf16[256,1024]{1,0:T(8,128)(2,1)}, u32[]{:S(2)}) %copy-start.2) | copy-done | bytes 524312
  8.5 0.8 %copy-done.11 = f32[1024,16]{0,1:T(8,128)S(1)} copy-done((f32[1024,16]{0,1:T(8,128)S(1)}, f32[1024,16]{0,1:T(8,128)}, u32[]{:S(2)}) %copy-start.11) | copy-done | bytes 65560
  9.3 1.8 %end_state.1 = (f32[16,8,128]{2,1,0:T(8,128)S(1)}, f32[16,8,128]{2,1,0:T(8,128)S(1)}) custom-call(bf16[256,1024]{1,0:T(8,128)(2,1)S(1)} %copy-done, bf16[256,1024]{1,0:T(8,128)(2,1)S(1)} %copy-done.2, f32[16,1024]{1,0:T(8,128)S(1)} %bitcast.98), custom_call_target="tpu_custom_call" | custom-call | flops 9000000 | bytes 1200000 | tf_op jit(solution)/shard_map/end_state/pallas_call | solution.py:110
  11.1 1.1 %collective-permute-start = (f32[16,8,128]{2,1,0:T(8,128)S(1)}, f32[16,8,128]{2,1,0:T(8,128)S(1)}, u32[]{:S(2)}, u32[]{:S(2)}) collective-permute-start(f32[16,8,128]{2,1,0:T(8,128)S(1)} %get-tuple-element.22), channel_id=1, source_target_pairs={{0,8},{8,0},{1,9},{9,1},{2,10},{10,2},{3,11},{11,3},{4,12},{12,4},... | collective-permute-start | bytes 196616 | tf_op jit(solution)/shard_map/ppermute | solution.py:21
  12.3 0.6 broadcast_multiply_fusion
  12.9 0.3 collective-permute-done
  13.2 0.7 broadcast_in_dim.17
  13.9 4.2 %all-to-all-start = ((f32[8,8,8,128]{3,2,1,0:T(8,128)}), f32[8,8,8,128]{3,2,1,0:T(8,128)S(1)}, u32[]{:S(2)}, u32[]{:S(2)}) async-start(f32[8,8,8,128]{3,2,1,0:T(8,128)} %broadcast_in_dim.17), calls=%async_computation | async-start | bytes 524288 | tf_op jit(solution)/shard_map/all_to_all | solution.py:162
  18.2 0.7 collective-permute-done.1.refs_1_
  19.0 2.3 %collective-permute-start.5 = (bf16[1024,256]{1,0:T(8,128)(2,1)S(1)}, bf16[1024,256]{1,0:T(8,128)(2,1)S(1)}, u32[]{:S(2)}, u32[]{:S(2)}) collective-permute-start(bf16[1024,256]{1,0:T(8,128)(2,1)S(1)} %collective-permute-done.3.refs_3_), channel_id=1, source_target_pairs={{0,32},{16,48},{32,0},{48,16},{1,33},{17,49},{33,1},{49,17},{2,34}... | collective-permute-start | bytes 1572872 | tf_op jit(solution)/shard_map/ppermute | solution.py:21
  21.3 0.9 %pad_maximum_fusion = bf16[1632,256]{1,0:T(8,128)(2,1)} fusion(bf16[608,256]{1,0:T(8,128)(2,1)S(1)} %slice.63, bf16[1024,256]{1,0:T(8,128)(2,1)S(1)} %collective-permute-done.2.refs_2_), kind=kLoop, calls=%fused_computation | loop fusion | flops 1671168 | bytes 1671168 | tf_op jit(solution)/shard_map/concatenate | solution.py:189
  22.3 2.7 %collective-permute-start.8 = (bf16[1632,256]{1,0:T(8,128)(2,1)}, bf16[1632,256]{1,0:T(8,128)(2,1)S(1)}, u32[]{:S(2)}, u32[]{:S(2)}) collective-permute-start(bf16[1632,256]{1,0:T(8,128)(2,1)} %pad_maximum_fusion), channel_id=1, source_target_pairs={{0,64},{64,0},{1,65},{65,1},{2,66},{66,2},{3,67},{67,3},{4,68},{68... | collective-permute-start | bytes 2506760 | tf_op jit(solution)/shard_map/ppermute | solution.py:21
  25.0 3.6 %local_part.1 = (f32[2048,128]{1,0:T(8,128)S(1)}, f32[16,8,128]{2,1,0:T(8,128)S(1)}) custom-call(bf16[256,1024]{1,0:T(8,128)(2,1)S(1)} %copy-done.1, bf16[256,1024]{1,0:T(8,128)(2,1)S(1)} %copy-done.3, f32[16,8,128]{2,1,0:T(8,128)S(1)} %get-tuple-element.23.rate_ref, f32[16,1024]{1,0:T(8,128)S(1)} %bitcast.99, f32[8,128]{1,0:T(8,128)S(1)} %bitcast.100), custom_call_target="tpu_custom_call" | custom-call | tf_op jit(solution)/shard_map/local_part/pallas_call | solution.py:125
  28.6 1.0 %copy-done.8 = f32[2048,128]{1,0:T(8,128)} copy-done((f32[2048,128]{1,0:T(8,128)}, f32[2048,128]{1,0:T(8,128)S(1)}, u32[]{:S(2)}) %copy-start.8) | copy-done | bytes 1048600
  29.6 0.6 copy-done.13
  30.3 1.0 %fusion.6 = f32[8,8,128]{2,1,0:T(8,128)S(1)} fusion(f32[8,8,8,128]{3,2,1,0:T(8,128)S(1)} %all-to-all-done, f32[16,8,128]{2,1,0:T(8,128)} %get-tuple-element.42, s32[]{:T(128)S(6)} %select_n.208, f32[]{:T(128)S(6)} %convert_element_type.78, f32[]{:T(128)S(6)} %convert_element_type.77, f32[]{:T(128)S(6)} %convert_element_type.76, f32[]{:T(128)S(6)} %convert_element_type.75, ...), kind=kLoop, calls=%fused_computation.26 | loop fusion | flops 262144 | bytes 327724 | tf_op jit(solution)/shard_map/add | solution.py:168
  31.2 1.6 %collective-permute-start.4 = (f32[8,8,128]{2,1,0:T(8,128)S(1)}, f32[8,8,128]{2,1,0:T(8,128)S(1)}, u32[]{:S(2)}, u32[]{:S(2)}) collective-permute-start(f32[8,8,128]{2,1,0:T(8,128)S(1)} %fusion.6), channel_id=1, source_target_pairs={{0,8},{8,0},{1,9},{9,1},{2,10},{10,2},{3,11},{11,3},{4,12},{12,4},... | collective-permute-start | bytes 98312 | tf_op jit(solution)/shard_map/ppermute | solution.py:21
  32.8 0.9 %pad_maximum_fusion.1 = bf16[1440,256]{1,0:T(8,128)(2,1)} fusion(bf16[416,256]{1,0:T(8,128)(2,1)S(1)} %slice.62, bf16[1024,256]{1,0:T(8,128)(2,1)S(1)} %collective-permute-done.1.refs_1_), kind=kLoop, calls=%fused_computation.1 | loop fusion | flops 1474560 | bytes 1474560 | tf_op jit(solution)/shard_map/concatenate | solution.py:188
  33.7 0.9 %collective-permute-start.7 = (bf16[1440,256]{1,0:T(8,128)(2,1)}, bf16[1440,256]{1,0:T(8,128)(2,1)}, u32[]{:S(2)}, u32[]{:S(2)}) collective-permute-start(bf16[1440,256]{1,0:T(8,128)(2,1)} %pad_maximum_fusion.1), channel_id=1, source_target_pairs={{0,16},{8,56},{16,32},{24,8},{32,48},{40,24},{48,0},{56,40},{1,17}... | collective-permute-start | bytes 2211848 | tf_op jit(solution)/shard_map/ppermute | solution.py:175
  34.6 0.9 %collective-permute-done.5.refs_4_ = bf16[1024,256]{1,0:T(8,128)(2,1)S(1)} collective-permute-done((bf16[1024,256]{1,0:T(8,128)(2,1)S(1)}, bf16[1024,256]{1,0:T(8,128)(2,1)S(1)}, u32[]{:S(2)}, u32[]{:S(2)}) %collective-permute-start.5) | collective-permute-done | bytes 524320 | tf_op jit(solution)/shard_map/ppermute | solution.py:21
  35.5 0.8 %copy-done.5 = bf16[1024,256]{1,0:T(8,128)(2,1)} copy-done((bf16[1024,256]{1,0:T(8,128)(2,1)}, bf16[1024,256]{1,0:T(8,128)(2,1)S(1)}, u32[]{:S(2)}) %copy-start.5) | copy-done | bytes 524312
  36.3 1.8 %gated.1.gated_ref = bf16[256,1024]{1,0:T(8,128)(2,1)S(1)} custom-call(bf16[256,1024]{1,0:T(8,128)(2,1)S(1)} %copy-done.10, f32[2048,128]{1,0:T(8,128)S(1)} %copy-done.9, f32[16,8,128]{2,1,0:T(8,128)S(1)} %get-tuple-element.23.rate_ref, f32[16,8,128]{2,1,0:T(8,128)S(1)} %copy-done.14, f32[16,8,128]{2,1,0:T(8,128)S(1)} %add_select_fusion.state_ref), custom_call_target="tpu_custom_call" | custom-call | tf_op jit(solution)/shard_map/gated/pallas_call | solution.py:142
  38.1 1.6 %collective-permute-start.6 = (bf16[256,1024]{1,0:T(8,128)(2,1)S(1)}, bf16[256,1024]{1,0:T(8,128)(2,1)}, u32[]{:S(2)}, u32[]{:S(2)}) collective-permute-start(bf16[256,1024]{1,0:T(8,128)(2,1)S(1)} %gated.1.gated_ref), channel_id=1, source_target_pairs={{0,8},{8,0},{1,9},{9,1},{2,10},{10,2},{3,11},{11,3},{4,12},{12,4},... | collective-permute-start | bytes 1572872 | tf_op jit(solution)/shard_map/ppermute | solution.py:21
  39.7 0.1 stack.101
  39.8 0.1 stack.111
  40.0 1.0 %copy-done.6 = bf16[1024,256]{1,0:T(8,128)(2,1)S(1)} copy-done((bf16[1024,256]{1,0:T(8,128)(2,1)S(1)}, bf16[1024,256]{1,0:T(8,128)(2,1)}, u32[]{:S(2)}) %copy-start.6) | copy-done | bytes 524312
  41.1 0.8 %project_early.1.early_ref = bf16[5,256,256]{2,1,0:T(8,128)(2,1)S(1)} custom-call(bf16[256,1024]{1,0:T(8,128)(2,1)S(1)} %gated.1.gated_ref, bf16[1024,256]{1,0:T(8,128)(2,1)S(1)} %copy-done.4, bf16[1024,256]{1,0:T(8,128)(2,1)S(1)} %collective-permute-done.1.refs_1_, bf16[1024,256]{1,0:T(8,128)(2,1)S(1)} %collective-permute-done.2.refs_2_, ...), custom_call_target="tpu_custom_call" | custom-call | tf_op jit(solution)/shard_map/project_early/pallas_call | solution.py:200
  41.9 2.7 %collective-permute-done.7.refs_5_.onward_ref = bf16[1440,256]{1,0:T(8,128)(2,1)} collective-permute-done((bf16[1440,256]{1,0:T(8,128)(2,1)}, bf16[1440,256]{1,0:T(8,128)(2,1)}, u32[]{:S(2)}, u32[]{:S(2)}) %collective-permute-start.7) | collective-permute-done | bytes 737312 | tf_op jit(solution)/shard_map/ppermute | solution.py:175
  44.6 2.6 %project_other_kernel.1 = bf16[2,4,256,256]{3,2,1,0:T(8,128)(2,1)S(1)} custom-call(bf16[256,1024]{1,0:T(8,128)(2,1)} %collective-permute-done.6.other_ref, s32[3,8]{1,0:T(4,128)S(1)} %pad_add_fusion.place_ref, bf16[1024,256]{1,0:T(8,128)(2,1)S(1)} %copy-done.4, bf16[1024,256]{1,0:T(8,128)(2,1)S(1)} %collective-permute-done.1.refs_1_, ...), custom_call_target="tpu_custom_call" | custom-call | flops 800000000 | bytes 4000000 | tf_op jit(solution)/shard_map/project_other_kernel/pallas_call | solution.py:237
  47.3 1.1 %collective-permute-start.13 = (bf16[4,256,256]{2,1,0:T(8,128)(2,1)S(1)}, bf16[4,256,256]{2,1,0:T(8,128)(2,1)S(1)}, u32[]{:S(2)}, u32[]{:S(2)}) collective-permute-start(bf16[4,256,256]{2,1,0:T(8,128)(2,1)S(1)} %get-tuple-element.40), channel_id=1, source_target_pairs={{0,1},{1,0},{2,3},{3,2},{4,5},{5,4},{6,7},{7,6},{8,9},{9,8},{10,11... | collective-permute-start | bytes 1572872 | tf_op jit(solution)/shard_map/ppermute | solution.py:21
  48.5 1.8 %project_own_kernel.1 = bf16[4,2,256,256]{3,2,1,0:T(8,128)(2,1)S(1)} custom-call(bf16[256,1024]{1,0:T(8,128)(2,1)S(1)} %gated.1.gated_ref, s32[3,8]{1,0:T(4,128)S(1)} %pad_add_fusion.place_ref, bf16[5,256,256]{2,1,0:T(8,128)(2,1)S(1)} %project_early.1.early_ref, bf16[1440,256]{1,0:T(8,128)(2,1)} %collective-permute-done.7.refs_5_.onward_ref, ...), custom_call_target="tpu_custom_call" | custom-call | flops 800000000 | bytes 4000000 | tf_op jit(solution)/shard_map/project_own_kernel/pallas_call | solution.py:237
  50.3 3.7 %collective-permute-start.9 = (bf16[2,256,256]{2,1,0:T(8,128)(2,1)S(1)}, bf16[2,256,256]{2,1,0:T(8,128)(2,1)S(1)}, u32[]{:S(2)}, u32[]{:S(2)}) collective-permute-start(bf16[2,256,256]{2,1,0:T(8,128)(2,1)S(1)} %get-tuple-element.37), channel_id=1, source_target_pairs={{0,4},{2,6},{4,0},{6,2},{1,5},{3,7},{5,1},{7,3},{8,12},{10,14},{12... | collective-permute-start | bytes 786440 | tf_op jit(solution)/shard_map/ppermute | solution.py:21
  54.0 0.4 collective-permute-start.11
  54.4 1.0 %collective-permute-start.10 = (bf16[2,256,256]{2,1,0:T(8,128)(2,1)S(1)}, bf16[2,256,256]{2,1,0:T(8,128)(2,1)S(1)}, u32[]{:S(2)}, u32[]{:S(2)}) collective-permute-start(bf16[2,256,256]{2,1,0:T(8,128)(2,1)S(1)} %get-tuple-element.39), channel_id=1, source_target_pairs={{0,2},{2,4},{4,6},{6,0},{1,3},{3,5},{5,7},{7,1},{8,10},{10,12},{12... | collective-permute-start | bytes 786440 | tf_op jit(solution)/shard_map/ppermute | solution.py:21
  55.4 3.3 %collective-permute-done.13.right_ref = bf16[4,256,256]{2,1,0:T(8,128)(2,1)S(1)} collective-permute-done((bf16[4,256,256]{2,1,0:T(8,128)(2,1)S(1)}, bf16[4,256,256]{2,1,0:T(8,128)(2,1)S(1)}, u32[]{:S(2)}, u32[]{:S(2)}) %collective-permute-start.13) | collective-permute-done | bytes 524320 | tf_op jit(solution)/shard_map/ppermute | solution.py:21
  58.7 0.9 %add_pair.1 = bf16[4,256,256]{2,1,0:T(8,128)(2,1)} custom-call(bf16[4,256,256]{2,1,0:T(8,128)(2,1)S(1)} %get-tuple-element.41.left_ref, bf16[4,256,256]{2,1,0:T(8,128)(2,1)S(1)} %collective-permute-done.13.right_ref), custom_call_target="tpu_custom_call" | custom-call | bytes 1500000 | tf_op jit(solution)/shard_map/add_pair/pallas_call | solution.py:260
  59.6 5.0 %all-to-all-start.1 = ((bf16[4,256,256]{2,1,0:T(8,128)(2,1)}), bf16[4,256,256]{2,1,0:T(8,128)(2,1)S(1)}, u32[]{:S(2)}, u32[]{:S(2)}) async-start(bf16[4,256,256]{2,1,0:T(8,128)(2,1)} %add_pair.1), calls=%async_computation.1 | async-start | bytes 1048576 | tf_op jit(solution)/shard_map/all_to_all | solution.py:294
  64.7 1.3 %collective-permute-done.11 = bf16[2,256,256]{2,1,0:T(8,128)(2,1)S(1)} collective-permute-done((bf16[2,256,256]{2,1,0:T(8,128)(2,1)S(1)}, bf16[2,256,256]{2,1,0:T(8,128)(2,1)S(1)}, u32[]{:S(2)}, u32[]{:S(2)}) %collective-permute-start.11) | collective-permute-done | bytes 262176 | tf_op jit(solution)/shard_map/ppermute | solution.py:21
  65.9 0.1 fusion.2
  66.1 0.5 collective-permute-start.12
  66.6 5.0 %all-to-all-done.1 = bf16[4,256,256]{2,1,0:T(8,128)(2,1)S(1)} async-done(((bf16[4,256,256]{2,1,0:T(8,128)(2,1)}), bf16[4,256,256]{2,1,0:T(8,128)(2,1)S(1)}, u32[]{:S(2)}, u32[]{:S(2)}) %all-to-all-start.1) | async-done | bytes 524320 | tf_op jit(solution)/shard_map/all_to_all | solution.py:294
  71.7 4.5 %collective-permute-start.14 = (bf16[256,256]{1,0:T(8,128)(2,1)S(1)}, bf16[256,256]{1,0:T(8,128)(2,1)S(1)}, u32[]{:S(2)}, u32[]{:S(2)}) collective-permute-start(bf16[256,256]{1,0:T(8,128)(2,1)S(1)} %fusion.4), channel_id=1, source_target_pairs={{0,8},{8,0},{1,9},{9,1},{2,10},{10,2},{3,11},{11,3},{4,12},{12,4},... | collective-permute-start | bytes 393224 | tf_op jit(solution)/shard_map/ppermute | solution.py:21
  76.2 0.9 %collective-permute-done.14 = bf16[256,256]{1,0:T(8,128)(2,1)S(1)} collective-permute-done((bf16[256,256]{1,0:T(8,128)(2,1)S(1)}, bf16[256,256]{1,0:T(8,128)(2,1)S(1)}, u32[]{:S(2)}, u32[]{:S(2)}) %collective-permute-start.14) | collective-permute-done | bytes 131104 | tf_op jit(solution)/shard_map/ppermute | solution.py:21
  77.2 0.8 %maximum_select_fusion = bf16[256,512]{1,0:T(8,128)(2,1)} fusion(bf16[256,256]{1,0:T(8,128)(2,1)S(1)} %collective-permute-done.14, bf16[256,256]{1,0:T(8,128)(2,1)S(1)} %fusion.3, pred[]{:T(512)S(6)} %eq.31), kind=kLoop, calls=%fused_computation.12 | loop fusion | flops 1179648 | bytes 524289 | tf_op jit(solution)/shard_map/jit(_where)/select_n | solution.py:297
  (50 shorter events, 0.5 us)
Async XLA Ops:
  0.0 18.2 %collective-permute-start.3 = (bf16[1024,256]{1,0:T(8,128)(2,1)}, bf16[1024,256]{1,0:T(8,128)(2,1)S(1)}, u32[]{:S(2)}, u32[]{:S(2)}) collective-permute-start(bf16[1024,256]{1,0:T(8,128)(2,1)} %refs_0_.3), channel_id=1, source_target_pairs={{0,64},{64,0},{1,65},{65,1},{2,66},{66,2},{3,67},{67,3},{4,68},{68... | collective-permute-start | bytes 1572872 | tf_op jit(solution)/shard_map/ppermute | solution.py:21
  3.7 14.4 %collective-permute-start.2 = (bf16[1024,256]{1,0:T(8,128)(2,1)}, bf16[1024,256]{1,0:T(8,128)(2,1)S(1)}, u32[]{:S(2)}, u32[]{:S(2)}) collective-permute-start(bf16[1024,256]{1,0:T(8,128)(2,1)} %refs_0_.3), channel_id=1, source_target_pairs={{0,48},{8,24},{16,0},{24,40},{32,16},{40,56},{48,32},{56,8},{1,49}... | collective-permute-start | bytes 1572872 | tf_op jit(solution)/shard_map/ppermute | solution.py:175
  5.0 13.9 %collective-permute-start.1 = (bf16[1024,256]{1,0:T(8,128)(2,1)}, bf16[1024,256]{1,0:T(8,128)(2,1)S(1)}, u32[]{:S(2)}, u32[]{:S(2)}) collective-permute-start(bf16[1024,256]{1,0:T(8,128)(2,1)} %refs_0_.3), channel_id=1, source_target_pairs={{0,16},{8,56},{16,32},{24,8},{32,48},{40,24},{48,0},{56,40},{1,17}... | collective-permute-start | bytes 1572872 | tf_op jit(solution)/shard_map/ppermute | solution.py:175
  6.4 1.0 %copy-start = (bf16[256,1024]{1,0:T(8,128)(2,1)S(1)}, bf16[256,1024]{1,0:T(8,128)(2,1)}, u32[]{:S(2)}) copy-start(bf16[256,1024]{1,0:T(8,128)(2,1)} %keys_ref.3) | copy-start | bytes 1572868
  7.5 1.0 %copy-start.2 = (bf16[256,1024]{1,0:T(8,128)(2,1)S(1)}, bf16[256,1024]{1,0:T(8,128)(2,1)}, u32[]{:S(2)}) copy-start(bf16[256,1024]{1,0:T(8,128)(2,1)} %values_ref.3) | copy-start | bytes 1572868
  8.5 0.8 %copy-start.11 = (f32[1024,16]{0,1:T(8,128)S(1)}, f32[1024,16]{0,1:T(8,128)}, u32[]{:S(2)}) copy-start(f32[1024,16]{0,1:T(8,128)} %param.10) | copy-start | bytes 196612
  11.1 2.0 %collective-permute-start = (f32[16,8,128]{2,1,0:T(8,128)S(1)}, f32[16,8,128]{2,1,0:T(8,128)S(1)}, u32[]{:S(2)}, u32[]{:S(2)}) collective-permute-start(f32[16,8,128]{2,1,0:T(8,128)S(1)} %get-tuple-element.22), channel_id=1, source_target_pairs={{0,8},{8,0},{1,9},{9,1},{2,10},{10,2},{3,11},{11,3},{4,12},{12,4},... | collective-permute-start | bytes 196616 | tf_op jit(solution)/shard_map/ppermute | solution.py:21
  13.2 5.7 %copy-start.16 = (f32[16,8,128]{2,1,0:T(8,128)}, f32[16,8,128]{2,1,0:T(8,128)S(1)}, u32[]{:S(2)}) copy-start(f32[16,8,128]{2,1,0:T(8,128)S(1)} %broadcast_select_fusion) | copy-start | bytes 196612
  13.9 16.3 %all-to-all-start = ((f32[8,8,8,128]{3,2,1,0:T(8,128)}), f32[8,8,8,128]{3,2,1,0:T(8,128)S(1)}, u32[]{:S(2)}, u32[]{:S(2)}) async-start(f32[8,8,8,128]{3,2,1,0:T(8,128)} %broadcast_in_dim.17), calls=%async_computation | async-start | bytes 524288 | tf_op jit(solution)/shard_map/all_to_all | solution.py:162
  18.9 6.0 %copy-start.1 = (bf16[256,1024]{1,0:T(8,128)(2,1)S(1)}, bf16[256,1024]{1,0:T(8,128)(2,1)}, u32[]{:S(2)}) copy-start(bf16[256,1024]{1,0:T(8,128)(2,1)} %keys_ref.3) | copy-start | bytes 1572868
  18.9 6.0 %copy-start.3 = (bf16[256,1024]{1,0:T(8,128)(2,1)S(1)}, bf16[256,1024]{1,0:T(8,128)(2,1)}, u32[]{:S(2)}) copy-start(bf16[256,1024]{1,0:T(8,128)(2,1)} %values_ref.3) | copy-start | bytes 1572868
  18.9 6.0 %copy-start.12 = (f32[1024,16]{0,1:T(8,128)S(1)}, f32[1024,16]{0,1:T(8,128)}, u32[]{:S(2)}) copy-start(f32[1024,16]{0,1:T(8,128)} %param.11) | copy-start | bytes 196612
  19.0 6.0 %copy-start.15 = (f32[1024]{0:T(1024)S(1)}, f32[1024]{0:T(1024)}, u32[]{:S(2)}) copy-start(f32[1024]{0:T(1024)} %param.12) | copy-start | bytes 12292
  19.0 16.5 %collective-permute-start.5 = (bf16[1024,256]{1,0:T(8,128)(2,1)S(1)}, bf16[1024,256]{1,0:T(8,128)(2,1)S(1)}, u32[]{:S(2)}, u32[]{:S(2)}) collective-permute-start(bf16[1024,256]{1,0:T(8,128)(2,1)S(1)} %collective-permute-done.3.refs_3_), channel_id=1, source_target_pairs={{0,32},{16,48},{32,0},{48,16},{1,33},{17,49},{33,1},{49,17},{2,34}... | collective-permute-start | bytes 1572872 | tf_op jit(solution)/shard_map/ppermute | solution.py:21
  22.3 22.3 %collective-permute-start.8 = (bf16[1632,256]{1,0:T(8,128)(2,1)}, bf16[1632,256]{1,0:T(8,128)(2,1)S(1)}, u32[]{:S(2)}, u32[]{:S(2)}) collective-permute-start(bf16[1632,256]{1,0:T(8,128)(2,1)} %pad_maximum_fusion), channel_id=1, source_target_pairs={{0,64},{64,0},{1,65},{65,1},{2,66},{66,2},{3,67},{67,3},{4,68},{68... | collective-permute-start | bytes 2506760 | tf_op jit(solution)/shard_map/ppermute | solution.py:21
  28.6 1.0 %copy-start.8 = (f32[2048,128]{1,0:T(8,128)}, f32[2048,128]{1,0:T(8,128)S(1)}, u32[]{:S(2)}) copy-start(f32[2048,128]{1,0:T(8,128)S(1)} %get-tuple-element.25.y_ref) | copy-start | bytes 3145732
  29.6 0.6 copy-start.13
  30.3 4.3 %copy-start.17 = (f32[16,8,128]{2,1,0:T(8,128)S(1)}, f32[16,8,128]{2,1,0:T(8,128)}, u32[]{:S(2)}) copy-start(f32[16,8,128]{2,1,0:T(8,128)} %copy-done.16) | copy-start | bytes 196612
  30.3 6.1 %copy-start.9 = (f32[2048,128]{1,0:T(8,128)S(1)}, f32[2048,128]{1,0:T(8,128)}, u32[]{:S(2)}) copy-start(f32[2048,128]{1,0:T(8,128)} %copy-done.8) | copy-start | bytes 3145732
  30.3 6.1 %copy-start.10 = (bf16[256,1024]{1,0:T(8,128)(2,1)S(1)}, bf16[256,1024]{1,0:T(8,128)(2,1)}, u32[]{:S(2)}) copy-start(bf16[256,1024]{1,0:T(8,128)(2,1)} %queries_ref.1) | copy-start | bytes 1572868
  30.3 6.0 %copy-start.14 = (f32[16,8,128]{2,1,0:T(8,128)S(1)}, f32[16,8,128]{2,1,0:T(8,128)}, u32[]{:S(2)}) copy-start(f32[16,8,128]{2,1,0:T(8,128)} %copy-done.13) | copy-start | bytes 196612
  31.2 3.4 %collective-permute-start.4 = (f32[8,8,128]{2,1,0:T(8,128)S(1)}, f32[8,8,128]{2,1,0:T(8,128)S(1)}, u32[]{:S(2)}, u32[]{:S(2)}) collective-permute-start(f32[8,8,128]{2,1,0:T(8,128)S(1)} %fusion.6), channel_id=1, source_target_pairs={{0,8},{8,0},{1,9},{9,1},{2,10},{10,2},{3,11},{11,3},{4,12},{12,4},... | collective-permute-start | bytes 98312 | tf_op jit(solution)/shard_map/ppermute | solution.py:21
  33.7 10.9 %collective-permute-start.7 = (bf16[1440,256]{1,0:T(8,128)(2,1)}, bf16[1440,256]{1,0:T(8,128)(2,1)}, u32[]{:S(2)}, u32[]{:S(2)}) collective-permute-start(bf16[1440,256]{1,0:T(8,128)(2,1)} %pad_maximum_fusion.1), channel_id=1, source_target_pairs={{0,16},{8,56},{16,32},{24,8},{32,48},{40,24},{48,0},{56,40},{1,17}... | collective-permute-start | bytes 2211848 | tf_op jit(solution)/shard_map/ppermute | solution.py:175
  35.5 0.8 %copy-start.5 = (bf16[1024,256]{1,0:T(8,128)(2,1)}, bf16[1024,256]{1,0:T(8,128)(2,1)S(1)}, u32[]{:S(2)}) copy-start(bf16[1024,256]{1,0:T(8,128)(2,1)S(1)} %collective-permute-done.5.refs_4_) | copy-start | bytes 1572868
  36.3 3.7 %copy-start.4 = (bf16[1024,256]{1,0:T(8,128)(2,1)S(1)}, bf16[1024,256]{1,0:T(8,128)(2,1)}, u32[]{:S(2)}) copy-start(bf16[1024,256]{1,0:T(8,128)(2,1)} %refs_0_.3) | copy-start | bytes 1572868
  38.1 3.8 %collective-permute-start.6 = (bf16[256,1024]{1,0:T(8,128)(2,1)S(1)}, bf16[256,1024]{1,0:T(8,128)(2,1)}, u32[]{:S(2)}, u32[]{:S(2)}) collective-permute-start(bf16[256,1024]{1,0:T(8,128)(2,1)S(1)} %gated.1.gated_ref), channel_id=1, source_target_pairs={{0,8},{8,0},{1,9},{9,1},{2,10},{10,2},{3,11},{11,3},{4,12},{12,4},... | collective-permute-start | bytes 1572872 | tf_op jit(solution)/shard_map/ppermute | solution.py:21
  40.0 1.0 %copy-start.6 = (bf16[1024,256]{1,0:T(8,128)(2,1)S(1)}, bf16[1024,256]{1,0:T(8,128)(2,1)}, u32[]{:S(2)}) copy-start(bf16[1024,256]{1,0:T(8,128)(2,1)} %copy-done.5) | copy-start | bytes 1572868
  41.1 3.6 %copy-start.7 = (bf16[1024,256]{1,0:T(8,128)(2,1)S(1)}, bf16[1024,256]{1,0:T(8,128)(2,1)}, u32[]{:S(2)}) copy-start(bf16[1024,256]{1,0:T(8,128)(2,1)} %copy-done.5) | copy-start | bytes 1572868
  47.3 11.4 %collective-permute-start.13 = (bf16[4,256,256]{2,1,0:T(8,128)(2,1)S(1)}, bf16[4,256,256]{2,1,0:T(8,128)(2,1)S(1)}, u32[]{:S(2)}, u32[]{:S(2)}) collective-permute-start(bf16[4,256,256]{2,1,0:T(8,128)(2,1)S(1)} %get-tuple-element.40), channel_id=1, source_target_pairs={{0,1},{1,0},{2,3},{3,2},{4,5},{5,4},{6,7},{7,6},{8,9},{9,8},{10,11... | collective-permute-start | bytes 1572872 | tf_op jit(solution)/shard_map/ppermute | solution.py:21
  50.3 14.4 %collective-permute-start.9 = (bf16[2,256,256]{2,1,0:T(8,128)(2,1)S(1)}, bf16[2,256,256]{2,1,0:T(8,128)(2,1)S(1)}, u32[]{:S(2)}, u32[]{:S(2)}) collective-permute-start(bf16[2,256,256]{2,1,0:T(8,128)(2,1)S(1)} %get-tuple-element.37), channel_id=1, source_target_pairs={{0,4},{2,6},{4,0},{6,2},{1,5},{3,7},{5,1},{7,3},{8,12},{10,14},{12... | collective-permute-start | bytes 786440 | tf_op jit(solution)/shard_map/ppermute | solution.py:21
  54.0 12.0 %collective-permute-start.11 = (bf16[2,256,256]{2,1,0:T(8,128)(2,1)S(1)}, bf16[2,256,256]{2,1,0:T(8,128)(2,1)S(1)}, u32[]{:S(2)}, u32[]{:S(2)}) collective-permute-start(bf16[2,256,256]{2,1,0:T(8,128)(2,1)S(1)} %get-tuple-element.38), channel_id=1, source_target_pairs={{0,6},{2,0},{4,2},{6,4},{1,7},{3,1},{5,3},{7,5},{8,14},{10,8},{12,... | collective-permute-start | bytes 786440 | tf_op jit(solution)/shard_map/ppermute | solution.py:21
  54.4 11.6 %collective-permute-start.10 = (bf16[2,256,256]{2,1,0:T(8,128)(2,1)S(1)}, bf16[2,256,256]{2,1,0:T(8,128)(2,1)S(1)}, u32[]{:S(2)}, u32[]{:S(2)}) collective-permute-start(bf16[2,256,256]{2,1,0:T(8,128)(2,1)S(1)} %get-tuple-element.39), channel_id=1, source_target_pairs={{0,2},{2,4},{4,6},{6,0},{1,3},{3,5},{5,7},{7,1},{8,10},{10,12},{12... | collective-permute-start | bytes 786440 | tf_op jit(solution)/shard_map/ppermute | solution.py:21
  59.6 12.0 %all-to-all-start.1 = ((bf16[4,256,256]{2,1,0:T(8,128)(2,1)}), bf16[4,256,256]{2,1,0:T(8,128)(2,1)S(1)}, u32[]{:S(2)}, u32[]{:S(2)}) async-start(bf16[4,256,256]{2,1,0:T(8,128)(2,1)} %add_pair.1), calls=%async_computation.1 | async-start | bytes 1048576 | tf_op jit(solution)/shard_map/all_to_all | solution.py:294
  66.1 10.1 %collective-permute-start.12 = (bf16[256,256]{1,0:T(8,128)(2,1)S(1)}, bf16[256,256]{1,0:T(8,128)(2,1)S(1)}, u32[]{:S(2)}, u32[]{:S(2)}) collective-permute-start(bf16[256,256]{1,0:T(8,128)(2,1)S(1)} %slice_bitcast_fusion.6), channel_id=1, source_target_pairs={{0,1},{1,0},{2,3},{3,2},{4,5},{5,4},{6,7},{7,6},{8,9},{9,8},{10,11... | collective-permute-start | bytes 393224 | tf_op jit(solution)/shard_map/ppermute | solution.py:21
  71.7 5.5 %collective-permute-start.14 = (bf16[256,256]{1,0:T(8,128)(2,1)S(1)}, bf16[256,256]{1,0:T(8,128)(2,1)S(1)}, u32[]{:S(2)}, u32[]{:S(2)}) collective-permute-start(bf16[256,256]{1,0:T(8,128)(2,1)S(1)} %fusion.4), channel_id=1, source_target_pairs={{0,8},{8,0},{1,9},{9,1},{2,10},{10,2},{3,11},{11,3},{4,12},{12,4},... | collective-permute-start | bytes 393224 | tf_op jit(solution)/shard_map/ppermute | solution.py:21

commit v5 on v4

--- a/solution.py
+++ b/solution.py
@@ -292,7 +292,7 @@
     away = project(project_own_kernel, (4, 2), gated, places, (early, onward, across))
     pair = add_pair(near[0], shift(near[1], "yl", 1))
     got = shift(add_up(*lax.all_to_all(pair, "z", 0, 0)), "core", 1)
-    ring = add_up(away[0], *[shift(away[j], "z", j) for j in (2, 1, 3)])
+    ring = add_up(away[0], *[shift(away[j], "z", j) for j in (1, 3, 2)])
     kept = add_up(ring[0], shift(ring[1], "yl", 1))
     return jnp.where(
         core == 0, jnp.concatenate([kept, got], 1), jnp.concatenate([got, kept], 1)

time: 78.5 us -> 78.5 us (level)
  starting transfers between devices: 37.1 us -> 38 us
  waiting for transfers between devices: 15.2 us -> 14.3 us
    ppermute x12, waiting for transfers between devices: 6.7 us -> 5.25 us  [shift(): lax.ppermute(value, axis, [(i, (i + step) % size) for i in range(size)])]
    ppermute x12, starting transfers between devices: 24.3 us -> 25.2 us  [shift(): lax.ppermute(value, axis, [(i, (i + step) % size) for i in range(size)])]
where the time goes in v5:
time: 78.5 us; the launch traced here: 78 us
  starting transfers between devices  38 us (48%)
  waiting for transfers between devices  14.3 us (18%)
  Pallas kernels  13.3 us (17%)
  local copies, waits for them, and re-layouts  7.56 us (10%)
  other arithmetic  4.57 us (6%)
    ppermute x12, starting transfers between devices, shift(): lax.ppermute(value, axis, [(i, (i + step) % size) for i in range(size)])  25.2 us
    unnamed x36, local copies, waits for them, and re-layouts  6.42 us
    all_to_all x1, waiting for transfers between devices, body(): got = shift(add_up(*lax.all_to_all(pair, 'z', 0, 0)), 'core', 1)  5.6 us
    ppermute x12, waiting for transfers between devices, shift(): lax.ppermute(value, axis, [(i, (i + step) % size) for i in range(size)])  5.25 us
    all_to_all x1, starting transfers between devices, body(): got = shift(add_up(*lax.all_to_all(pair, 'z', 0, 0)), 'core', 1)  5.02 us
    pallas_call x2, Pallas kernels, project(): pl.pallas_call(kernel, out_shape=jax.ShapeDtypeStruct((*lead, rows.shape[...  4.35 us
    all_to_all x1, starting transfers between devices, incoming_state(): lax.all_to_all(jnp.broadcast_to(mine[None], (8, *mine.shape)), ('yh', 'x'...  4.23 us
    pallas_call x1, Pallas kernels, local_part(): pl.pallas_call(local_kernel, out_shape=(jax.ShapeDtypeStruct((ROWS * step...  3.64 us
  transfers between devices with their start and end apart: 17, of which 8 were waited for; matrix products, arithmetic and copies ran while one was open for 6% of the time, Pallas kernels for 14%

profile of v5, /device:TPU:1, one launch (start us, length us, event | category | flops | bytes accessed | tf_op | source)
XLA Modules:
  0.0 78.0 jit_solution(8629425944231550460)
XLA Ops:
  0.0 3.7 %collective-permute-start.3 = (bf16[1024,256]{1,0:T(8,128)(2,1)}, bf16[1024,256]{1,0:T(8,128)(2,1)S(1)}, u32[]{:S(2)}, u32[]{:S(2)}) collective-permute-start(bf16[1024,256]{1,0:T(8,128)(2,1)} %refs_0_.3), channel_id=1, source_target_pairs={{0,64},{64,0},{1,65},{65,1},{2,66},{66,2},{3,67},{67,3},{4,68},{68... | collective-permute-start | bytes 1572872 | tf_op jit(solution)/shard_map/ppermute | solution.py:21
  3.7 1.2 %collective-permute-start.2 = (bf16[1024,256]{1,0:T(8,128)(2,1)}, bf16[1024,256]{1,0:T(8,128)(2,1)S(1)}, u32[]{:S(2)}, u32[]{:S(2)}) collective-permute-start(bf16[1024,256]{1,0:T(8,128)(2,1)} %refs_0_.3), channel_id=1, source_target_pairs={{0,48},{8,24},{16,0},{24,40},{32,16},{40,56},{48,32},{56,8},{1,49}... | collective-permute-start | bytes 1572872 | tf_op jit(solution)/shard_map/ppermute | solution.py:175
  5.0 1.5 %collective-permute-start.1 = (bf16[1024,256]{1,0:T(8,128)(2,1)}, bf16[1024,256]{1,0:T(8,128)(2,1)S(1)}, u32[]{:S(2)}, u32[]{:S(2)}) collective-permute-start(bf16[1024,256]{1,0:T(8,128)(2,1)} %refs_0_.3), channel_id=1, source_target_pairs={{0,16},{8,56},{16,32},{24,8},{32,48},{40,24},{48,0},{56,40},{1,17}... | collective-permute-start | bytes 1572872 | tf_op jit(solution)/shard_map/ppermute | solution.py:175
  6.4 1.0 %copy-done = bf16[256,1024]{1,0:T(8,128)(2,1)S(1)} copy-done((bf16[256,1024]{1,0:T(8,128)(2,1)S(1)}, bf16[256,1024]{1,0:T(8,128)(2,1)}, u32[]{:S(2)}) %copy-start) | copy-done | bytes 524312
  7.5 1.0 %copy-done.2 = bf16[256,1024]{1,0:T(8,128)(2,1)S(1)} copy-done((bf16[256,1024]{1,0:T(8,128)(2,1)S(1)}, bf16[256,1024]{1,0:T(8,128)(2,1)}, u32[]{:S(2)}) %copy-start.2) | copy-done | bytes 524312
  8.5 0.8 %copy-done.11 = f32[1024,16]{0,1:T(8,128)S(1)} copy-done((f32[1024,16]{0,1:T(8,128)S(1)}, f32[1024,16]{0,1:T(8,128)}, u32[]{:S(2)}) %copy-start.11) | copy-done | bytes 65560
  9.3 1.8 %end_state.1 = (f32[16,8,128]{2,1,0:T(8,128)S(1)}, f32[16,8,128]{2,1,0:T(8,128)S(1)}) custom-call(bf16[256,1024]{1,0:T(8,128)(2,1)S(1)} %copy-done, bf16[256,1024]{1,0:T(8,128)(2,1)S(1)} %copy-done.2, f32[16,1024]{1,0:T(8,128)S(1)} %bitcast.98), custom_call_target="tpu_custom_call" | custom-call | flops 9000000 | bytes 1200000 | tf_op jit(solution)/shard_map/end_state/pallas_call | solution.py:110
  11.1 1.1 %collective-permute-start = (f32[16,8,128]{2,1,0:T(8,128)S(1)}, f32[16,8,128]{2,1,0:T(8,128)S(1)}, u32[]{:S(2)}, u32[]{:S(2)}) collective-permute-start(f32[16,8,128]{2,1,0:T(8,128)S(1)} %get-tuple-element.22), channel_id=1, source_target_pairs={{0,8},{8,0},{1,9},{9,1},{2,10},{10,2},{3,11},{11,3},{4,12},{12,4},... | collective-permute-start | bytes 196616 | tf_op jit(solution)/shard_map/ppermute | solution.py:21
  12.3 0.6 broadcast_multiply_fusion
  12.9 0.3 collective-permute-done
  13.2 0.7 broadcast_in_dim.17
  13.9 4.2 %all-to-all-start = ((f32[8,8,8,128]{3,2,1,0:T(8,128)}), f32[8,8,8,128]{3,2,1,0:T(8,128)S(1)}, u32[]{:S(2)}, u32[]{:S(2)}) async-start(f32[8,8,8,128]{3,2,1,0:T(8,128)} %broadcast_in_dim.17), calls=%async_computation | async-start | bytes 524288 | tf_op jit(solution)/shard_map/all_to_all | solution.py:162
  18.2 0.7 collective-permute-done.1.refs_1_
  19.0 2.3 %collective-permute-start.5 = (bf16[1024,256]{1,0:T(8,128)(2,1)S(1)}, bf16[1024,256]{1,0:T(8,128)(2,1)S(1)}, u32[]{:S(2)}, u32[]{:S(2)}) collective-permute-start(bf16[1024,256]{1,0:T(8,128)(2,1)S(1)} %collective-permute-done.3.refs_3_), channel_id=1, source_target_pairs={{0,32},{16,48},{32,0},{48,16},{1,33},{17,49},{33,1},{49,17},{2,34}... | collective-permute-start | bytes 1572872 | tf_op jit(solution)/shard_map/ppermute | solution.py:21
  21.3 0.9 %pad_maximum_fusion = bf16[1632,256]{1,0:T(8,128)(2,1)} fusion(bf16[608,256]{1,0:T(8,128)(2,1)S(1)} %slice.63, bf16[1024,256]{1,0:T(8,128)(2,1)S(1)} %collective-permute-done.2.refs_2_), kind=kLoop, calls=%fused_computation | loop fusion | flops 1671168 | bytes 1671168 | tf_op jit(solution)/shard_map/concatenate | solution.py:189
  22.3 2.7 %collective-permute-start.8 = (bf16[1632,256]{1,0:T(8,128)(2,1)}, bf16[1632,256]{1,0:T(8,128)(2,1)S(1)}, u32[]{:S(2)}, u32[]{:S(2)}) collective-permute-start(bf16[1632,256]{1,0:T(8,128)(2,1)} %pad_maximum_fusion), channel_id=1, source_target_pairs={{0,64},{64,0},{1,65},{65,1},{2,66},{66,2},{3,67},{67,3},{4,68},{68... | collective-permute-start | bytes 2506760 | tf_op jit(solution)/shard_map/ppermute | solution.py:21
  25.0 3.6 %local_part.1 = (f32[2048,128]{1,0:T(8,128)S(1)}, f32[16,8,128]{2,1,0:T(8,128)S(1)}) custom-call(bf16[256,1024]{1,0:T(8,128)(2,1)S(1)} %copy-done.1, bf16[256,1024]{1,0:T(8,128)(2,1)S(1)} %copy-done.3, f32[16,8,128]{2,1,0:T(8,128)S(1)} %get-tuple-element.23.rate_ref, f32[16,1024]{1,0:T(8,128)S(1)} %bitcast.99, f32[8,128]{1,0:T(8,128)S(1)} %bitcast.100), custom_call_target="tpu_custom_call" | custom-call | tf_op jit(solution)/shard_map/local_part/pallas_call | solution.py:125
  28.6 1.0 %copy-done.8 = f32[2048,128]{1,0:T(8,128)} copy-done((f32[2048,128]{1,0:T(8,128)}, f32[2048,128]{1,0:T(8,128)S(1)}, u32[]{:S(2)}) %copy-start.8) | copy-done | bytes 1048600
  29.6 0.6 copy-done.13
  30.3 1.0 %fusion.6 = f32[8,8,128]{2,1,0:T(8,128)S(1)} fusion(f32[8,8,8,128]{3,2,1,0:T(8,128)S(1)} %all-to-all-done, f32[16,8,128]{2,1,0:T(8,128)} %get-tuple-element.42, s32[]{:T(128)S(6)} %select_n.208, f32[]{:T(128)S(6)} %convert_element_type.78, f32[]{:T(128)S(6)} %convert_element_type.77, f32[]{:T(128)S(6)} %convert_element_type.76, f32[]{:T(128)S(6)} %convert_element_type.75, ...), kind=kLoop, calls=%fused_computation.26 | loop fusion | flops 262144 | bytes 327724 | tf_op jit(solution)/shard_map/add | solution.py:168
  31.2 1.6 %collective-permute-start.4 = (f32[8,8,128]{2,1,0:T(8,128)S(1)}, f32[8,8,128]{2,1,0:T(8,128)S(1)}, u32[]{:S(2)}, u32[]{:S(2)}) collective-permute-start(f32[8,8,128]{2,1,0:T(8,128)S(1)} %fusion.6), channel_id=1, source_target_pairs={{0,8},{8,0},{1,9},{9,1},{2,10},{10,2},{3,11},{11,3},{4,12},{12,4},... | collective-permute-start | bytes 98312 | tf_op jit(solution)/shard_map/ppermute | solution.py:21
  32.8 0.9 %pad_maximum_fusion.1 = bf16[1440,256]{1,0:T(8,128)(2,1)} fusion(bf16[416,256]{1,0:T(8,128)(2,1)S(1)} %slice.62, bf16[1024,256]{1,0:T(8,128)(2,1)S(1)} %collective-permute-done.1.refs_1_), kind=kLoop, calls=%fused_computation.1 | loop fusion | flops 1474560 | bytes 1474560 | tf_op jit(solution)/shard_map/concatenate | solution.py:188
  33.7 0.9 %collective-permute-start.7 = (bf16[1440,256]{1,0:T(8,128)(2,1)}, bf16[1440,256]{1,0:T(8,128)(2,1)}, u32[]{:S(2)}, u32[]{:S(2)}) collective-permute-start(bf16[1440,256]{1,0:T(8,128)(2,1)} %pad_maximum_fusion.1), channel_id=1, source_target_pairs={{0,16},{8,56},{16,32},{24,8},{32,48},{40,24},{48,0},{56,40},{1,17}... | collective-permute-start | bytes 2211848 | tf_op jit(solution)/shard_map/ppermute | solution.py:175
  34.6 0.9 %collective-permute-done.5.refs_4_ = bf16[1024,256]{1,0:T(8,128)(2,1)S(1)} collective-permute-done((bf16[1024,256]{1,0:T(8,128)(2,1)S(1)}, bf16[1024,256]{1,0:T(8,128)(2,1)S(1)}, u32[]{:S(2)}, u32[]{:S(2)}) %collective-permute-start.5) | collective-permute-done | bytes 524320 | tf_op jit(solution)/shard_map/ppermute | solution.py:21
  35.5 0.8 %copy-done.5 = bf16[1024,256]{1,0:T(8,128)(2,1)} copy-done((bf16[1024,256]{1,0:T(8,128)(2,1)}, bf16[1024,256]{1,0:T(8,128)(2,1)S(1)}, u32[]{:S(2)}) %copy-start.5) | copy-done | bytes 524312
  36.3 1.8 %gated.1.gated_ref = bf16[256,1024]{1,0:T(8,128)(2,1)S(1)} custom-call(bf16[256,1024]{1,0:T(8,128)(2,1)S(1)} %copy-done.10, f32[2048,128]{1,0:T(8,128)S(1)} %copy-done.9, f32[16,8,128]{2,1,0:T(8,128)S(1)} %get-tuple-element.23.rate_ref, f32[16,8,128]{2,1,0:T(8,128)S(1)} %copy-done.14, f32[16,8,128]{2,1,0:T(8,128)S(1)} %add_select_fusion.state_ref), custom_call_target="tpu_custom_call" | custom-call | tf_op jit(solution)/shard_map/gated/pallas_call | solution.py:142
  38.1 1.6 %collective-permute-start.6 = (bf16[256,1024]{1,0:T(8,128)(2,1)S(1)}, bf16[256,1024]{1,0:T(8,128)(2,1)}, u32[]{:S(2)}, u32[]{:S(2)}) collective-permute-start(bf16[256,1024]{1,0:T(8,128)(2,1)S(1)} %gated.1.gated_ref), channel_id=1, source_target_pairs={{0,8},{8,0},{1,9},{9,1},{2,10},{10,2},{3,11},{11,3},{4,12},{12,4},... | collective-permute-start | bytes 1572872 | tf_op jit(solution)/shard_map/ppermute | solution.py:21
  39.7 0.1 stack.101
  39.8 0.1 stack.111
  40.0 1.0 %copy-done.6 = bf16[1024,256]{1,0:T(8,128)(2,1)S(1)} copy-done((bf16[1024,256]{1,0:T(8,128)(2,1)S(1)}, bf16[1024,256]{1,0:T(8,128)(2,1)}, u32[]{:S(2)}) %copy-start.6) | copy-done | bytes 524312
  41.1 0.8 %project_early.1.early_ref = bf16[5,256,256]{2,1,0:T(8,128)(2,1)S(1)} custom-call(bf16[256,1024]{1,0:T(8,128)(2,1)S(1)} %gated.1.gated_ref, bf16[1024,256]{1,0:T(8,128)(2,1)S(1)} %copy-done.4, bf16[1024,256]{1,0:T(8,128)(2,1)S(1)} %collective-permute-done.1.refs_1_, bf16[1024,256]{1,0:T(8,128)(2,1)S(1)} %collective-permute-done.2.refs_2_, ...), custom_call_target="tpu_custom_call" | custom-call | tf_op jit(solution)/shard_map/project_early/pallas_call | solution.py:200
  41.9 2.7 %collective-permute-done.7.refs_5_.onward_ref = bf16[1440,256]{1,0:T(8,128)(2,1)} collective-permute-done((bf16[1440,256]{1,0:T(8,128)(2,1)}, bf16[1440,256]{1,0:T(8,128)(2,1)}, u32[]{:S(2)}, u32[]{:S(2)}) %collective-permute-start.7) | collective-permute-done | bytes 737312 | tf_op jit(solution)/shard_map/ppermute | solution.py:175
  44.6 2.6 %project_other_kernel.1 = bf16[2,4,256,256]{3,2,1,0:T(8,128)(2,1)S(1)} custom-call(bf16[256,1024]{1,0:T(8,128)(2,1)} %collective-permute-done.6.other_ref, s32[3,8]{1,0:T(4,128)S(1)} %pad_add_fusion.place_ref, bf16[1024,256]{1,0:T(8,128)(2,1)S(1)} %copy-done.4, bf16[1024,256]{1,0:T(8,128)(2,1)S(1)} %collective-permute-done.1.refs_1_, ...), custom_call_target="tpu_custom_call" | custom-call | flops 800000000 | bytes 4000000 | tf_op jit(solution)/shard_map/project_other_kernel/pallas_call | solution.py:237
  47.3 1.1 %collective-permute-start.13 = (bf16[4,256,256]{2,1,0:T(8,128)(2,1)S(1)}, bf16[4,256,256]{2,1,0:T(8,128)(2,1)S(1)}, u32[]{:S(2)}, u32[]{:S(2)}) collective-permute-start(bf16[4,256,256]{2,1,0:T(8,128)(2,1)S(1)} %get-tuple-element.40), channel_id=1, source_target_pairs={{0,1},{1,0},{2,3},{3,2},{4,5},{5,4},{6,7},{7,6},{8,9},{9,8},{10,11... | collective-permute-start | bytes 1572872 | tf_op jit(solution)/shard_map/ppermute | solution.py:21
  48.5 1.8 %project_own_kernel.1 = bf16[4,2,256,256]{3,2,1,0:T(8,128)(2,1)S(1)} custom-call(bf16[256,1024]{1,0:T(8,128)(2,1)S(1)} %gated.1.gated_ref, s32[3,8]{1,0:T(4,128)S(1)} %pad_add_fusion.place_ref, bf16[5,256,256]{2,1,0:T(8,128)(2,1)S(1)} %project_early.1.early_ref, bf16[1440,256]{1,0:T(8,128)(2,1)} %collective-permute-done.7.refs_5_.onward_ref, ...), custom_call_target="tpu_custom_call" | custom-call | flops 800000000 | bytes 4000000 | tf_op jit(solution)/shard_map/project_own_kernel/pallas_call | solution.py:237
  50.3 1.7 %collective-permute-start.9 = (bf16[2,256,256]{2,1,0:T(8,128)(2,1)S(1)}, bf16[2,256,256]{2,1,0:T(8,128)(2,1)S(1)}, u32[]{:S(2)}, u32[]{:S(2)}) collective-permute-start(bf16[2,256,256]{2,1,0:T(8,128)(2,1)S(1)} %get-tuple-element.37), channel_id=1, source_target_pairs={{0,2},{2,4},{4,6},{6,0},{1,3},{3,5},{5,7},{7,1},{8,10},{10,12},{12... | collective-permute-start | bytes 786440 | tf_op jit(solution)/shard_map/ppermute | solution.py:21
  52.0 3.3 %collective-permute-start.11 = (bf16[2,256,256]{2,1,0:T(8,128)(2,1)S(1)}, bf16[2,256,256]{2,1,0:T(8,128)(2,1)S(1)}, u32[]{:S(2)}, u32[]{:S(2)}) collective-permute-start(bf16[2,256,256]{2,1,0:T(8,128)(2,1)S(1)} %get-tuple-element.38), channel_id=1, source_target_pairs={{0,4},{2,6},{4,0},{6,2},{1,5},{3,7},{5,1},{7,3},{8,12},{10,14},{12... | collective-permute-start | bytes 786440 | tf_op jit(solution)/shard_map/ppermute | solution.py:21
  55.3 0.7 collective-permute-start.10
  56.0 2.7 %collective-permute-done.13.right_ref = bf16[4,256,256]{2,1,0:T(8,128)(2,1)S(1)} collective-permute-done((bf16[4,256,256]{2,1,0:T(8,128)(2,1)S(1)}, bf16[4,256,256]{2,1,0:T(8,128)(2,1)S(1)}, u32[]{:S(2)}, u32[]{:S(2)}) %collective-permute-start.13) | collective-permute-done | bytes 524320 | tf_op jit(solution)/shard_map/ppermute | solution.py:21
  58.7 0.9 %add_pair.1 = bf16[4,256,256]{2,1,0:T(8,128)(2,1)} custom-call(bf16[4,256,256]{2,1,0:T(8,128)(2,1)S(1)} %get-tuple-element.41.left_ref, bf16[4,256,256]{2,1,0:T(8,128)(2,1)S(1)} %collective-permute-done.13.right_ref), custom_call_target="tpu_custom_call" | custom-call | bytes 1500000 | tf_op jit(solution)/shard_map/add_pair/pallas_call | solution.py:260
  59.6 5.0 %all-to-all-start.1 = ((bf16[4,256,256]{2,1,0:T(8,128)(2,1)}), bf16[4,256,256]{2,1,0:T(8,128)(2,1)S(1)}, u32[]{:S(2)}, u32[]{:S(2)}) async-start(bf16[4,256,256]{2,1,0:T(8,128)(2,1)} %add_pair.1), calls=%async_computation.1 | async-start | bytes 1048576 | tf_op jit(solution)/shard_map/all_to_all | solution.py:294
  64.7 0.4 collective-permute-done.10
  65.1 0.1 fusion.2
  65.2 0.7 collective-permute-start.12
  66.0 5.6 %all-to-all-done.1 = bf16[4,256,256]{2,1,0:T(8,128)(2,1)S(1)} async-done(((bf16[4,256,256]{2,1,0:T(8,128)(2,1)}), bf16[4,256,256]{2,1,0:T(8,128)(2,1)S(1)}, u32[]{:S(2)}, u32[]{:S(2)}) %all-to-all-start.1) | async-done | bytes 524320 | tf_op jit(solution)/shard_map/all_to_all | solution.py:294
  71.7 4.5 %collective-permute-start.14 = (bf16[256,256]{1,0:T(8,128)(2,1)S(1)}, bf16[256,256]{1,0:T(8,128)(2,1)S(1)}, u32[]{:S(2)}, u32[]{:S(2)}) collective-permute-start(bf16[256,256]{1,0:T(8,128)(2,1)S(1)} %fusion.4), channel_id=1, source_target_pairs={{0,8},{8,0},{1,9},{9,1},{2,10},{10,2},{3,11},{11,3},{4,12},{12,4},... | collective-permute-start | bytes 393224 | tf_op jit(solution)/shard_map/ppermute | solution.py:21
  76.2 0.9 %collective-permute-done.14 = bf16[256,256]{1,0:T(8,128)(2,1)S(1)} collective-permute-done((bf16[256,256]{1,0:T(8,128)(2,1)S(1)}, bf16[256,256]{1,0:T(8,128)(2,1)S(1)}, u32[]{:S(2)}, u32[]{:S(2)}) %collective-permute-start.14) | collective-permute-done | bytes 131104 | tf_op jit(solution)/shard_map/ppermute | solution.py:21
  77.2 0.8 %maximum_select_fusion = bf16[256,512]{1,0:T(8,128)(2,1)} fusion(bf16[256,256]{1,0:T(8,128)(2,1)S(1)} %collective-permute-done.14, bf16[256,256]{1,0:T(8,128)(2,1)S(1)} %fusion.3, pred[]{:T(512)S(6)} %eq.31), kind=kLoop, calls=%fused_computation.12 | loop fusion | flops 1179648 | bytes 524289 | tf_op jit(solution)/shard_map/jit(_where)/select_n | solution.py:297
  (50 shorter events, 0.5 us)
Async XLA Ops:
  0.0 18.2 %collective-permute-start.3 = (bf16[1024,256]{1,0:T(8,128)(2,1)}, bf16[1024,256]{1,0:T(8,128)(2,1)S(1)}, u32[]{:S(2)}, u32[]{:S(2)}) collective-permute-start(bf16[1024,256]{1,0:T(8,128)(2,1)} %refs_0_.3), channel_id=1, source_target_pairs={{0,64},{64,0},{1,65},{65,1},{2,66},{66,2},{3,67},{67,3},{4,68},{68... | collective-permute-start | bytes 1572872 | tf_op jit(solution)/shard_map/ppermute | solution.py:21
  3.7 14.4 %collective-permute-start.2 = (bf16[1024,256]{1,0:T(8,128)(2,1)}, bf16[1024,256]{1,0:T(8,128)(2,1)S(1)}, u32[]{:S(2)}, u32[]{:S(2)}) collective-permute-start(bf16[1024,256]{1,0:T(8,128)(2,1)} %refs_0_.3), channel_id=1, source_target_pairs={{0,48},{8,24},{16,0},{24,40},{32,16},{40,56},{48,32},{56,8},{1,49}... | collective-permute-start | bytes 1572872 | tf_op jit(solution)/shard_map/ppermute | solution.py:175
  5.0 13.9 %collective-permute-start.1 = (bf16[1024,256]{1,0:T(8,128)(2,1)}, bf16[1024,256]{1,0:T(8,128)(2,1)S(1)}, u32[]{:S(2)}, u32[]{:S(2)}) collective-permute-start(bf16[1024,256]{1,0:T(8,128)(2,1)} %refs_0_.3), channel_id=1, source_target_pairs={{0,16},{8,56},{16,32},{24,8},{32,48},{40,24},{48,0},{56,40},{1,17}... | collective-permute-start | bytes 1572872 | tf_op jit(solution)/shard_map/ppermute | solution.py:175
  6.4 1.0 %copy-start = (bf16[256,1024]{1,0:T(8,128)(2,1)S(1)}, bf16[256,1024]{1,0:T(8,128)(2,1)}, u32[]{:S(2)}) copy-start(bf16[256,1024]{1,0:T(8,128)(2,1)} %keys_ref.3) | copy-start | bytes 1572868
  7.5 1.0 %copy-start.2 = (bf16[256,1024]{1,0:T(8,128)(2,1)S(1)}, bf16[256,1024]{1,0:T(8,128)(2,1)}, u32[]{:S(2)}) copy-start(bf16[256,1024]{1,0:T(8,128)(2,1)} %values_ref.3) | copy-start | bytes 1572868
  8.5 0.8 %copy-start.11 = (f32[1024,16]{0,1:T(8,128)S(1)}, f32[1024,16]{0,1:T(8,128)}, u32[]{:S(2)}) copy-start(f32[1024,16]{0,1:T(8,128)} %param.10) | copy-start | bytes 196612
  11.1 2.0 %collective-permute-start = (f32[16,8,128]{2,1,0:T(8,128)S(1)}, f32[16,8,128]{2,1,0:T(8,128)S(1)}, u32[]{:S(2)}, u32[]{:S(2)}) collective-permute-start(f32[16,8,128]{2,1,0:T(8,128)S(1)} %get-tuple-element.22), channel_id=1, source_target_pairs={{0,8},{8,0},{1,9},{9,1},{2,10},{10,2},{3,11},{11,3},{4,12},{12,4},... | collective-permute-start | bytes 196616 | tf_op jit(solution)/shard_map/ppermute | solution.py:21
  13.2 5.7 %copy-start.16 = (f32[16,8,128]{2,1,0:T(8,128)}, f32[16,8,128]{2,1,0:T(8,128)S(1)}, u32[]{:S(2)}) copy-start(f32[16,8,128]{2,1,0:T(8,128)S(1)} %broadcast_select_fusion) | copy-start | bytes 196612
  13.9 16.3 %all-to-all-start = ((f32[8,8,8,128]{3,2,1,0:T(8,128)}), f32[8,8,8,128]{3,2,1,0:T(8,128)S(1)}, u32[]{:S(2)}, u32[]{:S(2)}) async-start(f32[8,8,8,128]{3,2,1,0:T(8,128)} %broadcast_in_dim.17), calls=%async_computation | async-start | bytes 524288 | tf_op jit(solution)/shard_map/all_to_all | solution.py:162
  18.9 6.0 %copy-start.1 = (bf16[256,1024]{1,0:T(8,128)(2,1)S(1)}, bf16[256,1024]{1,0:T(8,128)(2,1)}, u32[]{:S(2)}) copy-start(bf16[256,1024]{1,0:T(8,128)(2,1)} %keys_ref.3) | copy-start | bytes 1572868
  18.9 6.0 %copy-start.3 = (bf16[256,1024]{1,0:T(8,128)(2,1)S(1)}, bf16[256,1024]{1,0:T(8,128)(2,1)}, u32[]{:S(2)}) copy-start(bf16[256,1024]{1,0:T(8,128)(2,1)} %values_ref.3) | copy-start | bytes 1572868
  18.9 6.0 %copy-start.12 = (f32[1024,16]{0,1:T(8,128)S(1)}, f32[1024,16]{0,1:T(8,128)}, u32[]{:S(2)}) copy-start(f32[1024,16]{0,1:T(8,128)} %param.11) | copy-start | bytes 196612
  19.0 6.0 %copy-start.15 = (f32[1024]{0:T(1024)S(1)}, f32[1024]{0:T(1024)}, u32[]{:S(2)}) copy-start(f32[1024]{0:T(1024)} %param.12) | copy-start | bytes 12292
  19.0 16.5 %collective-permute-start.5 = (bf16[1024,256]{1,0:T(8,128)(2,1)S(1)}, bf16[1024,256]{1,0:T(8,128)(2,1)S(1)}, u32[]{:S(2)}, u32[]{:S(2)}) collective-permute-start(bf16[1024,256]{1,0:T(8,128)(2,1)S(1)} %collective-permute-done.3.refs_3_), channel_id=1, source_target_pairs={{0,32},{16,48},{32,0},{48,16},{1,33},{17,49},{33,1},{49,17},{2,34}... | collective-permute-start | bytes 1572872 | tf_op jit(solution)/shard_map/ppermute | solution.py:21
  22.3 22.3 %collective-permute-start.8 = (bf16[1632,256]{1,0:T(8,128)(2,1)}, bf16[1632,256]{1,0:T(8,128)(2,1)S(1)}, u32[]{:S(2)}, u32[]{:S(2)}) collective-permute-start(bf16[1632,256]{1,0:T(8,128)(2,1)} %pad_maximum_fusion), channel_id=1, source_target_pairs={{0,64},{64,0},{1,65},{65,1},{2,66},{66,2},{3,67},{67,3},{4,68},{68... | collective-permute-start | bytes 2506760 | tf_op jit(solution)/shard_map/ppermute | solution.py:21
  28.6 1.0 %copy-start.8 = (f32[2048,128]{1,0:T(8,128)}, f32[2048,128]{1,0:T(8,128)S(1)}, u32[]{:S(2)}) copy-start(f32[2048,128]{1,0:T(8,128)S(1)} %get-tuple-element.25.y_ref) | copy-start | bytes 3145732
  29.6 0.6 copy-start.13
  30.3 4.3 %copy-start.17 = (f32[16,8,128]{2,1,0:T(8,128)S(1)}, f32[16,8,128]{2,1,0:T(8,128)}, u32[]{:S(2)}) copy-start(f32[16,8,128]{2,1,0:T(8,128)} %copy-done.16) | copy-start | bytes 196612
  30.3 6.1 %copy-start.9 = (f32[2048,128]{1,0:T(8,128)S(1)}, f32[2048,128]{1,0:T(8,128)}, u32[]{:S(2)}) copy-start(f32[2048,128]{1,0:T(8,128)} %copy-done.8) | copy-start | bytes 3145732
  30.3 6.1 %copy-start.10 = (bf16[256,1024]{1,0:T(8,128)(2,1)S(1)}, bf16[256,1024]{1,0:T(8,128)(2,1)}, u32[]{:S(2)}) copy-start(bf16[256,1024]{1,0:T(8,128)(2,1)} %queries_ref.1) | copy-start | bytes 1572868
  30.3 6.0 %copy-start.14 = (f32[16,8,128]{2,1,0:T(8,128)S(1)}, f32[16,8,128]{2,1,0:T(8,128)}, u32[]{:S(2)}) copy-start(f32[16,8,128]{2,1,0:T(8,128)} %copy-done.13) | copy-start | bytes 196612
  31.2 3.4 %collective-permute-start.4 = (f32[8,8,128]{2,1,0:T(8,128)S(1)}, f32[8,8,128]{2,1,0:T(8,128)S(1)}, u32[]{:S(2)}, u32[]{:S(2)}) collective-permute-start(f32[8,8,128]{2,1,0:T(8,128)S(1)} %fusion.6), channel_id=1, source_target_pairs={{0,8},{8,0},{1,9},{9,1},{2,10},{10,2},{3,11},{11,3},{4,12},{12,4},... | collective-permute-start | bytes 98312 | tf_op jit(solution)/shard_map/ppermute | solution.py:21
  33.7 10.9 %collective-permute-start.7 = (bf16[1440,256]{1,0:T(8,128)(2,1)}, bf16[1440,256]{1,0:T(8,128)(2,1)}, u32[]{:S(2)}, u32[]{:S(2)}) collective-permute-start(bf16[1440,256]{1,0:T(8,128)(2,1)} %pad_maximum_fusion.1), channel_id=1, source_target_pairs={{0,16},{8,56},{16,32},{24,8},{32,48},{40,24},{48,0},{56,40},{1,17}... | collective-permute-start | bytes 2211848 | tf_op jit(solution)/shard_map/ppermute | solution.py:175
  35.5 0.8 %copy-start.5 = (bf16[1024,256]{1,0:T(8,128)(2,1)}, bf16[1024,256]{1,0:T(8,128)(2,1)S(1)}, u32[]{:S(2)}) copy-start(bf16[1024,256]{1,0:T(8,128)(2,1)S(1)} %collective-permute-done.5.refs_4_) | copy-start | bytes 1572868
  36.3 3.7 %copy-start.4 = (bf16[1024,256]{1,0:T(8,128)(2,1)S(1)}, bf16[1024,256]{1,0:T(8,128)(2,1)}, u32[]{:S(2)}) copy-start(bf16[1024,256]{1,0:T(8,128)(2,1)} %refs_0_.3) | copy-start | bytes 1572868
  38.1 3.8 %collective-permute-start.6 = (bf16[256,1024]{1,0:T(8,128)(2,1)S(1)}, bf16[256,1024]{1,0:T(8,128)(2,1)}, u32[]{:S(2)}, u32[]{:S(2)}) collective-permute-start(bf16[256,1024]{1,0:T(8,128)(2,1)S(1)} %gated.1.gated_ref), channel_id=1, source_target_pairs={{0,8},{8,0},{1,9},{9,1},{2,10},{10,2},{3,11},{11,3},{4,12},{12,4},... | collective-permute-start | bytes 1572872 | tf_op jit(solution)/shard_map/ppermute | solution.py:21
  40.0 1.0 %copy-start.6 = (bf16[1024,256]{1,0:T(8,128)(2,1)S(1)}, bf16[1024,256]{1,0:T(8,128)(2,1)}, u32[]{:S(2)}) copy-start(bf16[1024,256]{1,0:T(8,128)(2,1)} %copy-done.5) | copy-start | bytes 1572868
  41.1 3.6 %copy-start.7 = (bf16[1024,256]{1,0:T(8,128)(2,1)S(1)}, bf16[1024,256]{1,0:T(8,128)(2,1)}, u32[]{:S(2)}) copy-start(bf16[1024,256]{1,0:T(8,128)(2,1)} %copy-done.5) | copy-start | bytes 1572868
  47.3 11.4 %collective-permute-start.13 = (bf16[4,256,256]{2,1,0:T(8,128)(2,1)S(1)}, bf16[4,256,256]{2,1,0:T(8,128)(2,1)S(1)}, u32[]{:S(2)}, u32[]{:S(2)}) collective-permute-start(bf16[4,256,256]{2,1,0:T(8,128)(2,1)S(1)} %get-tuple-element.40), channel_id=1, source_target_pairs={{0,1},{1,0},{2,3},{3,2},{4,5},{5,4},{6,7},{7,6},{8,9},{9,8},{10,11... | collective-permute-start | bytes 1572872 | tf_op jit(solution)/shard_map/ppermute | solution.py:21
  50.3 14.4 %collective-permute-start.9 = (bf16[2,256,256]{2,1,0:T(8,128)(2,1)S(1)}, bf16[2,256,256]{2,1,0:T(8,128)(2,1)S(1)}, u32[]{:S(2)}, u32[]{:S(2)}) collective-permute-start(bf16[2,256,256]{2,1,0:T(8,128)(2,1)S(1)} %get-tuple-element.37), channel_id=1, source_target_pairs={{0,2},{2,4},{4,6},{6,0},{1,3},{3,5},{5,7},{7,1},{8,10},{10,12},{12... | collective-permute-start | bytes 786440 | tf_op jit(solution)/shard_map/ppermute | solution.py:21
  52.0 12.7 %collective-permute-start.11 = (bf16[2,256,256]{2,1,0:T(8,128)(2,1)S(1)}, bf16[2,256,256]{2,1,0:T(8,128)(2,1)S(1)}, u32[]{:S(2)}, u32[]{:S(2)}) collective-permute-start(bf16[2,256,256]{2,1,0:T(8,128)(2,1)S(1)} %get-tuple-element.38), channel_id=1, source_target_pairs={{0,4},{2,6},{4,0},{6,2},{1,5},{3,7},{5,1},{7,3},{8,12},{10,14},{12... | collective-permute-start | bytes 786440 | tf_op jit(solution)/shard_map/ppermute | solution.py:21
  55.3 9.8 %collective-permute-start.10 = (bf16[2,256,256]{2,1,0:T(8,128)(2,1)S(1)}, bf16[2,256,256]{2,1,0:T(8,128)(2,1)S(1)}, u32[]{:S(2)}, u32[]{:S(2)}) collective-permute-start(bf16[2,256,256]{2,1,0:T(8,128)(2,1)S(1)} %get-tuple-element.39), channel_id=1, source_target_pairs={{0,6},{2,0},{4,2},{6,4},{1,7},{3,1},{5,3},{7,5},{8,14},{10,8},{12,... | collective-permute-start | bytes 786440 | tf_op jit(solution)/shard_map/ppermute | solution.py:21
  59.6 12.0 %all-to-all-start.1 = ((bf16[4,256,256]{2,1,0:T(8,128)(2,1)}), bf16[4,256,256]{2,1,0:T(8,128)(2,1)S(1)}, u32[]{:S(2)}, u32[]{:S(2)}) async-start(bf16[4,256,256]{2,1,0:T(8,128)(2,1)} %add_pair.1), calls=%async_computation.1 | async-start | bytes 1048576 | tf_op jit(solution)/shard_map/all_to_all | solution.py:294
  65.2 10.9 %collective-permute-start.12 = (bf16[256,256]{1,0:T(8,128)(2,1)S(1)}, bf16[256,256]{1,0:T(8,128)(2,1)S(1)}, u32[]{:S(2)}, u32[]{:S(2)}) collective-permute-start(bf16[256,256]{1,0:T(8,128)(2,1)S(1)} %slice_bitcast_fusion.6), channel_id=1, source_target_pairs={{0,1},{1,0},{2,3},{3,2},{4,5},{5,4},{6,7},{7,6},{8,9},{9,8},{10,11... | collective-permute-start | bytes 393224 | tf_op jit(solution)/shard_map/ppermute | solution.py:21
  71.7 5.5 %collective-permute-start.14 = (bf16[256,256]{1,0:T(8,128)(2,1)S(1)}, bf16[256,256]{1,0:T(8,128)(2,1)S(1)}, u32[]{:S(2)}, u32[]{:S(2)}) collective-permute-start(bf16[256,256]{1,0:T(8,128)(2,1)S(1)} %fusion.4), channel_id=1, source_target_pairs={{0,8},{8,0},{1,9},{9,1},{2,10},{10,2},{3,11},{11,3},{4,12},{12,4},... | collective-permute-start | bytes 393224 | tf_op jit(solution)/shard_map/ppermute | solution.py:21
